TPU v7x, 32 devices: a whole 2x2x4 slice. The times are simulated.
32 devices in a mesh: groups: 2 (over y), expert: 4 (over z), fsdp: 2 (over x), ctx: 2 (over core).
Axes of the slice: x: 2, y: 2, z: 4, core: 2. Of those that a mesh axis runs over, the one named last changes fastest.
Arguments:
- inputs: bfloat16 [4, 1024, 2048], P(('groups', 'fsdp'), ('expert', 'ctx')), parts along dimension 0, may hold values from -6 to 6
- queries: bfloat16 [4, 1024, 2048], P(('groups', 'fsdp'), ('expert', 'ctx')), parts along dimension 0, may hold values from -131 to 131
- keys: bfloat16 [4, 1024, 2048], P(('groups', 'fsdp'), ('expert', 'ctx')), parts along dimension 0, may hold values from -5.1 to 5.1
- values: bfloat16 [4, 1024, 2048], P(('groups', 'fsdp'), ('expert', 'ctx')), parts along dimension 0, may hold values from -6 to 6
- doc_ids: int32 [4, 1024], P(('groups', 'fsdp')), parts along dimension 0, may hold values from 0 to 11, never falling along the last dimension, each value on 1 to 128 neighbouring positions
- norm_gain: float32 [2048], replicated, may hold values from 0.1 to 1.9
- expert_ids: int32 [4, 1024, 2], P(('groups', 'fsdp'), ('expert', 'ctx')), parts along dimension 0, may hold values from 0 to 3, all different within a row; in each aligned block of 128 rows (0 to 127, 128 to 255, ..., all dimensions but the last counted through in order) at most 80 rows name the same one
- gate_weights: float32 [4, 1024, 2], P(('groups', 'fsdp'), ('expert', 'ctx')), parts along dimension 0, may hold values from 0.1 to 0.9
- w_gate: bfloat16 [4, 2048, 768], P('expert', ('fsdp', 'ctx')), may hold values from -0.125 to 0.125
- w_up: bfloat16 [4, 2048, 768], P('expert', ('fsdp', 'ctx')), may hold values from -0.125 to 0.125
- w_down: bfloat16 [4, 768, 2048], P('expert', None, ('fsdp', 'ctx')), may hold values from -0.21875 to 0.21875
- out_grad: bfloat16 [4, 1024, 2048], P(('groups', 'fsdp'), ('expert', 'ctx')), parts along dimension 0, may hold values from -6 to 6
Outputs:
- layer_out: bfloat16 [4, 1024, 2048], P(('groups', 'fsdp'), ('expert', 'ctx')), parts along dimension 0
- input_grad: bfloat16 [4, 1024, 2048], P(('groups', 'fsdp'), ('expert', 'ctx')), parts along dimension 0
There are 2 independent parts, one for each index of `groups`. A program takes and returns all parts, laid end to end along the dimension named above; an argument that names none is the same for every part. Nothing has to cross between parts.
Inputs may be any that keep to these rules, and one draw needn't show every extreme that they name: `expert_ids`: in each aligned block of 128 positions (the positions of one device) no expert is named by more than 80 of the block's choices, and in every draw some block names some expert exactly 80 times; the two experts of a position differ. `doc_ids`: along a packed row document numbers never fall; every document has 1 to 128 positions, and some document has exactly 128.
All inputs are finite; a program needn't handle non-finite values.
Results may differ from a plain program's by a relative error of at most 0.0085.
Values may be sent and summed in bfloat16 or wider, within the bound.
No kernel may reach another device: no remote copies, remote signals or barrier semaphores. Data moves between devices by JAX's collectives and lax.ppermute only.
A program may use at most 64 MiB of HBM per device.

v0:
```python
import jax
import jax.numpy as jnp
from jax import lax
from jax.sharding import PartitionSpec as P

HEADS = 16
HD = 128


def shifted(block, axis, distance):
    devices = range(lax.axis_size(axis))
    route = [(i - distance, i) for i in devices if i - distance in devices]
    return lax.ppermute(block, axis, route)


def attend_block(query_rows, key_rows, value_rows, query_docs, key_docs):
    query_count = query_rows.shape[0]
    query_heads = query_rows.reshape(query_count, HEADS, HD)
    key_heads = key_rows.reshape(2 * query_count, HEADS, HD)
    value_heads = value_rows.reshape(2 * query_count, HEADS, HD)
    scores = jnp.einsum(
        "qhd,khd->hqk", query_heads, key_heads, preferred_element_type=jnp.float32
    ) * HD ** (-0.5)
    query_pos = jnp.arange(query_count, dtype=jnp.int32)
    key_pos = jnp.arange(2 * query_count, dtype=jnp.int32) - query_count
    visible = (query_docs[:, None] == key_docs[None, :]) & (key_pos[None, :] <= query_pos[:, None])
    scores = jnp.where(visible[None], scores, -jnp.inf)
    row_max = jnp.max(scores, axis=-1, keepdims=True)
    exp_scores = jnp.exp(scores - row_max)
    probs = (exp_scores / jnp.sum(exp_scores, axis=-1, keepdims=True)).astype(jnp.bfloat16)
    result = jnp.einsum("hqk,khd->qhd", probs, value_heads, preferred_element_type=jnp.float32)
    return result.reshape(query_count, HEADS * HD).astype(jnp.bfloat16)


def expert_rows(rows_in, rows_grad, gate_mat, up_mat, down_mat):
    gate_pre = jnp.dot(rows_in, gate_mat, preferred_element_type=jnp.float32)
    up_pre = jnp.dot(rows_in, up_mat, preferred_element_type=jnp.float32)
    sigmoid_val = 1.0 / (1.0 + jnp.exp(-gate_pre))
    silu_val = gate_pre * sigmoid_val
    hidden = (silu_val * up_pre).astype(jnp.bfloat16)
    expert_out = jnp.dot(hidden, down_mat, preferred_element_type=jnp.float32).astype(jnp.bfloat16)
    contract = (((1,), (1,)), ((), ()))
    hidden_grad = lax.dot_general(rows_grad, down_mat, contract, preferred_element_type=jnp.float32)
    gate_grad = (
        hidden_grad * up_pre * sigmoid_val * (1.0 + gate_pre * (1.0 - sigmoid_val))
    ).astype(jnp.bfloat16)
    up_grad = (hidden_grad * silu_val).astype(jnp.bfloat16)
    partial_value = lax.dot_general(
        gate_grad, gate_mat, contract, preferred_element_type=jnp.float32
    )
    partial_value = partial_value + lax.dot_general(
        up_grad, up_mat, contract, preferred_element_type=jnp.float32
    )
    return (expert_out, partial_value.astype(jnp.bfloat16))


def shards(
    inputs,
    queries,
    keys,
    values,
    doc_ids,
    norm_gain,
    expert_ids,
    gate_weights,
    w_gate,
    w_up,
    w_down,
    out_grad,
):
    tok_count = inputs.shape[1]
    feature_count = inputs.shape[2]
    first_pos = lax.axis_index(("expert", "ctx")) * tok_count
    prev_keys, prev_values = shifted((keys, values), ("expert", "ctx"), 1)
    key_rows = jnp.concatenate([prev_keys[0], keys[0]], 0)
    value_rows = jnp.concatenate([prev_values[0], values[0]], 0)
    doc_row = doc_ids[0]
    doc_pad = jnp.concatenate([jnp.full((tok_count,), -1, jnp.int32), doc_row], 0)
    query_docs = lax.dynamic_slice_in_dim(doc_row, first_pos, tok_count, 0)
    key_docs = lax.dynamic_slice_in_dim(doc_pad, first_pos, 2 * tok_count, 0)
    attended = attend_block(queries[0], key_rows, value_rows, query_docs, key_docs)
    full_gate, full_up, full_down = (
        lax.all_gather(w_gate, ("fsdp", "ctx"), axis=1, tiled=True),
        lax.all_gather(w_up, ("fsdp", "ctx"), axis=1, tiled=True),
        lax.all_gather(w_down, ("fsdp", "ctx"), axis=2, tiled=True),
    )
    gate_mat = full_gate[0]
    up_mat = full_up[0]
    down_mat = full_down[0]
    resid = inputs[0].astype(jnp.float32) + attended.astype(jnp.float32)
    inv_rms = lax.rsqrt(jnp.mean(resid * resid, axis=-1, keepdims=True) + 1e-06)
    normed = (resid * inv_rms * norm_gain).astype(jnp.bfloat16)
    peer_count = lax.axis_size("expert")
    slots_each = 5 * tok_count // (2 * peer_count)
    chosen = expert_ids[0].reshape(-1)
    onehot = (chosen[:, None] == jnp.arange(peer_count, dtype=jnp.int32)[None, :]).astype(jnp.int32)
    slot_rank = jnp.sum((jnp.cumsum(onehot, axis=0) - onehot) * onehot, axis=1)
    slot_index = chosen * slots_each + slot_rank
    empty_rows = jnp.zeros((peer_count * slots_each, feature_count), jnp.bfloat16)
    send_in = (
        empty_rows.at[slot_index]
        .set(jnp.repeat(normed, 2, axis=0))
        .reshape(peer_count, slots_each, feature_count)
    )
    send_grad = (
        empty_rows.at[slot_index]
        .set(jnp.repeat(out_grad[0], 2, axis=0))
        .reshape(peer_count, slots_each, feature_count)
    )
    recv_in, recv_grad = (
        lax.all_to_all(send_in, "expert", split_axis=0, concat_axis=0, tiled=True),
        lax.all_to_all(send_grad, "expert", split_axis=0, concat_axis=0, tiled=True),
    )
    sources = recv_in.shape[0]
    expert_out, part_grad = expert_rows(
        recv_in.reshape(-1, feature_count),
        recv_grad.reshape(-1, feature_count),
        gate_mat,
        up_mat,
        down_mat,
    )
    served_out = expert_out.reshape(sources, slots_each, feature_count)
    served_grad = part_grad.reshape(sources, slots_each, feature_count)
    back_out, back_grad = (
        lax.all_to_all(served_out, "expert", split_axis=0, concat_axis=0, tiled=True),
        lax.all_to_all(served_grad, "expert", split_axis=0, concat_axis=0, tiled=True),
    )
    picked_out = back_out.reshape(-1, feature_count)[slot_index]
    picked_grad = back_grad.reshape(-1, feature_count)[slot_index]
    route_weight = gate_weights[0].reshape(-1, 1)
    mixture = (
        (route_weight * picked_out.astype(jnp.float32))
        .reshape(tok_count, 2, feature_count)
        .sum(axis=1)
    )
    normed_grad = (
        (route_weight * picked_grad.astype(jnp.float32))
        .reshape(tok_count, 2, feature_count)
        .sum(axis=1)
    )
    layer_out = (resid + mixture).astype(jnp.bfloat16)
    gained = norm_gain * normed_grad
    input_grad = (
        out_grad[0].astype(jnp.float32)
        + inv_rms * gained
        - resid * inv_rms**3 * jnp.mean(resid * gained, axis=-1, keepdims=True)
    )
    return (layer_out[None], input_grad.astype(jnp.bfloat16)[None])


def solution(mesh):
    in_specs = (
        P(("groups", "fsdp"), ("expert", "ctx"), None),
        P(("groups", "fsdp"), ("expert", "ctx"), None),
        P(("groups", "fsdp"), ("expert", "ctx"), None),
        P(("groups", "fsdp"), ("expert", "ctx"), None),
        P(("groups", "fsdp"), None),
        P(),
        P(("groups", "fsdp"), ("expert", "ctx"), None),
        P(("groups", "fsdp"), ("expert", "ctx"), None),
        P("expert", ("fsdp", "ctx"), None),
        P("expert", ("fsdp", "ctx"), None),
        P("expert", None, ("fsdp", "ctx")),
        P(("groups", "fsdp"), ("expert", "ctx"), None),
    )
    out_specs = (
        P(("groups", "fsdp"), ("expert", "ctx"), None),
        P(("groups", "fsdp"), ("expert", "ctx"), None),
    )
    return jax.shard_map(shards, mesh=mesh, in_specs=in_specs, out_specs=out_specs, check_vma=False)
```

profile of v0, /device:TPU:0, one launch (start us, length us, event | category | flops | bytes accessed | tf_op | source)
XLA Modules:
  0.0 202.1 jit_solution(6529774560335338956)
XLA Ops:
  10.1 2.4 %collective-permute-start.1 = (bf16[1,128,2048]{1,2,0:T(8,128)(2,1)S(1)}, bf16[1,128,2048]{1,2,0:T(8,128)(2,1)S(1)}, u32[]{:S(2)}, u32[]{:S(2)}) collective-permute-start(bf16[1,128,2048]{1,2,0:T(8,128)(2,1)S(1)} %copy.25), channel_id=1, source_target_pairs={{0,1},{1,4},{4,5},{5,8},{8,9},{9,12},{12,13},{2,3},{3,6},{6,7},{7,... | collective-permute-start | bytes 1572872 | tf_op jit(solution)/shard_map/ppermute | solution.py:13
  12.5 4.6 %collective-permute-start = (bf16[1,128,2048]{2,1,0:T(8,128)(2,1)S(1)}, bf16[1,128,2048]{2,1,0:T(8,128)(2,1)S(1)}, u32[]{:S(2)}, u32[]{:S(2)}) collective-permute-start(bf16[1,128,2048]{2,1,0:T(8,128)(2,1)S(1)} %copy-done.10), channel_id=1, source_target_pairs={{0,1},{1,4},{4,5},{5,8},{8,9},{9,12},{12,13},{2,3},{3,6},{6,7},{7,... | collective-permute-start | bytes 1572872 | tf_op jit(solution)/shard_map/ppermute | solution.py:13
  22.2 3.3 %fusion.74 = (f32[16,128]{1,0:T(8,128)S(1)}, f32[16,128,256]{1,2,0:T(8,128)}) fusion(pred[128,256]{0,1:T(8,128)(4,1)S(1)} %fusion.57, bf16[128,16,128]{2,1,0:T(8,128)(2,1)} %bitcast.117, bf16[128,16,128]{2,0,1:T(8,128)(2,1)} %copy.28, bf16[128,16,128]{2,0,1:T(8,128)(2,1)S(1)} %copy.27), kind=kOutput, calls=%fused_computation.88 | convolution fusion | flops 138412288 | bytes 3710976 | tf_op jit(solution)/shard_map/sub | solution.py:29
  32.8 3.3 %scatter_custom_fusion = bf16[320,2048]{1,0:T(8,128)(2,1)} fusion(s32[256]{0:T(256)S(1)} %bitcast.119, bf16[256,2048]{1,0:T(8,128)(2,1)S(1)} %reshape.308, bf16[]{:T(256)} %constant.44.clone.1), kind=kCustom, calls=%fused_computation.58 | custom fusion | bytes 1310722 | tf_op jit(solution)/shard_map/scatter | solution.py:102
  36.1 7.0 %all-to-all-start = ((bf16[4,80,2048]{2,1,0:T(8,128)(2,1)}), bf16[4,80,2048]{2,1,0:T(8,128)(2,1)S(1)}, u32[]{:S(2)}, u32[]{:S(2)}) async-start(bf16[4,80,2048]{2,1,0:T(8,128)(2,1)} %bitcast.16), calls=%async_computation | async-start | bytes 2621440 | tf_op jit(solution)/shard_map/all_to_all | solution.py:111
  44.9 4.0 %scatter_custom_fusion.1 = bf16[320,2048]{1,0:T(8,128)(2,1)} fusion(s32[256]{0:T(256)S(1)} %bitcast.120, bf16[256,2048]{1,0:T(8,128)(2,1)} %reshape.316, bf16[]{:T(256)} %constant.44.clone.1), kind=kCustom, calls=%fused_computation.56 | custom fusion | bytes 1311232 | tf_op jit(solution)/shard_map/scatter | solution.py:107
  48.9 23.9 %all-to-all-done = bf16[4,80,2048]{2,1,0:T(8,128)(2,1)S(1)} async-done(((bf16[4,80,2048]{2,1,0:T(8,128)(2,1)}), bf16[4,80,2048]{2,1,0:T(8,128)(2,1)S(1)}, u32[]{:S(2)}, u32[]{:S(2)}) %all-to-all-start) | async-done | bytes 1310752 | tf_op jit(solution)/shard_map/all_to_all | solution.py:111
  73.9 3.7 %all-to-all-start.2 = ((bf16[4,80,2048]{2,1,0:T(8,128)(2,1)}), bf16[4,80,2048]{2,1,0:T(8,128)(2,1)S(1)}, u32[]{:S(2)}, u32[]{:S(2)}) async-start(bf16[4,80,2048]{2,1,0:T(8,128)(2,1)} %bitcast.25), calls=%async_computation.2 | async-start | bytes 2621440 | tf_op jit(solution)/shard_map/all_to_all | solution.py:112
  77.6 4.9 %fusion.11 = f32[320,768]{1,0:T(8,128)} fusion(bf16[320,2048]{1,0:T(8,128)(2,1)} %bitcast.110, bf16[1,2048,768]{2,1,0:T(8,128)(2,1)} %all-gather.4.cloned.1.call-done), kind=kOutput, calls=%fused_computation.15 | convolution fusion | flops 1006632960 | bytes 5439488 | tf_op jit(solution)/shard_map/dot_general | solution.py:36
  82.5 4.0 %fusion.7 = f32[320,768]{1,0:T(8,128)} fusion(bf16[320,2048]{1,0:T(8,128)(2,1)S(1)} %bitcast.111, bf16[1,2048,768]{2,1,0:T(8,128)(2,1)} %all-gather.6.cloned.1.call-done), kind=kOutput, calls=%fused_computation.11 | convolution fusion | flops 1006632960 | bytes 5439488 | tf_op jit(solution)/shard_map/dot_general | solution.py:37
  86.6 14.6 %all-gather.8.cloned.1.call-done = bf16[1,768,2048]{2,1,0:T(8,128)(2,1)} async-done(((bf16[1,768,512]{2,1,0:T(8,128)(2,1)}), bf16[1,768,2048]{2,1,0:T(8,128)(2,1)}) %all-gather.8.cloned.1.call-update) | async-done | bytes 3145744 | tf_op jit(solution)/shard_map/all_gather | solution.py:85
  101.1 4.8 %fusion.19 = bf16[320,2048]{1,0:T(8,128)(2,1)} fusion(bf16[1,768,2048]{2,1,0:T(8,128)(2,1)} %all-gather.8.cloned.1.call-done, f32[320,768]{1,0:T(8,128)} %fusion.7, f32[320,768]{1,0:T(8,128)} %fusion.11), kind=kOutput, calls=%fused_computation.19 | convolution fusion | flops 1008762880 | bytes 6422528 | tf_op jit(solution)/shard_map/dot_general | solution.py:41
  108.2 3.5 %all-to-all-start.1 = ((bf16[4,80,2048]{2,1,0:T(8,128)(2,1)}), bf16[4,80,2048]{2,1,0:T(8,128)(2,1)S(1)}, u32[]{:S(2)}, u32[]{:S(2)}) async-start(bf16[4,80,2048]{2,1,0:T(8,128)(2,1)} %bitcast.113), calls=%async_computation.1 | async-start | bytes 2621440 | tf_op jit(solution)/shard_map/all_to_all | solution.py:125
  111.8 3.3 %fusion.1 = f32[320,768]{1,0:T(8,128)S(1)} fusion(bf16[320,2048]{1,0:T(8,128)(2,1)S(1)} %bitcast.109, bf16[1,768,2048]{2,1,0:T(8,128)(2,1)} %all-gather.8.cloned.1.call-done), kind=kOutput, calls=%fused_computation.5 | convolution fusion | flops 1006632960 | bytes 5439488 | tf_op jit(solution)/shard_map/dot_general | solution.py:43
  117.2 2.5 %fusion.16 = bf16[320,2048]{1,0:T(8,128)(2,1)} fusion(f32[320,2048]{1,0:T(8,128)S(1)} %fusion.5, bf16[1,2048,768]{2,1,0:T(8,128)(2,1)S(1)} %copy-done.15, f32[320,768]{1,0:T(8,128)S(1)} %copy-done.17, f32[320,768]{1,0:T(8,128)S(1)} %fusion.1, f32[320,768]{1,0:T(8,128)S(1)} %copy-done.18), kind=kOutput, calls=%fused_computation.18 | convolution fusion | flops 1010401280 | bytes 10027008 | tf_op jit(solution)/shard_map/dot_general | solution.py:48
  119.7 22.9 %all-to-all-done.1 = bf16[4,80,2048]{2,1,0:T(8,128)(2,1)S(1)} async-done(((bf16[4,80,2048]{2,1,0:T(8,128)(2,1)}), bf16[4,80,2048]{2,1,0:T(8,128)(2,1)S(1)}, u32[]{:S(2)}, u32[]{:S(2)}) %all-to-all-start.1) | async-done | bytes 1310752 | tf_op jit(solution)/shard_map/all_to_all | solution.py:125
  142.5 3.8 %all-to-all-start.3 = ((bf16[4,80,2048]{2,1,0:T(8,128)(2,1)}), bf16[4,80,2048]{2,1,0:T(8,128)(2,1)S(1)}, u32[]{:S(2)}, u32[]{:S(2)}) async-start(bf16[4,80,2048]{2,1,0:T(8,128)(2,1)} %bitcast.112), calls=%async_computation.3 | async-start | bytes 2621440 | tf_op jit(solution)/shard_map/all_to_all | solution.py:126
  146.4 2.5 %copy.31 = f32[1,128,2048]{2,1,0:T(8,128)} copy(f32[1,128,2048]{1,2,0:T(8,128)} %bitcast.106) | data formatting | bytes 2097152 | tf_op jit(solution)/shard_map/convert_element_type | solution.py:90
  149.0 2.4 %gather_fusion = bf16[256,2048]{1,0:T(8,128)(2,1)} fusion(bf16[320,2048]{1,0:T(8,128)(2,1)S(1)} %bitcast.103, s32[1024]{0:T(1024)S(1)} %pad_clamp_fusion), kind=kCustom, calls=%fused_computation | custom fusion | bytes 2098176 | tf_op jit(solution)/shard_map/gather | solution.py:128
  151.3 25.6 %all-to-all-done.3 = bf16[4,80,2048]{2,1,0:T(8,128)(2,1)S(1)} async-done(((bf16[4,80,2048]{2,1,0:T(8,128)(2,1)}), bf16[4,80,2048]{2,1,0:T(8,128)(2,1)S(1)}, u32[]{:S(2)}, u32[]{:S(2)}) %all-to-all-start.3) | async-done | bytes 1310752 | tf_op jit(solution)/shard_map/all_to_all | solution.py:126
  176.9 2.3 %gather_fusion.1 = bf16[256,2048]{1,0:T(8,128)(2,1)} fusion(bf16[320,2048]{1,0:T(8,128)(2,1)S(1)} %bitcast.104, s32[1024]{0:T(1024)S(1)} %pad_clamp_fusion), kind=kCustom, calls=%fused_computation.1 | custom fusion | bytes 2098176 | tf_op jit(solution)/shard_map/gather | solution.py:129
  179.2 2.4 %reshape.287 = f32[128,2,2048]{2,1,0:T(2,128)S(1)} reshape(bf16[256,2048]{1,0:T(8,128)(2,1)} %gather_fusion.1) | data formatting | bytes 3145728 | tf_op jit(solution)/shard_map/convert_element_type | solution.py:137
  181.6 3.4 %reshape.286 = f32[128,2,2048]{2,1,0:T(2,128)} reshape(bf16[256,2048]{1,0:T(8,128)(2,1)} %gather_fusion) | data formatting | bytes 3145728 | tf_op jit(solution)/shard_map/convert_element_type | solution.py:132
  185.0 7.8 %multiply_reduce_fusion = (f32[128,2048]{1,0:T(8,128)S(1)}, f32[128,2048]{1,0:T(8,128)S(1)}) fusion(f32[128,2,2048]{2,1,0:T(2,128)S(1)} %reshape.287, f32[128,2]{1,0:T(8,128)S(1)} %copy.32, f32[128,2,2048]{2,1,0:T(2,128)} %reshape.286), kind=kLoop, calls=%fused_computation.21 | loop fusion | flops 1572864 | bytes 6292480 | tf_op jit(solution)/shard_map/reduce_sum | solution.py:139
  (89 shorter events, 25.3 us)
Async XLA Ops:
  7.2 5.3 %copy-start.10 = (bf16[1,128,2048]{2,1,0:T(8,128)(2,1)S(1)}, bf16[1,128,2048]{2,1,0:T(8,128)(2,1)}, u32[]{:S(2)}) copy-start(bf16[1,128,2048]{2,1,0:T(8,128)(2,1)} %param.15) | copy-start | bytes 1572868
  7.2 10.0 %copy-start.12 = (s32[1,128,2]{1,2,0:T(2,128)S(1)}, s32[1,128,2]{1,2,0:T(2,128)}, u32[]{:S(2)}) copy-start(s32[1,128,2]{1,2,0:T(2,128)} %param.18) | copy-start | bytes 3076
  7.2 12.3 %copy-start.13 = (s32[1,1024]{1,0:T(1,128)S(1)}, s32[1,1024]{1,0:T(1,128)}, u32[]{:S(2)}) copy-start(s32[1,1024]{1,0:T(1,128)} %param.16) | copy-start | bytes 12292
  7.2 70.4 %all-gather.4.cloned.1.call-start = ((), (), s32[]{:S(2)}) async-start(), calls=%async_computation.4 | async-start | bytes 3932160 | tf_op jit(solution)/shard_map/all_gather | solution.py:83
  7.9 74.6 %all-gather.6.cloned.1.call-start = ((), (), s32[]{:S(2)}) async-start(), calls=%async_computation.5 | async-start | bytes 3932160 | tf_op jit(solution)/shard_map/all_gather | solution.py:84
  8.7 12.2 %copy-start.9 = (bf16[1,128,2048]{2,1,0:T(8,128)(2,1)S(1)}, bf16[1,128,2048]{2,1,0:T(8,128)(2,1)}, u32[]{:S(2)}) copy-start(bf16[1,128,2048]{2,1,0:T(8,128)(2,1)} %param.13) | copy-start | bytes 1572868
  8.7 92.4 %all-gather.8.cloned.1.call-start = ((), (), s32[]{:S(2)}) async-start(), calls=%async_computation.6 | async-start | bytes 3932160 | tf_op jit(solution)/shard_map/all_gather | solution.py:85
  10.1 11.8 %collective-permute-start.1 = (bf16[1,128,2048]{1,2,0:T(8,128)(2,1)S(1)}, bf16[1,128,2048]{1,2,0:T(8,128)(2,1)S(1)}, u32[]{:S(2)}, u32[]{:S(2)}) collective-permute-start(bf16[1,128,2048]{1,2,0:T(8,128)(2,1)S(1)} %copy.25), channel_id=1, source_target_pairs={{0,1},{1,4},{4,5},{5,8},{8,9},{9,12},{12,13},{2,3},{3,6},{6,7},{7,... | collective-permute-start | bytes 1572872 | tf_op jit(solution)/shard_map/ppermute | solution.py:13
  12.5 13.0 %collective-permute-start = (bf16[1,128,2048]{2,1,0:T(8,128)(2,1)S(1)}, bf16[1,128,2048]{2,1,0:T(8,128)(2,1)S(1)}, u32[]{:S(2)}, u32[]{:S(2)}) collective-permute-start(bf16[1,128,2048]{2,1,0:T(8,128)(2,1)S(1)} %copy-done.10), channel_id=1, source_target_pairs={{0,1},{1,4},{4,5},{5,8},{8,9},{9,12},{12,13},{2,3},{3,6},{6,7},{7,... | collective-permute-start | bytes 1572872 | tf_op jit(solution)/shard_map/ppermute | solution.py:13
  27.8 1.9 copy-start.3
  27.9 1.6 copy-start.11
  29.3 2.0 %copy-start = (f32[128,2048]{1,0:T(8,128)}, f32[128,2048]{1,0:T(8,128)S(1)}, u32[]{:S(2)}) copy-start(f32[128,2048]{1,0:T(8,128)S(1)} %copy.38) | copy-start | bytes 3145732
  32.8 10.3 %copy-start.5 = (bf16[1,128,2048]{2,1,0:T(8,128)(2,1)S(1)}, bf16[1,128,2048]{2,1,0:T(8,128)(2,1)}, u32[]{:S(2)}) copy-start(bf16[1,128,2048]{2,1,0:T(8,128)(2,1)} %param.23) | copy-start | bytes 1572868
  36.1 36.7 %all-to-all-start = ((bf16[4,80,2048]{2,1,0:T(8,128)(2,1)}), bf16[4,80,2048]{2,1,0:T(8,128)(2,1)S(1)}, u32[]{:S(2)}, u32[]{:S(2)}) async-start(bf16[4,80,2048]{2,1,0:T(8,128)(2,1)} %bitcast.16), calls=%async_computation | async-start | bytes 2621440 | tf_op jit(solution)/shard_map/all_to_all | solution.py:111
  73.9 34.4 %all-to-all-start.2 = ((bf16[4,80,2048]{2,1,0:T(8,128)(2,1)}), bf16[4,80,2048]{2,1,0:T(8,128)(2,1)S(1)}, u32[]{:S(2)}, u32[]{:S(2)}) async-start(bf16[4,80,2048]{2,1,0:T(8,128)(2,1)} %bitcast.25), calls=%async_computation.2 | async-start | bytes 2621440 | tf_op jit(solution)/shard_map/all_to_all | solution.py:112
  77.6 4.9 %copy-start.8 = (bf16[4,80,2048]{2,1,0:T(8,128)(2,1)S(1)}, bf16[4,80,2048]{2,1,0:T(8,128)(2,1)}, u32[]{:S(2)}) copy-start(bf16[4,80,2048]{2,1,0:T(8,128)(2,1)} %copy-done.7) | copy-start | bytes 3932164
  108.2 34.3 %all-to-all-start.1 = ((bf16[4,80,2048]{2,1,0:T(8,128)(2,1)}), bf16[4,80,2048]{2,1,0:T(8,128)(2,1)S(1)}, u32[]{:S(2)}, u32[]{:S(2)}) async-start(bf16[4,80,2048]{2,1,0:T(8,128)(2,1)} %bitcast.113), calls=%async_computation.1 | async-start | bytes 2621440 | tf_op jit(solution)/shard_map/all_to_all | solution.py:125
  111.8 3.3 %copy-start.16 = (bf16[1,2048,768]{2,1,0:T(8,128)(2,1)S(1)}, bf16[1,2048,768]{2,1,0:T(8,128)(2,1)}, u32[]{:S(2)}) copy-start(bf16[1,2048,768]{2,1,0:T(8,128)(2,1)} %all-gather.6.cloned.1.call-done) | copy-start | bytes 9437188
  111.8 3.3 %copy-start.17 = (f32[320,768]{1,0:T(8,128)S(1)}, f32[320,768]{1,0:T(8,128)}, u32[]{:S(2)}) copy-start(f32[320,768]{1,0:T(8,128)} %fusion.11) | copy-start | bytes 2949124
  115.1 1.9 copy-start.15
  115.1 2.1 %copy-start.18 = (f32[320,768]{1,0:T(8,128)S(1)}, f32[320,768]{1,0:T(8,128)}, u32[]{:S(2)}) copy-start(f32[320,768]{1,0:T(8,128)} %fusion.7) | copy-start | bytes 2949124
  119.7 26.6 %copy-start.14 = (f32[1,128,2]{1,2,0:T(2,128)S(1)}, f32[1,128,2]{1,2,0:T(2,128)}, u32[]{:S(2)}) copy-start(f32[1,128,2]{1,2,0:T(2,128)} %param.19) | copy-start | bytes 3076
  142.5 34.3 %all-to-all-start.3 = ((bf16[4,80,2048]{2,1,0:T(8,128)(2,1)}), bf16[4,80,2048]{2,1,0:T(8,128)(2,1)S(1)}, u32[]{:S(2)}, u32[]{:S(2)}) async-start(bf16[4,80,2048]{2,1,0:T(8,128)(2,1)} %bitcast.112), calls=%async_computation.3 | async-start | bytes 2621440 | tf_op jit(solution)/shard_map/all_to_all | solution.py:126
  185.0 7.8 %copy-start.1 = (f32[128,2048]{1,0:T(8,128)S(1)}, f32[128,2048]{1,0:T(8,128)}, u32[]{:S(2)}) copy-start(f32[128,2048]{1,0:T(8,128)} %copy-done) | copy-start | bytes 3145732
  (4 other events, 5.1 us)
Sparse Core Ops, SparseCore 0:
  9.6 31.2 all-gather.3
  42.4 28.5 all-gather.5
  72.6 28.5 all-gather.7
where the time goes:
time: 203 us; the launch traced here: 202 us
  waiting for transfers between devices  90.6 us (45%)
  local copies, waits for them, and re-layouts  34.6 us (17%)
  matrix products  26.1 us (13%)
  starting transfers between devices  25.1 us (12%)
  between operations  14.2 us (7%)
  other arithmetic  11.6 us (6%)
    all_to_all x1, waiting for transfers between devices, shards(): lax.all_to_all(served_grad, 'expert', split_axis=0, concat_axis=0, tiled=...  25.6 us
    all_to_all x1, waiting for transfers between devices, shards(): lax.all_to_all(send_in, 'expert', split_axis=0, concat_axis=0, tiled=True)  23.9 us
    all_to_all x1, waiting for transfers between devices, shards(): lax.all_to_all(served_out, 'expert', split_axis=0, concat_axis=0, tiled=T...  22.9 us
    all_gather x1, waiting for transfers between devices, shards(): lax.all_gather(w_down, ('fsdp', 'ctx'), axis=2, tiled=True)  14.6 us
    reduce_sum x1, other arithmetic, shards(): normed_grad = (route_weight * picked_grad.astype(jnp.float32)).reshape(to...  7.8 us
    all_to_all x1, starting transfers between devices, shards(): lax.all_to_all(send_in, 'expert', split_axis=0, concat_axis=0, tiled=True)  7 us
    ppermute x2, starting transfers between devices, shifted(): return lax.ppermute(block, axis, route)  6.98 us
    unnamed x42, local copies, waits for them, and re-layouts  6.68 us
  transfers between devices with their start and end apart: 9, of which 5 were waited for; matrix products, arithmetic and copies ran while one was open for 25% of the time, Pallas kernels for 0%

commit v1 on v0

v1 whole, which is shorter than its diff:
```python
import jax
import jax.numpy as jnp
from jax import lax
from jax.experimental import pallas as pl
from jax.experimental.pallas import tpu as pltpu
from jax.sharding import PartitionSpec as P

HEADS = 16
HD = 128
BF = jnp.bfloat16
F32 = jnp.float32
VM = pl.BlockSpec(memory_space=pltpu.VMEM)
ANY = pl.BlockSpec(memory_space=pl.ANY)
MIB = 1024 * 1024


def params(mib):
    return pltpu.CompilerParams(vmem_limit_bytes=mib * MIB)


def swapped(block, axis, distance):
    count = lax.axis_size(axis)
    return lax.ppermute(block, axis, [(i, i ^ distance) for i in range(count)])


def shifted(block, axis, distance):
    devices = range(lax.axis_size(axis))
    route = [(i - distance, i) for i in devices if i - distance in devices]
    return lax.ppermute(block, axis, route)


def dot(a, b):
    return jnp.dot(a, b, preferred_element_type=F32)


def dot_t(a, b):
    return lax.dot_general(a, b, (((1,), (1,)), ((), ())), preferred_element_type=F32)


def routing(ids_ref, here):
    tok = ids_ref.shape[1]
    lane = lax.broadcasted_iota(jnp.int32, (tok, 128), 1)
    row = lax.broadcasted_iota(jnp.int32, (tok, tok), 0)
    col = lax.broadcasted_iota(jnp.int32, (tok, tok), 1)
    first, second = ids_ref[0, :, 0:1] ^ here, ids_ref[0, :, 1:2] ^ here
    chosen = (first == lane) | (second == lane)
    before = (col < row).astype(BF)
    rank = dot(before, chosen.astype(BF))
    slot = jnp.where(chosen, rank, -1.0)
    return first, second, slot


def placing(slot, k, slots):
    tok = slot.shape[0]
    lane = lax.broadcasted_iota(jnp.int32, (tok, 128), 1)
    return jnp.where(lane == slot[:, k : k + 1].astype(jnp.int32), 1.0, 0.0)


def pack(rows, slot, slots, out_refs):
    places = [placing(slot, k, slots).T[:slots] for k in range(len(out_refs))]
    table = jnp.concatenate(places, 0).astype(BF)
    packed = dot(table, rows).astype(BF)
    for k, out in enumerate(out_refs):
        out[...] = packed[k * slots : (k + 1) * slots]


def pack_kernel(slots, ids_ref, rows_ref, *out_refs):
    here = lax.axis_index("expert")
    _, _, slot = routing(ids_ref, here)
    pack(rows_ref[0], slot, slots, out_refs)


def attend_kernel(
    slots, q_ref, k_ref, v_ref, kp_ref, vp_ref, doc_ref, in_ref, gain_ref, ids_ref, att_ref, *out_refs
):
    tok = q_ref.shape[1]
    here = lax.axis_index("expert")
    first = (here * lax.axis_size("ctx") + lax.axis_index("ctx")) * tok
    before = jnp.maximum(first - tok, 0)
    own_docs = doc_ref[:, pl.ds(pl.multiple_of(first, tok), tok)]
    past_docs = doc_ref[:, pl.ds(pl.multiple_of(before, tok), tok)]
    row = lax.broadcasted_iota(jnp.int32, (tok, tok), 0)
    col = lax.broadcasted_iota(jnp.int32, (tok, tok), 1)
    own_all = jnp.broadcast_to(own_docs, (tok, tok))
    query_docs = own_all.T
    see_own = (query_docs == own_all) & (col <= row)
    see_past = (query_docs == past_docs) & (first > 0)
    scale = HD ** (-0.5)
    squares = jnp.zeros((tok, HD), F32)
    for h in range(q_ref.shape[2] // HD):
        at = slice(h * HD, (h + 1) * HD)
        q = q_ref[0, :, at]
        own = jnp.where(see_own, dot_t(q, k_ref[0, :, at]) * scale, -jnp.inf)
        past = jnp.where(see_past, dot_t(q, kp_ref[0, :, at]) * scale, -jnp.inf)
        top = jnp.maximum(own, past).max(axis=1, keepdims=True)
        own, past = jnp.exp(own - top), jnp.exp(past - top)
        total = (own + past).sum(axis=1, keepdims=True)
        inverse = 1.0 / total
        own, past = (own * inverse).astype(BF), (past * inverse).astype(BF)
        part = dot(own, v_ref[0, :, at]) + dot(past, vp_ref[0, :, at])
        part = part.astype(BF)
        att_ref[:, at] = part
        resid = in_ref[0, :, at].astype(F32) + part.astype(F32)
        squares = squares + resid * resid
    width = q_ref.shape[2]
    inv_rms = lax.rsqrt(squares.sum(axis=1, keepdims=True) / width + 1e-06)
    resid = in_ref[0].astype(F32) + att_ref[...].astype(F32)
    normed = (resid * inv_rms * gain_ref[...]).astype(BF)
    _, _, slot = routing(ids_ref, here)
    pack(normed, slot, slots, out_refs)


def load_pieces(piece_refs, whole_ref, sems, axis):
    mine = lax.axis_index("fsdp") * lax.axis_size("ctx") + lax.axis_index("ctx")
    size = piece_refs[0].shape[1 + axis]
    copies = []
    for j, piece in enumerate(piece_refs):
        at = pl.ds(pl.multiple_of((mine ^ j) * size, size), size)
        target = whole_ref.at[at, :] if axis == 0 else whole_ref.at[:, at]
        copies.append(pltpu.make_async_copy(piece.at[0], target, sems.at[j]))
    for copy in copies:
        copy.start()
    return copies


def wait_all(copies):
    for copy in copies:
        copy.wait()


def forward_kernel(peers, pieces, *refs):
    rows, refs = refs[:peers], refs[peers:]
    gates, refs = refs[:pieces], refs[pieces:]
    ups, refs = refs[:pieces], refs[pieces:]
    downs, refs = refs[:pieces], refs[pieces:]
    outs, refs = refs[:peers], refs[peers:]
    slope_ref, silu_ref, gate, up, down, x, hidden, sems = refs
    copies_g = load_pieces(gates, gate, sems.at[0], 0)
    copies_u = load_pieces(ups, up, sems.at[1], 0)
    copies_d = load_pieces(downs, down, sems.at[2], 1)
    slots = rows[0].shape[0]
    for k, block in enumerate(rows):
        x[k * slots : (k + 1) * slots] = block[...]
    wait_all(copies_g)
    wait_all(copies_u)
    step = 256
    for n in range(gate.shape[1] // step):
        at = slice(n * step, (n + 1) * step)
        gate_pre = dot(x[...], gate[:, at])
        up_pre = dot(x[...], up[:, at])
        sig = 1.0 / (1.0 + jnp.exp(-gate_pre))
        silu = gate_pre * sig
        hidden[:, at] = (silu * up_pre).astype(BF)
        slope_ref[:, at] = up_pre * sig * (1.0 + gate_pre * (1.0 - sig))
        silu_ref[:, at] = silu
    wait_all(copies_d)
    step = 512
    for n in range(down.shape[1] // step):
        at = slice(n * step, (n + 1) * step)
        part = dot(hidden[...], down[:, at]).astype(BF)
        for k, out in enumerate(outs):
            out[:, at] = part[k * slots : (k + 1) * slots]


def backward_kernel(peers, pieces, *refs):
    rows, refs = refs[:peers], refs[peers:]
    gates, refs = refs[:pieces], refs[pieces:]
    ups, refs = refs[:pieces], refs[pieces:]
    downs, refs = refs[:pieces], refs[pieces:]
    slope_ref, silu_ref, refs = refs[0], refs[1], refs[2:]
    outs, refs = refs[:peers], refs[peers:]
    gate, up, down, x, gate_grad, up_grad, sems = refs
    copies_d = load_pieces(downs, down, sems.at[2], 1)
    copies_g = load_pieces(gates, gate, sems.at[0], 0)
    copies_u = load_pieces(ups, up, sems.at[1], 0)
    slots = rows[0].shape[0]
    for k, block in enumerate(rows):
        x[k * slots : (k + 1) * slots] = block[...]
    wait_all(copies_d)
    step = 256
    for n in range(gate.shape[1] // step):
        at = slice(n * step, (n + 1) * step)
        hidden_grad = dot_t(x[...], down[at, :])
        gate_grad[:, at] = (hidden_grad * slope_ref[:, at]).astype(BF)
        up_grad[:, at] = (hidden_grad * silu_ref[:, at]).astype(BF)
    wait_all(copies_g)
    wait_all(copies_u)
    step = 512
    for n in range(gate.shape[0] // step):
        at = slice(n * step, (n + 1) * step)
        part = dot_t(gate_grad[...], gate[at, :]) + dot_t(up_grad[...], up[at, :])
        part = part.astype(BF)
        for k, out in enumerate(outs):
            out[:, at] = part[k * slots : (k + 1) * slots]


def mixed(ids_ref, weight_ref, backs, at, cache):
    if not cache:
        first, second, slot = routing(ids_ref, lax.axis_index("expert"))
        slots = backs[0].shape[0]
        for k in range(len(backs)):
            place = placing(slot, k, slots)[:, :slots].astype(BF)
            weight = jnp.where(first == k, weight_ref[0, :, 0:1], 0.0) + jnp.where(
                second == k, weight_ref[0, :, 1:2], 0.0
            )
            cache.append((place, weight))
    total = None
    for back, (place, weight) in zip(backs, cache):
        term = weight * dot(place, back[:, at])
        total = term if total is None else total + term
    return total


def layer_kernel(ids_ref, weight_ref, in_ref, att_ref, *refs):
    backs, out_ref = refs[:-1], refs[-1]
    step, cache = 512, []
    for n in range(in_ref.shape[2] // step):
        at = slice(n * step, (n + 1) * step)
        resid = in_ref[0, :, at].astype(F32) + att_ref[:, at].astype(F32)
        out_ref[0, :, at] = (resid + mixed(ids_ref, weight_ref, backs, at, cache)).astype(BF)


def grad_kernel(ids_ref, weight_ref, in_ref, att_ref, gain_ref, up_ref, *refs):
    backs, out_ref, gained_ref = refs[:-2], refs[-2], refs[-1]
    tok, width = in_ref.shape[1], in_ref.shape[2]
    step, cache = 512, []
    squares = jnp.zeros((tok, 1), F32)
    cross = jnp.zeros((tok, 1), F32)
    for n in range(width // step):
        at = slice(n * step, (n + 1) * step)
        resid = in_ref[0, :, at].astype(F32) + att_ref[:, at].astype(F32)
        gained = gain_ref[:, at] * mixed(ids_ref, weight_ref, backs, at, cache)
        gained_ref[:, at] = gained
        squares = squares + (resid * resid).sum(axis=1, keepdims=True)
        cross = cross + (resid * gained).sum(axis=1, keepdims=True)
    inv_rms = lax.rsqrt(squares / width + 1e-06)
    pull = inv_rms * inv_rms * inv_rms * (cross / width)
    for n in range(width // step):
        at = slice(n * step, (n + 1) * step)
        resid = in_ref[0, :, at].astype(F32) + att_ref[:, at].astype(F32)
        out_ref[0, :, at] = (
            up_ref[0, :, at].astype(F32) + inv_rms * gained_ref[:, at] - resid * pull
        ).astype(BF)


def shards(
    inputs, queries, keys, values, doc_ids, norm_gain, expert_ids, gate_weights, w_gate, w_up, w_down, out_grad
):
    tok, width = inputs.shape[1], inputs.shape[2]
    hidden_count = w_gate.shape[2]
    peers = lax.axis_size("expert")
    slots = 5 * tok // (2 * peers)
    slots = -(-slots // 16) * 16
    pieces = lax.axis_size("fsdp") * lax.axis_size("ctx")
    total = peers * slots
    slab = jax.ShapeDtypeStruct((slots, width), BF)
    slabs = [slab] * peers
    gain = norm_gain.reshape(1, width)

    prev_keys = shifted(keys, ("expert", "ctx"), 1)
    prev_values = shifted(values, ("expert", "ctx"), 1)

    def gathered(weight):
        blocks = []
        for dx in range(lax.axis_size("fsdp")):
            block = weight if dx == 0 else swapped(weight, "fsdp", dx)
            blocks.append(block)
            blocks.append(swapped(block, "ctx", 1))
        return blocks

    gates, ups, downs = gathered(w_gate), gathered(w_up), gathered(w_down)

    def exchanged(blocks):
        return [block if k == 0 else swapped(block, "expert", k) for k, block in enumerate(blocks)]

    sent_grads = pl.pallas_call(
        lambda *refs: pack_kernel(slots, *refs),
        out_shape=slabs,
        in_specs=[VM] * 2,
        out_specs=[VM] * peers,
        compiler_params=params(32),
        name="pack_grad",
    )(expert_ids, out_grad)
    grads = exchanged(sent_grads)

    attended, *sent_rows = pl.pallas_call(
        lambda *refs: attend_kernel(slots, *refs),
        out_shape=[jax.ShapeDtypeStruct((tok, width), BF)] + slabs,
        in_specs=[VM] * 9,
        out_specs=[VM] * (1 + peers),
        compiler_params=params(32),
        name="attend",
    )(queries, keys, values, prev_keys, prev_values, doc_ids, inputs, gain, expert_ids)
    rows = exchanged(sent_rows)

    wide = jax.ShapeDtypeStruct((total, hidden_count), F32)
    weights = [
        pltpu.VMEM((width, hidden_count), BF),
        pltpu.VMEM((width, hidden_count), BF),
        pltpu.VMEM((hidden_count, width), BF),
        pltpu.VMEM((total, width), BF),
    ]
    sems = pltpu.SemaphoreType.DMA((3, pieces))
    *served_out, slope, silu = pl.pallas_call(
        lambda *refs: forward_kernel(peers, pieces, *refs),
        out_shape=slabs + [wide] * 2,
        in_specs=[VM] * peers + [ANY] * (3 * pieces),
        out_specs=[VM] * (peers + 2),
        scratch_shapes=weights + [pltpu.VMEM((total, hidden_count), BF), sems],
        compiler_params=params(48),
        name="forward",
    )(*rows, *gates, *ups, *downs)
    back_out = exchanged(served_out)

    served_grad = pl.pallas_call(
        lambda *refs: backward_kernel(peers, pieces, *refs),
        out_shape=slabs,
        in_specs=[VM] * peers + [ANY] * (3 * pieces) + [VM] * 2,
        out_specs=[VM] * peers,
        scratch_shapes=weights + [pltpu.VMEM((total, hidden_count), BF)] * 2 + [sems],
        compiler_params=params(48),
        name="backward",
    )(*grads, *gates, *ups, *downs, slope, silu)
    back_grad = exchanged(served_grad)

    out_block = jax.ShapeDtypeStruct(inputs.shape, BF)
    layer_out = pl.pallas_call(
        layer_kernel,
        out_shape=out_block,
        in_specs=[VM] * (4 + peers),
        out_specs=VM,
        compiler_params=params(32),
        name="layer",
    )(expert_ids, gate_weights, inputs, attended, *back_out)
    input_grad = pl.pallas_call(
        grad_kernel,
        out_shape=out_block,
        in_specs=[VM] * (6 + peers),
        out_specs=VM,
        scratch_shapes=[pltpu.VMEM((tok, width), F32)],
        compiler_params=params(32),
        name="grad",
    )(expert_ids, gate_weights, inputs, attended, gain, out_grad, *back_grad)
    return layer_out, input_grad


def solution(mesh):
    rows = P(("groups", "fsdp"), ("expert", "ctx"), None)
    in_specs = (
        rows,
        rows,
        rows,
        rows,
        P(("groups", "fsdp"), None),
        P(),
        rows,
        rows,
        P("expert", ("fsdp", "ctx"), None),
        P("expert", ("fsdp", "ctx"), None),
        P("expert", None, ("fsdp", "ctx")),
        rows,
    )
    return jax.shard_map(shards, mesh=mesh, in_specs=in_specs, out_specs=(rows, rows), check_vma=False)
```

time: 203 us -> 194 us (0.956)
  the two profiles are of different devices: /device:TPU:0 before, /device:TPU:10 now
where the time goes in v1:
time: 194 us; the launch traced here: 193 us
  waiting for transfers between devices  131 us (68%)
  Pallas kernels  27.4 us (14%)
  starting transfers between devices  23.2 us (12%)
  local copies, waits for them, and re-layouts  11.4 us (6%)
    ppermute x21, waiting for transfers between devices, swapped(): return lax.ppermute(block, axis, [(i, i ^ distance) for i in range(count)])  123 us
    ppermute x21, starting transfers between devices, swapped(): return lax.ppermute(block, axis, [(i, i ^ distance) for i in range(count)])  17.7 us
    unnamed x42, local copies, waits for them, and re-layouts  11.4 us
    ppermute x2, waiting for transfers between devices, shifted(): return lax.ppermute(block, axis, route)  8.09 us
    pallas_call x1, Pallas kernels, shards(): pl.pallas_call(lambda *refs: backward_kernel(peers, pieces, *refs), out_s...  7.98 us
    pallas_call x1, Pallas kernels, shards(): pl.pallas_call(lambda *refs: forward_kernel(peers, pieces, *refs), out_sh...  7.03 us
    pallas_call x1, Pallas kernels, shards(): pl.pallas_call(lambda *refs: attend_kernel(slots, *refs), out_shape=[jax....  6.33 us
    ppermute x2, starting transfers between devices, shifted(): return lax.ppermute(block, axis, route)  5.51 us
  transfers between devices with their start and end apart: 23, of which 13 were waited for; matrix products, arithmetic and copies ran while one was open for 0% of the time, Pallas kernels for 13%

profile of v1, /device:TPU:10, one launch (start us, length us, event | category | flops | bytes accessed | tf_op | source)
XLA Modules:
  0.0 193.5 jit_solution(18222018821156047073)
XLA Ops:
  0.6 1.9 collective-permute-start
  2.6 3.6 %collective-permute-start.1 = (bf16[1,128,2048]{2,1,0:T(8,128)(2,1)}, bf16[1,128,2048]{2,1,0:T(8,128)(2,1)S(1)}, u32[]{:S(2)}, u32[]{:S(2)}) collective-permute-start(bf16[1,128,2048]{2,1,0:T(8,128)(2,1)} %refs_2_.1), channel_id=1, source_target_pairs={{0,1},{1,4},{4,5},{5,8},{8,9},{9,12},{12,13},{2,3},{3,6},{6,7},{7,... | collective-permute-start | bytes 1572872 | tf_op jit(solution)/shard_map/ppermute | solution.py:29
  8.3 3.0 %collective-permute-done.refs_3_ = bf16[1,128,2048]{2,1,0:T(8,128)(2,1)S(1)} collective-permute-done((bf16[1,128,2048]{2,1,0:T(8,128)(2,1)}, bf16[1,128,2048]{2,1,0:T(8,128)(2,1)S(1)}, u32[]{:S(2)}, u32[]{:S(2)}) %collective-permute-start) | collective-permute-done | bytes 524320 | tf_op jit(solution)/shard_map/ppermute | solution.py:29
  11.9 5.1 %collective-permute-done.1.refs_4_ = bf16[1,128,2048]{2,1,0:T(8,128)(2,1)S(1)} collective-permute-done((bf16[1,128,2048]{2,1,0:T(8,128)(2,1)}, bf16[1,128,2048]{2,1,0:T(8,128)(2,1)S(1)}, u32[]{:S(2)}, u32[]{:S(2)}) %collective-permute-start.1) | collective-permute-done | bytes 524320 | tf_op jit(solution)/shard_map/ppermute | solution.py:29
  18.3 8.6 %collective-permute-done.6.refs_6_ = bf16[1,512,768]{2,1,0:T(8,128)(2,1)S(1)} collective-permute-done((bf16[1,512,768]{2,1,0:T(8,128)(2,1)}, bf16[1,512,768]{2,1,0:T(8,128)(2,1)S(1)}, u32[]{:S(2)}, u32[]{:S(2)}) %collective-permute-start.6) | collective-permute-done | bytes 786464 | tf_op jit(solution)/shard_map/ppermute | solution.py:23
  26.9 17.0 %collective-permute-done.9.refs_10_ = bf16[1,512,768]{2,1,0:T(8,128)(2,1)} collective-permute-done((bf16[1,512,768]{2,1,0:T(8,128)(2,1)}, bf16[1,512,768]{2,1,0:T(8,128)(2,1)}, u32[]{:S(2)}, u32[]{:S(2)}) %collective-permute-start.9) | collective-permute-done | bytes 786464 | tf_op jit(solution)/shard_map/ppermute | solution.py:23
  43.8 16.4 %collective-permute-done.12.refs_14_ = bf16[1,768,512]{2,1,0:T(8,128)(2,1)} collective-permute-done((bf16[1,768,512]{2,1,0:T(8,128)(2,1)}, bf16[1,768,512]{2,1,0:T(8,128)(2,1)}, u32[]{:S(2)}, u32[]{:S(2)}) %collective-permute-start.12) | collective-permute-done | bytes 786464 | tf_op jit(solution)/shard_map/ppermute | solution.py:23
  66.3 6.3 %attend.1 = (bf16[128,2048]{1,0:T(8,128)(2,1)S(1)}, bf16[80,2048]{1,0:T(8,128)(2,1)S(1)}, bf16[80,2048]{1,0:T(8,128)(2,1)S(1)}, bf16[80,2048]{1,0:T(8,128)(2,1)S(1)}, bf16[80,2048]{1,0:T(8,128)(2,1)S(1)}) custom-call(bf16[1,128,2048]{2,1,0:T(8,128)(2,1)S(1)} %copy-done.6, bf16[1,128,2048]{2,1,0:T(8,128)(2,1)S(1)} %copy-done.7, ...), custom_call_target="tpu_custom_call" | custom-call | tf_op jit(solution)/shard_map/attend/pallas_call | solution.py:286
  73.2 2.6 %collective-permute-start.3 = (bf16[80,2048]{1,0:T(8,128)(2,1)S(1)}, bf16[80,2048]{1,0:T(8,128)(2,1)S(1)}, u32[]{:S(2)}, u32[]{:S(2)}) collective-permute-start(bf16[80,2048]{1,0:T(8,128)(2,1)S(1)} %get-tuple-element.24), channel_id=1, source_target_pairs={{0,8},{4,12},{8,0},{12,4},{1,9},{5,13},{9,1},{13,5},{2,10},{6,14},... | collective-permute-start | bytes 983048 | tf_op jit(solution)/shard_map/ppermute | solution.py:23
  75.7 12.0 %collective-permute-done.2.refs_1_ = bf16[80,2048]{1,0:T(8,128)(2,1)S(1)} collective-permute-done((bf16[80,2048]{1,0:T(8,128)(2,1)S(1)}, bf16[80,2048]{1,0:T(8,128)(2,1)S(1)}, u32[]{:S(2)}, u32[]{:S(2)}) %collective-permute-start.2) | collective-permute-done | bytes 327712 | tf_op jit(solution)/shard_map/ppermute | solution.py:23
  88.9 2.1 %collective-permute-done.3.refs_2_ = bf16[80,2048]{1,0:T(8,128)(2,1)S(1)} collective-permute-done((bf16[80,2048]{1,0:T(8,128)(2,1)S(1)}, bf16[80,2048]{1,0:T(8,128)(2,1)S(1)}, u32[]{:S(2)}, u32[]{:S(2)}) %collective-permute-start.3) | collective-permute-done | bytes 327712 | tf_op jit(solution)/shard_map/ppermute | solution.py:23
  92.6 12.5 %collective-permute-done.4.refs_3_ = bf16[80,2048]{1,0:T(8,128)(2,1)S(1)} collective-permute-done((bf16[80,2048]{1,0:T(8,128)(2,1)S(1)}, bf16[80,2048]{1,0:T(8,128)(2,1)S(1)}, u32[]{:S(2)}, u32[]{:S(2)}) %collective-permute-start.4) | collective-permute-done | bytes 327712 | tf_op jit(solution)/shard_map/ppermute | solution.py:23
  105.1 1.6 collective-permute-start.19
  106.8 7.0 %forward.1 = (bf16[80,2048]{1,0:T(8,128)(2,1)S(1)}, bf16[80,2048]{1,0:T(8,128)(2,1)S(1)}, bf16[80,2048]{1,0:T(8,128)(2,1)}, bf16[80,2048]{1,0:T(8,128)(2,1)}, f32[320,768]{1,0:T(8,128)}, /*index=5*/f32[320,768]{1,0:T(8,128)}) custom-call(bf16[80,2048]{1,0:T(8,128)(2,1)S(1)} %get-tuple-element.22.refs_0_, ...), custom_call_target="tpu_custom_call" | custom-call | tf_op jit(solution)/shard_map/forward/pallas_call | solution.py:304
  113.8 2.8 %collective-permute-start.14 = (bf16[80,2048]{1,0:T(8,128)(2,1)S(1)}, bf16[80,2048]{1,0:T(8,128)(2,1)S(1)}, u32[]{:S(2)}, u32[]{:S(2)}) collective-permute-start(bf16[80,2048]{1,0:T(8,128)(2,1)S(1)} %get-tuple-element.27), channel_id=1, source_target_pairs={{0,4},{4,0},{8,12},{12,8},{1,5},{5,1},{9,13},{13,9},{2,6},{6,2},{1... | collective-permute-start | bytes 983048 | tf_op jit(solution)/shard_map/ppermute | solution.py:23
  118.2 9.2 %collective-permute-done.18.refs_2_ = bf16[80,2048]{1,0:T(8,128)(2,1)S(1)} collective-permute-done((bf16[80,2048]{1,0:T(8,128)(2,1)S(1)}, bf16[80,2048]{1,0:T(8,128)(2,1)S(1)}, u32[]{:S(2)}, u32[]{:S(2)}) %collective-permute-start.18) | collective-permute-done | bytes 327712 | tf_op jit(solution)/shard_map/ppermute | solution.py:23
  127.4 23.1 %collective-permute-done.19.refs_3_ = bf16[80,2048]{1,0:T(8,128)(2,1)S(1)} collective-permute-done((bf16[80,2048]{1,0:T(8,128)(2,1)S(1)}, bf16[80,2048]{1,0:T(8,128)(2,1)S(1)}, u32[]{:S(2)}, u32[]{:S(2)}) %collective-permute-start.19) | collective-permute-done | bytes 327712 | tf_op jit(solution)/shard_map/ppermute | solution.py:23
  150.4 8.0 %backward.1 = (bf16[80,2048]{1,0:T(8,128)(2,1)S(1)}, bf16[80,2048]{1,0:T(8,128)(2,1)}, bf16[80,2048]{1,0:T(8,128)(2,1)}, bf16[80,2048]{1,0:T(8,128)(2,1)}) custom-call(bf16[80,2048]{1,0:T(8,128)(2,1)S(1)} %get-tuple-element.30.refs_0_, bf16[80,2048]{1,0:T(8,128)(2,1)S(1)} %collective-permute-done.17.refs_1_, ...), custom_call_target="tpu_custom_call" | custom-call | tf_op jit(solution)/shard_map/backward/pallas_call | solution.py:315
  159.2 1.8 collective-permute-start.21
  161.7 1.6 collective-permute-start.22
  167.6 2.9 %layer.1 = bf16[1,128,2048]{2,1,0:T(8,128)(2,1)} custom-call(s32[1,128,2]{2,1,0:T(8,128)S(1)} %copy.15.refs_8_.ids_ref.refs_0_, f32[1,128,2]{2,1,0:T(8,128)S(1)} %copy.16.weight_ref, bf16[1,128,2048]{2,1,0:T(8,128)(2,1)S(1)} %copy-done.1, bf16[128,2048]{1,0:T(8,128)(2,1)S(1)} %copy-done.5, bf16[80,2048]{1,0:T(8,128)(2,1)S(1)} %copy-done.12, ...), custom_call_target="tpu_custom_call" | custom-call | tf_op jit(solution)/shard_map/layer/pallas_call | solution.py:327
  170.5 13.0 %collective-permute-done.21.refs_2_ = bf16[80,2048]{1,0:T(8,128)(2,1)S(1)} collective-permute-done((bf16[80,2048]{1,0:T(8,128)(2,1)}, bf16[80,2048]{1,0:T(8,128)(2,1)S(1)}, u32[]{:S(2)}, u32[]{:S(2)}) %collective-permute-start.21) | collective-permute-done | bytes 327712 | tf_op jit(solution)/shard_map/ppermute | solution.py:23
  183.6 7.7 %collective-permute-done.22.refs_3_ = bf16[80,2048]{1,0:T(8,128)(2,1)S(1)} collective-permute-done((bf16[80,2048]{1,0:T(8,128)(2,1)}, bf16[80,2048]{1,0:T(8,128)(2,1)S(1)}, u32[]{:S(2)}, u32[]{:S(2)}) %collective-permute-start.22) | collective-permute-done | bytes 327712 | tf_op jit(solution)/shard_map/ppermute | solution.py:23
  191.3 2.2 %grad.1 = bf16[1,128,2048]{2,1,0:T(8,128)(2,1)} custom-call(s32[1,128,2]{2,1,0:T(8,128)S(1)} %copy.15.refs_8_.ids_ref.refs_0_, f32[1,128,2]{2,1,0:T(8,128)S(1)} %copy.16.weight_ref, bf16[1,128,2048]{2,1,0:T(8,128)(2,1)S(1)} %copy-done.1, bf16[128,2048]{1,0:T(8,128)(2,1)S(1)} %copy-done.5, f32[1,2048]{1,0:T(1,128)S(1)} %bitcast.2, ...), custom_call_target="tpu_custom_call" | custom-call | tf_op jit(solution)/shard_map/grad/pallas_call | solution.py:335
  (70 shorter events, 20.6 us)
Async XLA Ops:
  0.6 60.4 %copy-start.17 = (f32[2048]{0:T(1024)S(1)}, f32[2048]{0:T(1024)}, u32[]{:S(2)}) copy-start(f32[2048]{0:T(1024)} %param.17) | copy-start | bytes 24580
  0.6 10.7 %collective-permute-start = (bf16[1,128,2048]{2,1,0:T(8,128)(2,1)}, bf16[1,128,2048]{2,1,0:T(8,128)(2,1)S(1)}, u32[]{:S(2)}, u32[]{:S(2)}) collective-permute-start(bf16[1,128,2048]{2,1,0:T(8,128)(2,1)} %refs_1_.2), channel_id=1, source_target_pairs={{0,1},{1,4},{4,5},{5,8},{8,9},{9,12},{12,13},{2,3},{3,6},{6,7},{7,... | collective-permute-start | bytes 1572872 | tf_op jit(solution)/shard_map/ppermute | solution.py:29
  2.6 14.4 %collective-permute-start.1 = (bf16[1,128,2048]{2,1,0:T(8,128)(2,1)}, bf16[1,128,2048]{2,1,0:T(8,128)(2,1)S(1)}, u32[]{:S(2)}, u32[]{:S(2)}) collective-permute-start(bf16[1,128,2048]{2,1,0:T(8,128)(2,1)} %refs_2_.1), channel_id=1, source_target_pairs={{0,1},{1,4},{4,5},{5,8},{8,9},{9,12},{12,13},{2,3},{3,6},{6,7},{7,... | collective-permute-start | bytes 1572872 | tf_op jit(solution)/shard_map/ppermute | solution.py:29
  6.2 11.6 %collective-permute-start.5 = (bf16[1,512,768]{2,1,0:T(8,128)(2,1)}, bf16[1,512,768]{2,1,0:T(8,128)(2,1)S(1)}, u32[]{:S(2)}, u32[]{:S(2)}) collective-permute-start(bf16[1,512,768]{2,1,0:T(8,128)(2,1)} %refs_4_.3), channel_id=1, source_target_pairs={{0,1},{1,0},{2,3},{3,2},{4,5},{5,4},{6,7},{7,6},{8,9},{9,8},{10,11... | collective-permute-start | bytes 2359304 | tf_op jit(solution)/shard_map/ppermute | solution.py:23
  6.2 20.6 %collective-permute-start.6 = (bf16[1,512,768]{2,1,0:T(8,128)(2,1)}, bf16[1,512,768]{2,1,0:T(8,128)(2,1)S(1)}, u32[]{:S(2)}, u32[]{:S(2)}) collective-permute-start(bf16[1,512,768]{2,1,0:T(8,128)(2,1)} %refs_4_.3), channel_id=1, source_target_pairs={{0,2},{2,0},{1,3},{3,1},{4,6},{6,4},{5,7},{7,5},{8,10},{10,8},{9,1... | collective-permute-start | bytes 2359304 | tf_op jit(solution)/shard_map/ppermute | solution.py:23
  6.8 37.0 %collective-permute-start.9 = (bf16[1,512,768]{2,1,0:T(8,128)(2,1)}, bf16[1,512,768]{2,1,0:T(8,128)(2,1)}, u32[]{:S(2)}, u32[]{:S(2)}) collective-permute-start(bf16[1,512,768]{2,1,0:T(8,128)(2,1)} %refs_8_.4), channel_id=1, source_target_pairs={{0,2},{2,0},{1,3},{3,1},{4,6},{6,4},{5,7},{7,5},{8,10},{10,8},{9,1... | collective-permute-start | bytes 2359304 | tf_op jit(solution)/shard_map/ppermute | solution.py:23
  11.4 48.9 %collective-permute-start.12 = (bf16[1,768,512]{2,1,0:T(8,128)(2,1)}, bf16[1,768,512]{2,1,0:T(8,128)(2,1)}, u32[]{:S(2)}, u32[]{:S(2)}) collective-permute-start(bf16[1,768,512]{2,1,0:T(8,128)(2,1)} %refs_12_.3), channel_id=1, source_target_pairs={{0,2},{2,0},{1,3},{3,1},{4,6},{6,4},{5,7},{7,5},{8,10},{10,8},{9,1... | collective-permute-start | bytes 2359304 | tf_op jit(solution)/shard_map/ppermute | solution.py:23
  17.8 54.9 %collective-permute-start.8 = (bf16[1,512,768]{2,1,0:T(8,128)(2,1)}, bf16[1,512,768]{2,1,0:T(8,128)(2,1)}, u32[]{:S(2)}, u32[]{:S(2)}) collective-permute-start(bf16[1,512,768]{2,1,0:T(8,128)(2,1)} %refs_8_.4), channel_id=1, source_target_pairs={{0,1},{1,0},{2,3},{3,2},{4,5},{5,4},{6,7},{7,6},{8,9},{9,8},{10,11... | collective-permute-start | bytes 2359304 | tf_op jit(solution)/shard_map/ppermute | solution.py:23
  17.8 55.4 %collective-permute-start.11 = (bf16[1,768,512]{2,1,0:T(8,128)(2,1)}, bf16[1,768,512]{2,1,0:T(8,128)(2,1)}, u32[]{:S(2)}, u32[]{:S(2)}) collective-permute-start(bf16[1,768,512]{2,1,0:T(8,128)(2,1)} %refs_12_.3), channel_id=1, source_target_pairs={{0,1},{1,0},{2,3},{3,2},{4,5},{5,4},{6,7},{7,6},{8,9},{9,8},{10,11... | collective-permute-start | bytes 2359304 | tf_op jit(solution)/shard_map/ppermute | solution.py:23
  26.9 78.2 %collective-permute-start.7 = (bf16[1,512,768]{2,1,0:T(8,128)(2,1)S(1)}, bf16[1,512,768]{2,1,0:T(8,128)(2,1)S(1)}, u32[]{:S(2)}, u32[]{:S(2)}) collective-permute-start(bf16[1,512,768]{2,1,0:T(8,128)(2,1)S(1)} %collective-permute-done.6.refs_6_), channel_id=1, source_target_pairs={{0,1},{1,0},{2,3},{3,2},{4,5},{5,4},{6,7},{7,6},{8,9},{9,8},{10,11... | collective-permute-start | bytes 2359304 | tf_op jit(solution)/shard_map/ppermute | solution.py:23
  43.8 62.9 %collective-permute-start.10 = (bf16[1,512,768]{2,1,0:T(8,128)(2,1)}, bf16[1,512,768]{2,1,0:T(8,128)(2,1)}, u32[]{:S(2)}, u32[]{:S(2)}) collective-permute-start(bf16[1,512,768]{2,1,0:T(8,128)(2,1)} %collective-permute-done.9.refs_10_), channel_id=1, source_target_pairs={{0,1},{1,0},{2,3},{3,2},{4,5},{5,4},{6,7},{7,6},{8,9},{9,8},{10,11... | collective-permute-start | bytes 2359304 | tf_op jit(solution)/shard_map/ppermute | solution.py:23
  60.2 46.5 %collective-permute-start.13 = (bf16[1,768,512]{2,1,0:T(8,128)(2,1)}, bf16[1,768,512]{2,1,0:T(8,128)(2,1)}, u32[]{:S(2)}, u32[]{:S(2)}) collective-permute-start(bf16[1,768,512]{2,1,0:T(8,128)(2,1)} %collective-permute-done.12.refs_14_), channel_id=1, source_target_pairs={{0,1},{1,0},{2,3},{3,2},{4,5},{5,4},{6,7},{7,6},{8,9},{9,8},{10,11... | collective-permute-start | bytes 2359304 | tf_op jit(solution)/shard_map/ppermute | solution.py:23
  72.6 15.1 %collective-permute-start.2 = (bf16[80,2048]{1,0:T(8,128)(2,1)S(1)}, bf16[80,2048]{1,0:T(8,128)(2,1)S(1)}, u32[]{:S(2)}, u32[]{:S(2)}) collective-permute-start(bf16[80,2048]{1,0:T(8,128)(2,1)S(1)} %get-tuple-element.23), channel_id=1, source_target_pairs={{0,4},{4,0},{8,12},{12,8},{1,5},{5,1},{9,13},{13,9},{2,6},{6,2},{1... | collective-permute-start | bytes 983048 | tf_op jit(solution)/shard_map/ppermute | solution.py:23
  73.2 17.8 %collective-permute-start.3 = (bf16[80,2048]{1,0:T(8,128)(2,1)S(1)}, bf16[80,2048]{1,0:T(8,128)(2,1)S(1)}, u32[]{:S(2)}, u32[]{:S(2)}) collective-permute-start(bf16[80,2048]{1,0:T(8,128)(2,1)S(1)} %get-tuple-element.24), channel_id=1, source_target_pairs={{0,8},{4,12},{8,0},{12,4},{1,9},{5,13},{9,1},{13,5},{2,10},{6,14},... | collective-permute-start | bytes 983048 | tf_op jit(solution)/shard_map/ppermute | solution.py:23
  87.7 17.4 %collective-permute-start.4 = (bf16[80,2048]{1,0:T(8,128)(2,1)S(1)}, bf16[80,2048]{1,0:T(8,128)(2,1)S(1)}, u32[]{:S(2)}, u32[]{:S(2)}) collective-permute-start(bf16[80,2048]{1,0:T(8,128)(2,1)S(1)} %get-tuple-element.25), channel_id=1, source_target_pairs={{0,12},{4,8},{8,4},{12,0},{1,13},{5,9},{9,5},{13,1},{2,14},{6,10},... | collective-permute-start | bytes 983048 | tf_op jit(solution)/shard_map/ppermute | solution.py:23
  90.9 26.8 %collective-permute-start.17 = (bf16[80,2048]{1,0:T(8,128)(2,1)S(1)}, bf16[80,2048]{1,0:T(8,128)(2,1)S(1)}, u32[]{:S(2)}, u32[]{:S(2)}) collective-permute-start(bf16[80,2048]{1,0:T(8,128)(2,1)S(1)} %get-tuple-element.31), channel_id=1, source_target_pairs={{0,4},{4,0},{8,12},{12,8},{1,5},{5,1},{9,13},{13,9},{2,6},{6,2},{1... | collective-permute-start | bytes 983048 | tf_op jit(solution)/shard_map/ppermute | solution.py:23
  105.1 22.3 %collective-permute-start.18 = (bf16[80,2048]{1,0:T(8,128)(2,1)S(1)}, bf16[80,2048]{1,0:T(8,128)(2,1)S(1)}, u32[]{:S(2)}, u32[]{:S(2)}) collective-permute-start(bf16[80,2048]{1,0:T(8,128)(2,1)S(1)} %get-tuple-element.32), channel_id=1, source_target_pairs={{0,8},{4,12},{8,0},{12,4},{1,9},{5,13},{9,1},{13,5},{2,10},{6,14},... | collective-permute-start | bytes 983048 | tf_op jit(solution)/shard_map/ppermute | solution.py:23
  105.1 45.3 %collective-permute-start.19 = (bf16[80,2048]{1,0:T(8,128)(2,1)S(1)}, bf16[80,2048]{1,0:T(8,128)(2,1)S(1)}, u32[]{:S(2)}, u32[]{:S(2)}) collective-permute-start(bf16[80,2048]{1,0:T(8,128)(2,1)S(1)} %get-tuple-element.33), channel_id=1, source_target_pairs={{0,12},{4,8},{8,4},{12,0},{1,13},{5,9},{9,5},{13,1},{2,14},{6,10},... | collective-permute-start | bytes 983048 | tf_op jit(solution)/shard_map/ppermute | solution.py:23
  113.8 47.2 %collective-permute-start.14 = (bf16[80,2048]{1,0:T(8,128)(2,1)S(1)}, bf16[80,2048]{1,0:T(8,128)(2,1)S(1)}, u32[]{:S(2)}, u32[]{:S(2)}) collective-permute-start(bf16[80,2048]{1,0:T(8,128)(2,1)S(1)} %get-tuple-element.27), channel_id=1, source_target_pairs={{0,4},{4,0},{8,12},{12,8},{1,5},{5,1},{9,13},{13,9},{2,6},{6,2},{1... | collective-permute-start | bytes 983048 | tf_op jit(solution)/shard_map/ppermute | solution.py:23
  116.6 46.9 %collective-permute-start.15 = (bf16[80,2048]{1,0:T(8,128)(2,1)}, bf16[80,2048]{1,0:T(8,128)(2,1)}, u32[]{:S(2)}, u32[]{:S(2)}) collective-permute-start(bf16[80,2048]{1,0:T(8,128)(2,1)} %get-tuple-element.28), channel_id=1, source_target_pairs={{0,8},{4,12},{8,0},{12,4},{1,9},{5,13},{9,1},{13,5},{2,10},{6,14},... | collective-permute-start | bytes 983048 | tf_op jit(solution)/shard_map/ppermute | solution.py:23
  117.7 46.9 %collective-permute-start.16 = (bf16[80,2048]{1,0:T(8,128)(2,1)}, bf16[80,2048]{1,0:T(8,128)(2,1)}, u32[]{:S(2)}, u32[]{:S(2)}) collective-permute-start(bf16[80,2048]{1,0:T(8,128)(2,1)} %get-tuple-element.29), channel_id=1, source_target_pairs={{0,12},{4,8},{8,4},{12,0},{1,13},{5,9},{9,5},{13,1},{2,14},{6,10},... | collective-permute-start | bytes 983048 | tf_op jit(solution)/shard_map/ppermute | solution.py:23
  159.2 11.4 %collective-permute-start.20 = (bf16[80,2048]{1,0:T(8,128)(2,1)}, bf16[80,2048]{1,0:T(8,128)(2,1)S(1)}, u32[]{:S(2)}, u32[]{:S(2)}) collective-permute-start(bf16[80,2048]{1,0:T(8,128)(2,1)} %get-tuple-element.37), channel_id=1, source_target_pairs={{0,4},{4,0},{8,12},{12,8},{1,5},{5,1},{9,13},{13,9},{2,6},{6,2},{1... | collective-permute-start | bytes 983048 | tf_op jit(solution)/shard_map/ppermute | solution.py:23
  159.2 24.4 %collective-permute-start.21 = (bf16[80,2048]{1,0:T(8,128)(2,1)}, bf16[80,2048]{1,0:T(8,128)(2,1)S(1)}, u32[]{:S(2)}, u32[]{:S(2)}) collective-permute-start(bf16[80,2048]{1,0:T(8,128)(2,1)} %get-tuple-element.38), channel_id=1, source_target_pairs={{0,8},{4,12},{8,0},{12,4},{1,9},{5,13},{9,1},{13,5},{2,10},{6,14},... | collective-permute-start | bytes 983048 | tf_op jit(solution)/shard_map/ppermute | solution.py:23
  161.7 29.5 %collective-permute-start.22 = (bf16[80,2048]{1,0:T(8,128)(2,1)}, bf16[80,2048]{1,0:T(8,128)(2,1)S(1)}, u32[]{:S(2)}, u32[]{:S(2)}) collective-permute-start(bf16[80,2048]{1,0:T(8,128)(2,1)} %get-tuple-element.39), channel_id=1, source_target_pairs={{0,12},{4,8},{8,4},{12,0},{1,13},{5,9},{9,5},{13,1},{2,14},{6,10},... | collective-permute-start | bytes 983048 | tf_op jit(solution)/shard_map/ppermute | solution.py:23
  (19 other events, 192.6 us)

commit v2 on v1

--- a/solution.py
+++ b/solution.py
@@ -27,6 +27,10 @@
     devices = range(lax.axis_size(axis))
     route = [(i - distance, i) for i in devices if i - distance in devices]
     return lax.ppermute(block, axis, route)
+
+
+def after(block, other):
+    return lax.optimization_barrier((block, other))[0]
 
 
 def dot(a, b):
@@ -243,7 +247,7 @@
         ).astype(BF)
 
 
-def shards(
+def slot_shards(
     inputs, queries, keys, values, doc_ids, norm_gain, expert_ids, gate_weights, w_gate, w_up, w_down, out_grad
 ):
     tok, width = inputs.shape[1], inputs.shape[2]
@@ -261,12 +265,7 @@
     prev_values = shifted(values, ("expert", "ctx"), 1)
 
     def gathered(weight):
-        blocks = []
-        for dx in range(lax.axis_size("fsdp")):
-            block = weight if dx == 0 else swapped(weight, "fsdp", dx)
-            blocks.append(block)
-            blocks.append(swapped(block, "ctx", 1))
-        return blocks
+        return [weight if dx == 0 else swapped(weight, "fsdp", dx) for dx in range(lax.axis_size("fsdp"))]
 
     gates, ups, downs = gathered(w_gate), gathered(w_up), gathered(w_down)
 
@@ -282,6 +281,7 @@
         name="pack_grad",
     )(expert_ids, out_grad)
     grads = exchanged(sent_grads)
+    queries = after(queries, sent_grads[0])
 
     attended, *sent_rows = pl.pallas_call(
         lambda *refs: attend_kernel(slots, *refs),
@@ -292,6 +292,11 @@
         name="attend",
     )(queries, keys, values, prev_keys, prev_values, doc_ids, inputs, gain, expert_ids)
     rows = exchanged(sent_rows)
+
+    def spread(blocks):
+        return [part for block in blocks for part in (block, swapped(after(block, attended), "ctx", 1))]
+
+    gates, ups, downs = spread(gates), spread(ups), spread(downs)
 
     wide = jax.ShapeDtypeStruct((total, hidden_count), F32)
     weights = [
@@ -344,6 +349,363 @@
     return layer_out, input_grad
 
 
+def ready(block, *others):
+    return lax.optimization_barrier((block, *others))[0]
+
+
+def lay_kernel(g_ref, u_ref, d_ref, ids_ref, weight_ref, near_ref, far_ref, *refs):
+    near, far, router_ref = refs[:3], refs[3:6], refs[6]
+    half = g_ref.shape[2] // 2
+    unit = half // 3
+    group = lax.axis_index("groups")
+    for whole, units, start in ((near_ref, near, group), (far_ref, far, 1 - group)):
+        at = pl.ds(pl.multiple_of(start * half, half), half)
+        for i, block in enumerate((g_ref[0, :, at], u_ref[0, :, at], d_ref[0, at, :].T)):
+            whole[i] = block
+            for n in range(3):
+                units[n][i] = block[:, n * unit : (n + 1) * unit]
+    here = lax.axis_index("expert")
+    lane = lax.broadcasted_iota(jnp.int32, router_ref.shape, 1)
+    first, second = ids_ref[0, :, 0:1] ^ here, ids_ref[0, :, 1:2] ^ here
+    router_ref[...] = jnp.where(first == lane, weight_ref[0, :, 0:1], 0.0) + jnp.where(
+        second == lane, weight_ref[0, :, 1:2], 0.0
+    )
+
+
+def attend_rows(q_ref, k_ref, v_ref, kp_ref, vp_ref, doc_ref, in_ref, gain_ref, att_ref):
+    tok, width = q_ref.shape[1], q_ref.shape[2]
+    first = (lax.axis_index("expert") * lax.axis_size("ctx") + lax.axis_index("ctx")) * tok
+    before = jnp.maximum(first - tok, 0)
+    own_docs = doc_ref[:, pl.ds(pl.multiple_of(first, tok), tok)]
+    past_docs = doc_ref[:, pl.ds(pl.multiple_of(before, tok), tok)]
+    row = lax.broadcasted_iota(jnp.int32, (tok, tok), 0)
+    col = lax.broadcasted_iota(jnp.int32, (tok, tok), 1)
+    own_all = jnp.broadcast_to(own_docs, (tok, tok))
+    query_docs = own_all.T
+    see_own = (query_docs == own_all) & (col <= row)
+    see_past = (query_docs == past_docs) & (first > 0)
+    scale = HD ** (-0.5)
+    squares = jnp.zeros((tok, HD), F32)
+    for h in range(width // HD):
+        at = slice(h * HD, (h + 1) * HD)
+        q = q_ref[0, :, at]
+        own = jnp.where(see_own, dot_t(q, k_ref[0, :, at]) * scale, -jnp.inf)
+        past = jnp.where(see_past, dot_t(q, kp_ref[0, :, at]) * scale, -jnp.inf)
+        top = jnp.maximum(own, past).max(axis=1, keepdims=True)
+        own, past = jnp.exp(own - top), jnp.exp(past - top)
+        total = (own + past).sum(axis=1, keepdims=True)
+        inverse = 1.0 / total
+        own, past = (own * inverse).astype(BF), (past * inverse).astype(BF)
+        part = dot(own, v_ref[0, :, at]) + dot(past, vp_ref[0, :, at])
+        part = part.astype(BF)
+        att_ref[:, at] = part
+        resid = in_ref[0, :, at].astype(F32) + part.astype(F32)
+        squares = squares + resid * resid
+    inv_rms = lax.rsqrt(squares.sum(axis=1, keepdims=True) / width + 1e-06)
+    resid = in_ref[0].astype(F32) + att_ref[...].astype(F32)
+    return (resid * inv_rms * gain_ref[...]).astype(BF)
+
+
+def normed_kernel(*refs):
+    refs[-1][...] = attend_rows(*refs[:-1])
+
+
+def load_units(groups, piece_refs, whole_ref, sems):
+    mine = lax.axis_index("fsdp") * lax.axis_size("ctx") + lax.axis_index("ctx")
+    copies, start = [], 0
+    for g, (_, count) in enumerate(groups):
+        for j in range(4):
+            piece = piece_refs[4 * g + j]
+            size = piece.shape[1]
+            at = pl.ds(pl.multiple_of((mine ^ j) * size, size), size)
+            target = whole_ref.at[:, at, start : start + count]
+            copies.append(pltpu.make_async_copy(piece, target, sems.at[4 * g + j]))
+        start += count
+    for copy in copies:
+        copy.start()
+    return copies
+
+
+def spans(groups):
+    found, start = [], 0
+    for expert, count in groups:
+        if found and found[-1][0] == expert and found[-1][2] - found[-1][1] + count <= 256:
+            found[-1][2] = start + count
+        else:
+            found.append([expert, start, start + count])
+        start += count
+    return found
+
+
+def join(x, own_ref, pair_ref):
+    tok = x.shape[0] // 2
+    own, pair = own_ref, pair_ref
+    x[:tok] = own[...].reshape(tok, x.shape[1])
+    x[tok:] = pair[...].reshape(tok, x.shape[1])
+
+
+def router_columns(router_ref, pair_router_ref):
+    return [
+        jnp.concatenate([router_ref[:, 2 * e : 2 * e + 1], pair_router_ref[:, 2 * e + 1 : 2 * e + 2]], 0)
+        for e in range(2)
+    ]
+
+
+def slice_grads(groups, whole, x, y, hidden, gate_grad, up_grad):
+    for _, lo, hi in spans(groups):
+        gate_pre = dot(x[...], whole[0, :, lo:hi])
+        up_pre = dot(x[...], whole[1, :, lo:hi])
+        hidden_grad = dot(y[...], whole[2, :, lo:hi])
+        sig = 1.0 / (1.0 + jnp.exp(-gate_pre))
+        silu = gate_pre * sig
+        hidden[:, lo:hi] = (silu * up_pre).astype(BF)
+        gate_grad[:, lo:hi] = (hidden_grad * up_pre * sig * (1.0 + gate_pre * (1.0 - sig))).astype(BF)
+        up_grad[:, lo:hi] = (hidden_grad * silu).astype(BF)
+
+
+def experts_of(groups):
+    found, start = [], 0
+    for expert, count in groups:
+        if found and found[-1][0] == expert:
+            found[-1][2] = start + count
+        else:
+            found.append([expert, start, start + count])
+        start += count
+    return found
+
+
+def slice_kernel(groups, carried, *refs):
+    rows, pair_rows, grads, pair_grads, router_ref, pair_router_ref = refs[:6]
+    refs = refs[6:]
+    pieces, refs = refs[: 4 * len(groups)], refs[4 * len(groups) :]
+    if carried:
+        out_in, grad_in, refs = refs[0], refs[1], refs[2:]
+    out_sum, grad_sum, whole, x, y, hidden, gate_grad, up_grad, sems = refs
+    copies = load_units(groups, pieces, whole, sems)
+    join(x, rows, pair_rows)
+    join(y, grads, pair_grads)
+    weights = router_columns(router_ref, pair_router_ref)
+    for copy in copies:
+        copy.wait()
+    slice_grads(groups, whole, x, y, hidden, gate_grad, up_grad)
+    step = 512
+    for n in range(x.shape[1] // step):
+        at = slice(n * step, (n + 1) * step)
+        out_term = out_in[:, at] if carried else None
+        grad_term = grad_in[:, at] if carried else None
+        for expert, lo, hi in experts_of(groups):
+            w = weights[expert]
+            out_new = w * dot_t(hidden[:, lo:hi], whole[2, at, lo:hi])
+            grad_new = w * (
+                dot_t(gate_grad[:, lo:hi], whole[0, at, lo:hi]) + dot_t(up_grad[:, lo:hi], whole[1, at, lo:hi])
+            )
+            out_term = out_new if out_term is None else out_term + out_new
+            grad_term = grad_new if grad_term is None else grad_term + grad_new
+        out_sum[:, at] = out_term
+        grad_sum[:, at] = grad_term
+
+
+def last_out_kernel(groups, *refs):
+    rows, pair_rows, grads, pair_grads, router_ref, pair_router_ref = refs[:6]
+    refs = refs[6:]
+    pieces, refs = refs[: 4 * len(groups)], refs[4 * len(groups) :]
+    out_in, own_out, pair_out, gate_grad, up_grad, whole, x, y, hidden, sems = refs
+    copies = load_units(groups, pieces, whole, sems)
+    join(x, rows, pair_rows)
+    join(y, grads, pair_grads)
+    weights = router_columns(router_ref, pair_router_ref)
+    for copy in copies:
+        copy.wait()
+    slice_grads(groups, whole, x, y, hidden, gate_grad, up_grad)
+    tok, step = own_out.shape[0], 512
+    for n in range(x.shape[1] // step):
+        at = slice(n * step, (n + 1) * step)
+        total = out_in[:, at]
+        for expert, lo, hi in experts_of(groups):
+            total = total + weights[expert] * dot_t(hidden[:, lo:hi], whole[2, at, lo:hi])
+        own_out[:, at] = total[:tok]
+        pair_out[:, at] = total[tok:].astype(BF)
+
+
+def last_grad_kernel(groups, router_ref, pair_router_ref, *refs):
+    pieces, refs = refs[: 4 * len(groups)], refs[4 * len(groups) :]
+    gate_grad, up_grad, grad_in, own_grad, pair_grad, whole, sems = refs
+    copies = load_units(groups, pieces, whole, sems)
+    weights = router_columns(router_ref, pair_router_ref)
+    for copy in copies:
+        copy.wait()
+    tok, step = own_grad.shape[0], 512
+    for n in range(grad_in.shape[1] // step):
+        at = slice(n * step, (n + 1) * step)
+        total = grad_in[:, at]
+        for expert, lo, hi in experts_of(groups):
+            total = total + weights[expert] * (
+                dot_t(gate_grad[:, lo:hi], whole[0, at, lo:hi]) + dot_t(up_grad[:, lo:hi], whole[1, at, lo:hi])
+            )
+        own_grad[:, at] = total[:tok]
+        pair_grad[:, at] = total[tok:].astype(BF)
+
+
+def pair_layer_kernel(in_ref, att_ref, own_ref, back_ref, out_ref):
+    resid = in_ref[0].astype(F32) + att_ref[...].astype(F32)
+    out_ref[0] = (resid + own_ref[...] + back_ref[...].astype(F32)).astype(BF)
+
+
+def pair_grad_kernel(in_ref, att_ref, gain_ref, up_ref, own_ref, back_ref, out_ref):
+    width = in_ref.shape[2]
+    resid = in_ref[0].astype(F32) + att_ref[...].astype(F32)
+    gained = gain_ref[...] * (own_ref[...] + back_ref[...].astype(F32))
+    inv_rms = lax.rsqrt((resid * resid).sum(axis=1, keepdims=True) / width + 1e-06)
+    pull = inv_rms * inv_rms * inv_rms * ((resid * gained).sum(axis=1, keepdims=True) / width)
+    out_ref[0] = (up_ref[0].astype(F32) + inv_rms * gained - resid * pull).astype(BF)
+
+
+def pair_shards(
+    inputs, queries, keys, values, doc_ids, norm_gain, expert_ids, gate_weights, w_gate, w_up, w_down, out_grad
+):
+    tok, width = inputs.shape[1], inputs.shape[2]
+    half = w_gate.shape[2] // 2
+    unit = half // 3
+    shard = w_gate.shape[1]
+    gain = norm_gain.reshape(1, width)
+
+    def shape(*dims, kind=BF):
+        return jax.ShapeDtypeStruct(dims, kind)
+
+    def call(kernel, name, out_shape, in_specs, scratch=(), mib=32, aliases=None):
+        single = not isinstance(out_shape, list)
+        return pl.pallas_call(
+            kernel,
+            out_shape=out_shape,
+            in_specs=in_specs,
+            out_specs=VM if single else [VM] * len(out_shape),
+            scratch_shapes=list(scratch),
+            input_output_aliases=aliases or {},
+            compiler_params=params(mib),
+            name=name,
+        )
+
+    def over_x(block):
+        return swapped(block, "fsdp", 1)
+
+    def over_y(block):
+        return swapped(block, "groups", 1)
+
+    def over_core(block):
+        return swapped(block, "ctx", 1)
+
+    prev_keys = shifted(keys, ("expert", "ctx"), 1)
+    prev_values = shifted(values, ("expert", "ctx"), 1)
+
+    big, small = shape(3, shard, half), shape(3, shard, unit)
+    near, far, *laid = call(lay_kernel, "lay", [big, big] + [small] * 6 + [shape(tok, 128, kind=F32)], [VM] * 5)(
+        w_gate, w_up, w_down, expert_ids, gate_weights
+    )
+    near_units, far_units, router = laid[:3], laid[3:6], laid[6]
+    own_near_x = over_x(near)
+    z_units = [swapped(near_units[0], "expert", 2), swapped(near_units[1], "expert", 2)]
+    pair_router = swapped(router, "expert", 1)
+    pair_grads = swapped(out_grad, "expert", 1)
+    near_core, far_core = over_core(near), over_core(far)
+
+    attended, rows = call(
+        lambda *refs: normed_kernel(*refs), "attend", [shape(tok, width)] * 2, [VM] * 8
+    )(queries, keys, values, prev_keys, prev_values, doc_ids, inputs, gain)
+    pair_rows = swapped(rows, "expert", 1)
+
+    def both(block):
+        return [block, over_core(block)]
+
+    def spread_near(block):
+        return over_x(block), over_y(block)
+
+    zero = ready(z_units[0], rows)
+    z_units.append(swapped(ready(near_units[2], zero), "expert", 2))
+    x0, y0 = spread_near(zero)
+    own_near = [near, near_core] + both(ready(own_near_x, rows))
+    far_x = [over_x(ready(far_units[0], zero))]
+
+    scratch = lambda count: [
+        pltpu.VMEM((3, width, count), BF),
+        pltpu.VMEM((2 * tok, width), BF),
+        pltpu.VMEM((2 * tok, width), BF),
+    ]
+    acts = lambda count, number: [pltpu.VMEM((2 * tok, count), BF)] * number
+    sems = lambda groups: [pltpu.SemaphoreType.DMA((4 * len(groups),))]
+    sums = [shape(2 * tok, width, kind=F32)] * 2
+    token_args = [rows, pair_rows, out_grad, pair_grads, router, pair_router]
+
+    groups = ((0, half),)
+    out_sum, grad_sum = call(
+        lambda *refs: slice_kernel(((0, half),), False, *refs),
+        "slice_a",
+        sums,
+        [VM] * 6 + [ANY] * 4,
+        scratch(half) + acts(half, 3) + sems(groups),
+        48,
+    )(*token_args[:1], *token_args[1:], *own_near)
+
+    xy0 = over_y(ready(x0, out_sum))
+    unit_pieces = lambda z, x, y, xy: (both(z) + both(x), both(y) + both(xy))
+    one = ready(z_units[1], out_sum)
+    x1, y1 = spread_near(one)
+    far_x.append(over_x(ready(far_units[1], one)))
+    two = z_units[2]
+    xy1 = over_y(x1)
+    x2, y2 = spread_near(ready(two, one))
+    far_x.append(over_x(ready(far_units[2], two)))
+    near0, away0 = unit_pieces(zero, x0, y0, xy0)
+    near1, away1 = unit_pieces(one, x1, y1, xy1)
+
+    def home(i):
+        return [far_units[i], over_core(far_units[i])] + both(far_x[i])
+
+    mid_groups = ((1, unit),) * 4 + ((0, unit),) * 2
+    mid_pieces = near0 + away0 + near1 + away1 + home(0) + home(1)
+    count = 6 * unit
+    out_sum, grad_sum = call(
+        lambda *refs: slice_kernel(mid_groups, True, *refs),
+        "slice_b",
+        sums,
+        [VM] * 6 + [ANY] * 24 + [VM] * 2,
+        scratch(count) + acts(count, 3) + sems(mid_groups),
+        56,
+        {30: 0, 31: 1},
+    )(*token_args, *mid_pieces, out_sum, grad_sum)
+
+    xy2 = over_y(x2)
+    near2, away2 = unit_pieces(two, x2, y2, xy2)
+    last_groups = ((1, unit),) * 2 + ((0, unit),)
+    last_pieces = near2 + away2 + home(2)
+    count = 3 * unit
+    act = shape(2 * tok, count)
+    own_out, pair_out, gate_grad, up_grad = call(
+        lambda *refs: last_out_kernel(last_groups, *refs),
+        "slice_out",
+        [shape(tok, width, kind=F32), shape(tok, width), act, act],
+        [VM] * 6 + [ANY] * 12 + [VM],
+        scratch(count) + acts(count, 1) + sems(last_groups),
+        48,
+    )(*token_args, *last_pieces, out_sum)
+    back_out = swapped(pair_out, "expert", 1)
+    own_grad, pair_grad = call(
+        lambda *refs: last_grad_kernel(last_groups, *refs),
+        "slice_grad",
+        [shape(tok, width, kind=F32), shape(tok, width)],
+        [VM] * 2 + [ANY] * 12 + [VM] * 3,
+        scratch(count)[:1] + sems(last_groups),
+        48,
+    )(router, pair_router, *last_pieces, gate_grad, up_grad, grad_sum)
+    back_grad = swapped(pair_grad, "expert", 1)
+
+    block = jax.ShapeDtypeStruct(inputs.shape, BF)
+    layer_out = call(pair_layer_kernel, "layer", block, [VM] * 4)(inputs, attended, own_out, back_out)
+    input_grad = call(pair_grad_kernel, "grad", block, [VM] * 6)(
+        inputs, attended, gain, out_grad, own_grad, back_grad
+    )
+    return layer_out, input_grad
+
+
 def solution(mesh):
     rows = P(("groups", "fsdp"), ("expert", "ctx"), None)
     in_specs = (
@@ -360,4 +722,6 @@
         P("expert", None, ("fsdp", "ctx")),
         rows,
     )
+    paired = (mesh.shape["expert"], mesh.shape["fsdp"], mesh.shape["groups"], mesh.shape["ctx"]) == (4, 2, 2, 2)
+    shards = pair_shards if paired else slot_shards
     return jax.shard_map(shards, mesh=mesh, in_specs=in_specs, out_specs=(rows, rows), check_vma=False)

time: 194 us -> 209 us (1.077)
  starting transfers between devices: 23.2 us -> 54 us
  waiting for transfers between devices: 131 us -> 102 us
  Pallas kernels: 27.4 us -> 42.7 us
  local copies, waits for them, and re-layouts: 11.4 us -> 7.06 us
    ppermute x21 -> x41, waiting for transfers between devices: 123 us -> 88.5 us  [swapped(): return lax.ppermute(block, axis, [(i, i ^ distance) for i in range(count)])]
    ppermute x21 -> x41, starting transfers between devices: 17.7 us -> 48.5 us  [swapped(): return lax.ppermute(block, axis, [(i, i ^ distance) for i in range(count)])]
    pallas_call x6 -> x8, Pallas kernels: 27.4 us -> 42.7 us  [the longest x1 13.9 us: pair_shards(): call(lambda *refs: slice_kernel(mid_groups, True, *refs), 'slice_b', sums...]
    ppermute x2, waiting for transfers between devices: 8.09 us -> 13.5 us  [shifted(): return lax.ppermute(block, axis, route)]
    unnamed x42 -> x92, local copies, waits for them, and re-layouts: 11.4 us -> 7.06 us
  transfers between devices with their start and end apart: 23 -> 43, of which waited for: 13 -> 15; matrix products, arithmetic and copies ran while one was open for 0% -> 0% of each run, Pallas kernels for 13% -> 14%
where the time goes in v2:
time: 209 us; the launch traced here: 207 us
  waiting for transfers between devices  102 us (49%)
  starting transfers between devices  54 us (26%)
  Pallas kernels  42.7 us (20%)
  local copies, waits for them, and re-layouts  7.06 us (3%)
    ppermute x41, waiting for transfers between devices, swapped(): return lax.ppermute(block, axis, [(i, i ^ distance) for i in range(count)])  88.5 us
    ppermute x41, starting transfers between devices, swapped(): return lax.ppermute(block, axis, [(i, i ^ distance) for i in range(count)])  48.5 us
    pallas_call x1, Pallas kernels, pair_shards(): call(lambda *refs: slice_kernel(mid_groups, True, *refs), 'slice_b', sums...  13.9 us
    ppermute x2, waiting for transfers between devices, shifted(): return lax.ppermute(block, axis, route)  13.5 us
    unnamed x92, local copies, waits for them, and re-layouts  7.06 us
    pallas_call x1, Pallas kernels, pair_shards(): call(lambda *refs: slice_kernel(((0, half),), False, *refs), 'slice_a', s...  6.96 us
    pallas_call x1, Pallas kernels, pair_shards(): call(lambda *refs: last_out_kernel(last_groups, *refs), 'slice_out', [sha...  6.9 us
    pallas_call x1, Pallas kernels, pair_shards(): call(lambda *refs: normed_kernel(*refs), 'attend', [shape(tok, width)] *...  5.85 us
  transfers between devices with their start and end apart: 43, of which 15 were waited for; matrix products, arithmetic and copies ran while one was open for 0% of the time, Pallas kernels for 14%

profile of v2, /device:TPU:10, one launch (start us, length us, event | category | flops | bytes accessed | tf_op | source)
XLA Modules:
  0.0 206.7 jit_solution(86303206057508851)
XLA Ops:
  7.8 1.9 collective-permute-start
  9.7 3.6 %collective-permute-start.1 = (bf16[1,128,2048]{2,1,0:T(8,128)(2,1)S(1)}, bf16[1,128,2048]{2,1,0:T(8,128)(2,1)S(1)}, u32[]{:S(2)}, u32[]{:S(2)}) collective-permute-start(bf16[1,128,2048]{2,1,0:T(8,128)(2,1)S(1)} %copy-done.17), channel_id=1, source_target_pairs={{0,1},{1,4},{4,5},{5,8},{8,9},{9,12},{12,13},{2,3},{3,6},{6,7},{7,... | collective-permute-start | bytes 1572872 | tf_op jit(solution)/shard_map/ppermute | solution.py:29
  14.3 2.0 collective-permute-start.8
  16.3 2.2 %collective-permute-done.refs_3_ = bf16[1,128,2048]{2,1,0:T(8,128)(2,1)S(1)} collective-permute-done((bf16[1,128,2048]{2,1,0:T(8,128)(2,1)S(1)}, bf16[1,128,2048]{2,1,0:T(8,128)(2,1)S(1)}, u32[]{:S(2)}, u32[]{:S(2)}) %collective-permute-start) | collective-permute-done | bytes 524320 | tf_op jit(solution)/shard_map/ppermute | solution.py:29
  18.5 11.2 %collective-permute-done.1.refs_4_ = bf16[1,128,2048]{2,1,0:T(8,128)(2,1)S(1)} collective-permute-done((bf16[1,128,2048]{2,1,0:T(8,128)(2,1)S(1)}, bf16[1,128,2048]{2,1,0:T(8,128)(2,1)S(1)}, u32[]{:S(2)}, u32[]{:S(2)}) %collective-permute-start.1) | collective-permute-done | bytes 524320 | tf_op jit(solution)/shard_map/ppermute | solution.py:29
  29.8 17.7 %collective-permute-start.35 = (bf16[3,512,128]{2,1,0:T(8,128)(2,1)S(1)}, bf16[3,512,128]{2,1,0:T(8,128)(2,1)S(1)}, u32[]{:S(2)}, u32[]{:S(2)}) collective-permute-start(bf16[3,512,128]{2,1,0:T(8,128)(2,1)S(1)} %get-tuple-element.48.refs_22_), channel_id=1, source_target_pairs={{0,1},{1,0},{2,3},{3,2},{4,5},{5,4},{6,7},{7,6},{8,9},{9,8},{10,11... | collective-permute-start | bytes 1179656 | tf_op jit(solution)/shard_map/ppermute | solution.py:23
  47.5 5.9 %attend.1 = (bf16[128,2048]{1,0:T(8,128)(2,1)S(1)}, bf16[128,2048]{1,0:T(8,128)(2,1)S(1)}) custom-call(bf16[1,128,2048]{2,1,0:T(8,128)(2,1)S(1)} %copy-done.15, bf16[1,128,2048]{2,1,0:T(8,128)(2,1)S(1)} %copy-done.16, bf16[1,128,2048]{2,1,0:T(8,128)(2,1)S(1)} %copy-done.17, bf16[1,128,2048]{2,1,0:T(8,128)(2,1)S(1)} %collective-permute-done.refs_3_, ...), custom_call_target="tpu_custom_call" | custom-call | tf_op jit(solution)/shard_map/attend/pallas_call | solution.py:611
  56.3 10.9 %collective-permute-done.3.refs_3_ = bf16[1,128,2048]{2,1,0:T(8,128)(2,1)S(1)} collective-permute-done((bf16[1,128,2048]{2,1,0:T(8,128)(2,1)S(1)}, bf16[1,128,2048]{2,1,0:T(8,128)(2,1)S(1)}, u32[]{:S(2)}, u32[]{:S(2)}) %collective-permute-start.3) | collective-permute-done | bytes 524320 | tf_op jit(solution)/shard_map/ppermute | solution.py:23
  68.8 4.1 %collective-permute-done.36.refs_24_ = bf16[3,512,128]{2,1,0:T(8,128)(2,1)S(1)} collective-permute-done((bf16[3,512,128]{2,1,0:T(8,128)(2,1)S(1)}, bf16[3,512,128]{2,1,0:T(8,128)(2,1)S(1)}, u32[]{:S(2)}, u32[]{:S(2)}) %collective-permute-start.36) | collective-permute-done | bytes 393248 | tf_op jit(solution)/shard_map/ppermute | solution.py:23
  72.9 5.3 %collective-permute-start.6 = (bf16[3,512,128]{2,1,0:T(8,128)(2,1)S(1)}, bf16[3,512,128]{2,1,0:T(8,128)(2,1)S(1)}, u32[]{:S(2)}, u32[]{:S(2)}) collective-permute-start(bf16[3,512,128]{2,1,0:T(8,128)(2,1)S(1)} %get-tuple-element.37), channel_id=1, source_target_pairs={{0,8},{4,12},{8,0},{12,4},{1,9},{5,13},{9,1},{13,5},{2,10},{6,14},... | collective-permute-start | bytes 1179656 | tf_op jit(solution)/shard_map/ppermute | solution.py:23
  79.4 16.5 %collective-permute-done.6.refs_6_.refs_2_ = bf16[3,512,128]{2,1,0:T(8,128)(2,1)S(1)} collective-permute-done((bf16[3,512,128]{2,1,0:T(8,128)(2,1)S(1)}, bf16[3,512,128]{2,1,0:T(8,128)(2,1)S(1)}, u32[]{:S(2)}, u32[]{:S(2)}) %collective-permute-start.6) | collective-permute-done | bytes 393248 | tf_op jit(solution)/shard_map/ppermute | solution.py:23
  97.6 7.0 %slice_a.1 = (f32[256,2048]{1,0:T(8,128)}, f32[256,2048]{1,0:T(8,128)}) custom-call(bf16[128,2048]{1,0:T(8,128)(2,1)S(1)} %get-tuple-element.32.refs_0_, bf16[128,2048]{1,0:T(8,128)(2,1)S(1)} %collective-permute-done.2.refs_1_, bf16[1,128,2048]{2,1,0:T(8,128)(2,1)S(1)} %copy-done, bf16[1,128,2048]{2,1,0:T(8,128)(2,1)S(1)} %collective-permute-done.3.refs_3_, ...), custom_call_target="tpu_custom_call" | custom-call | tf_op jit(solution)/shard_map/slice_a/pallas_call | solution.py:639
  110.3 6.3 %collective-permute-done.19.refs_16_.refs_12_ = bf16[3,512,128]{2,1,0:T(8,128)(2,1)S(1)} collective-permute-done((bf16[3,512,128]{2,1,0:T(8,128)(2,1)S(1)}, bf16[3,512,128]{2,1,0:T(8,128)(2,1)S(1)}, u32[]{:S(2)}, u32[]{:S(2)}) %collective-permute-start.19) | collective-permute-done | bytes 393248 | tf_op jit(solution)/shard_map/ppermute | solution.py:23
  118.7 6.3 %collective-permute-done.39.refs_28_ = bf16[3,512,128]{2,1,0:T(8,128)(2,1)S(1)} collective-permute-done((bf16[3,512,128]{2,1,0:T(8,128)(2,1)S(1)}, bf16[3,512,128]{2,1,0:T(8,128)(2,1)S(1)}, u32[]{:S(2)}, u32[]{:S(2)}) %collective-permute-start.39) | collective-permute-done | bytes 393248 | tf_op jit(solution)/shard_map/ppermute | solution.py:23
  126.5 6.9 %collective-permute-done.29.refs_16_ = bf16[3,512,128]{2,1,0:T(8,128)(2,1)S(1)} collective-permute-done((bf16[3,512,128]{2,1,0:T(8,128)(2,1)S(1)}, bf16[3,512,128]{2,1,0:T(8,128)(2,1)S(1)}, u32[]{:S(2)}, u32[]{:S(2)}) %collective-permute-start.29) | collective-permute-done | bytes 393248 | tf_op jit(solution)/shard_map/ppermute | solution.py:23
  135.2 6.2 %collective-permute-done.12.refs_8_.refs_4_ = bf16[3,512,128]{2,1,0:T(8,128)(2,1)S(1)} collective-permute-done((bf16[3,512,128]{2,1,0:T(8,128)(2,1)S(1)}, bf16[3,512,128]{2,1,0:T(8,128)(2,1)S(1)}, u32[]{:S(2)}, u32[]{:S(2)}) %collective-permute-start.12) | collective-permute-done | bytes 393248 | tf_op jit(solution)/shard_map/ppermute | solution.py:23
  143.5 1.8 collective-permute-done.33.refs_20_
  146.5 6.9 %collective-permute-done.16.refs_12_.refs_8_ = bf16[3,512,128]{2,1,0:T(8,128)(2,1)S(1)} collective-permute-done((bf16[3,512,128]{2,1,0:T(8,128)(2,1)S(1)}, bf16[3,512,128]{2,1,0:T(8,128)(2,1)S(1)}, u32[]{:S(2)}, u32[]{:S(2)}) %collective-permute-start.16) | collective-permute-done | bytes 393248 | tf_op jit(solution)/shard_map/ppermute | solution.py:23
  154.2 13.9 %slice_b.1 = (f32[256,2048]{1,0:T(8,128)}, f32[256,2048]{1,0:T(8,128)}) custom-call(bf16[128,2048]{1,0:T(8,128)(2,1)} %copy-done.3, bf16[128,2048]{1,0:T(8,128)(2,1)} %copy-done.5, bf16[1,128,2048]{2,1,0:T(8,128)(2,1)} %up_ref.1, bf16[1,128,2048]{2,1,0:T(8,128)(2,1)} %copy-done.4, ...), custom_call_target="tpu_custom_call", output_to_operand_aliasing={{0}: (30, {}), {1}: (31, {})} | custom-call | tf_op jit(solution)/shard_map/slice_b/pallas_call | solution.py:666
  168.2 6.9 %slice_out.1 = (f32[128,2048]{1,0:T(8,128)}, bf16[128,2048]{1,0:T(8,128)(2,1)S(1)}, bf16[256,384]{1,0:T(8,128)(2,1)S(1)}, bf16[256,384]{1,0:T(8,128)(2,1)S(1)}) custom-call(bf16[128,2048]{1,0:T(8,128)(2,1)} %copy-done.3, bf16[128,2048]{1,0:T(8,128)(2,1)} %copy-done.5, bf16[1,128,2048]{2,1,0:T(8,128)(2,1)} %up_ref.1, bf16[1,128,2048]{2,1,0:T(8,128)(2,1)} %copy-done.4, ...), custom_call_target="tpu_custom_call" | custom-call | tf_op jit(solution)/shard_map/slice_out/pallas_call | solution.py:682
  175.1 4.9 %slice_grad.1 = (f32[128,2048]{1,0:T(8,128)}, bf16[128,2048]{1,0:T(8,128)(2,1)S(1)}) custom-call(f32[128,128]{1,0:T(8,128)S(1)} %copy-done.7, f32[128,128]{1,0:T(8,128)S(1)} %copy-done.9, bf16[3,512,128]{2,1,0:T(8,128)(2,1)S(1)} %collective-permute-done.6.refs_6_.refs_2_, bf16[3,512,128]{2,1,0:T(8,128)(2,1)S(1)} %collective-permute-done.7.refs_7_.refs_3_, ...), custom_call_target="tpu_custom_call" | custom-call | tf_op jit(solution)/shard_map/slice_grad/pallas_call | solution.py:691
  180.4 1.7 collective-permute-start.41
  182.1 12.7 %collective-permute-done.42.back_ref = bf16[128,2048]{1,0:T(8,128)(2,1)S(1)} collective-permute-done((bf16[128,2048]{1,0:T(8,128)(2,1)S(1)}, bf16[128,2048]{1,0:T(8,128)(2,1)S(1)}, u32[]{:S(2)}, u32[]{:S(2)}) %collective-permute-start.42) | collective-permute-done | bytes 524320 | tf_op jit(solution)/shard_map/ppermute | solution.py:23
  197.6 8.1 %collective-permute-done.41.back_ref = bf16[128,2048]{1,0:T(8,128)(2,1)S(1)} collective-permute-done((bf16[128,2048]{1,0:T(8,128)(2,1)S(1)}, bf16[128,2048]{1,0:T(8,128)(2,1)S(1)}, u32[]{:S(2)}, u32[]{:S(2)}) %collective-permute-start.41) | collective-permute-done | bytes 524320 | tf_op jit(solution)/shard_map/ppermute | solution.py:23
  (162 shorter events, 34.7 us)
Async XLA Ops:
  7.2 40.3 %collective-permute-start.10 = (bf16[3,512,384]{2,1,0:T(8,128)(2,1)S(1)}, bf16[3,512,384]{2,1,0:T(8,128)(2,1)S(1)}, u32[]{:S(2)}, u32[]{:S(2)}) collective-permute-start(bf16[3,512,384]{2,1,0:T(8,128)(2,1)S(1)} %get-tuple-element.39.refs_6_), channel_id=1, source_target_pairs={{0,2},{2,0},{1,3},{3,1},{4,6},{6,4},{5,7},{7,5},{8,10},{10,8},{9,1... | collective-permute-start | bytes 3538952 | tf_op jit(solution)/shard_map/ppermute | solution.py:23
  9.7 20.1 %collective-permute-start.1 = (bf16[1,128,2048]{2,1,0:T(8,128)(2,1)S(1)}, bf16[1,128,2048]{2,1,0:T(8,128)(2,1)S(1)}, u32[]{:S(2)}, u32[]{:S(2)}) collective-permute-start(bf16[1,128,2048]{2,1,0:T(8,128)(2,1)S(1)} %copy-done.17), channel_id=1, source_target_pairs={{0,1},{1,4},{4,5},{5,8},{8,9},{9,12},{12,13},{2,3},{3,6},{6,7},{7,... | collective-permute-start | bytes 1572872 | tf_op jit(solution)/shard_map/ppermute | solution.py:29
  13.3 40.7 %collective-permute-start.5 = (bf16[3,512,128]{2,1,0:T(8,128)(2,1)S(1)}, bf16[3,512,128]{2,1,0:T(8,128)(2,1)S(1)}, u32[]{:S(2)}, u32[]{:S(2)}) collective-permute-start(bf16[3,512,128]{2,1,0:T(8,128)(2,1)S(1)} %get-tuple-element.35), channel_id=1, source_target_pairs={{0,8},{4,12},{8,0},{12,4},{1,9},{5,13},{9,1},{13,5},{2,10},{6,14},... | collective-permute-start | bytes 1179656 | tf_op jit(solution)/shard_map/ppermute | solution.py:23
  14.3 39.8 %collective-permute-start.8 = (bf16[3,512,128]{2,1,0:T(8,128)(2,1)S(1)}, bf16[3,512,128]{2,1,0:T(8,128)(2,1)S(1)}, u32[]{:S(2)}, u32[]{:S(2)}) collective-permute-start(bf16[3,512,128]{2,1,0:T(8,128)(2,1)S(1)} %get-tuple-element.38), channel_id=1, source_target_pairs={{0,8},{4,12},{8,0},{12,4},{1,9},{5,13},{9,1},{13,5},{2,10},{6,14},... | collective-permute-start | bytes 1179656 | tf_op jit(solution)/shard_map/ppermute | solution.py:23
  18.5 34.9 %collective-permute-start.4 = (f32[128,128]{1,0:T(8,128)S(1)}, f32[128,128]{1,0:T(8,128)S(1)}, u32[]{:S(2)}, u32[]{:S(2)}) collective-permute-start(f32[128,128]{1,0:T(8,128)S(1)} %get-tuple-element.33.refs_4_.refs_0_), channel_id=1, source_target_pairs={{0,4},{4,0},{8,12},{12,8},{1,5},{5,1},{9,13},{13,9},{2,6},{6,2},{1... | collective-permute-start | bytes 196616 | tf_op jit(solution)/shard_map/ppermute | solution.py:23
  29.8 24.4 %collective-permute-start.35 = (bf16[3,512,128]{2,1,0:T(8,128)(2,1)S(1)}, bf16[3,512,128]{2,1,0:T(8,128)(2,1)S(1)}, u32[]{:S(2)}, u32[]{:S(2)}) collective-permute-start(bf16[3,512,128]{2,1,0:T(8,128)(2,1)S(1)} %get-tuple-element.48.refs_22_), channel_id=1, source_target_pairs={{0,1},{1,0},{2,3},{3,2},{4,5},{5,4},{6,7},{7,6},{8,9},{9,8},{10,11... | collective-permute-start | bytes 1179656 | tf_op jit(solution)/shard_map/ppermute | solution.py:23
  53.4 43.0 %collective-permute-start.9 = (bf16[3,512,384]{2,1,0:T(8,128)(2,1)S(1)}, bf16[3,512,384]{2,1,0:T(8,128)(2,1)S(1)}, u32[]{:S(2)}, u32[]{:S(2)}) collective-permute-start(bf16[3,512,384]{2,1,0:T(8,128)(2,1)S(1)} %get-tuple-element.39.refs_6_), channel_id=1, source_target_pairs={{0,1},{1,0},{2,3},{3,2},{4,5},{5,4},{6,7},{7,6},{8,9},{9,8},{10,11... | collective-permute-start | bytes 3538952 | tf_op jit(solution)/shard_map/ppermute | solution.py:23
  54.0 42.6 %collective-permute-start.11 = (bf16[3,512,384]{2,1,0:T(8,128)(2,1)S(1)}, bf16[3,512,384]{2,1,0:T(8,128)(2,1)S(1)}, u32[]{:S(2)}, u32[]{:S(2)}) collective-permute-start(bf16[3,512,384]{2,1,0:T(8,128)(2,1)S(1)} %collective-permute-done.10.refs_8_), channel_id=1, source_target_pairs={{0,1},{1,0},{2,3},{3,2},{4,5},{5,4},{6,7},{7,6},{8,9},{9,8},{10,11... | collective-permute-start | bytes 3538952 | tf_op jit(solution)/shard_map/ppermute | solution.py:23
  55.7 17.2 %collective-permute-start.36 = (bf16[3,512,128]{2,1,0:T(8,128)(2,1)S(1)}, bf16[3,512,128]{2,1,0:T(8,128)(2,1)S(1)}, u32[]{:S(2)}, u32[]{:S(2)}) collective-permute-start(bf16[3,512,128]{2,1,0:T(8,128)(2,1)S(1)} %get-tuple-element.48.refs_22_), channel_id=1, source_target_pairs={{0,2},{2,0},{1,3},{3,1},{4,6},{6,4},{5,7},{7,5},{8,10},{10,8},{9,1... | collective-permute-start | bytes 1179656 | tf_op jit(solution)/shard_map/ppermute | solution.py:23
  67.2 28.7 %collective-permute-start.2 = (bf16[128,2048]{1,0:T(8,128)(2,1)S(1)}, bf16[128,2048]{1,0:T(8,128)(2,1)S(1)}, u32[]{:S(2)}, u32[]{:S(2)}) collective-permute-start(bf16[128,2048]{1,0:T(8,128)(2,1)S(1)} %get-tuple-element.32.refs_0_), channel_id=1, source_target_pairs={{0,4},{4,0},{8,12},{12,8},{1,5},{5,1},{9,13},{13,9},{2,6},{6,2},{1... | collective-permute-start | bytes 1572872 | tf_op jit(solution)/shard_map/ppermute | solution.py:23
  72.9 23.0 %collective-permute-start.6 = (bf16[3,512,128]{2,1,0:T(8,128)(2,1)S(1)}, bf16[3,512,128]{2,1,0:T(8,128)(2,1)S(1)}, u32[]{:S(2)}, u32[]{:S(2)}) collective-permute-start(bf16[3,512,128]{2,1,0:T(8,128)(2,1)S(1)} %get-tuple-element.37), channel_id=1, source_target_pairs={{0,8},{4,12},{8,0},{12,4},{1,9},{5,13},{9,1},{13,5},{2,10},{6,14},... | collective-permute-start | bytes 1179656 | tf_op jit(solution)/shard_map/ppermute | solution.py:23
  78.4 26.2 %collective-permute-start.18 = (bf16[3,512,128]{2,1,0:T(8,128)(2,1)S(1)}, bf16[3,512,128]{2,1,0:T(8,128)(2,1)S(1)}, u32[]{:S(2)}, u32[]{:S(2)}) collective-permute-start(bf16[3,512,128]{2,1,0:T(8,128)(2,1)S(1)} %get-tuple-element.45.refs_14_.refs_10_), channel_id=1, source_target_pairs={{0,1},{1,0},{2,3},{3,2},{4,5},{5,4},{6,7},{7,6},{8,9},{9,8},{10,11... | collective-permute-start | bytes 1179656 | tf_op jit(solution)/shard_map/ppermute | solution.py:23
  107.7 17.3 %collective-permute-start.39 = (bf16[3,512,128]{2,1,0:T(8,128)(2,1)S(1)}, bf16[3,512,128]{2,1,0:T(8,128)(2,1)S(1)}, u32[]{:S(2)}, u32[]{:S(2)}) collective-permute-start(bf16[3,512,128]{2,1,0:T(8,128)(2,1)S(1)} %get-tuple-element.50.refs_26_), channel_id=1, source_target_pairs={{0,2},{2,0},{1,3},{3,1},{4,6},{6,4},{5,7},{7,5},{8,10},{10,8},{9,1... | collective-permute-start | bytes 1179656 | tf_op jit(solution)/shard_map/ppermute | solution.py:23
  108.3 25.1 %collective-permute-start.29 = (bf16[3,512,128]{2,1,0:T(8,128)(2,1)S(1)}, bf16[3,512,128]{2,1,0:T(8,128)(2,1)S(1)}, u32[]{:S(2)}, u32[]{:S(2)}) collective-permute-start(bf16[3,512,128]{2,1,0:T(8,128)(2,1)S(1)} %collective-permute-done.8.refs_14_), channel_id=1, source_target_pairs={{0,2},{2,0},{1,3},{3,1},{4,6},{6,4},{5,7},{7,5},{8,10},{10,8},{9,1... | collective-permute-start | bytes 1179656 | tf_op jit(solution)/shard_map/ppermute | solution.py:23
  109.8 23.7 %collective-permute-start.31 = (bf16[3,512,128]{2,1,0:T(8,128)(2,1)S(1)}, bf16[3,512,128]{2,1,0:T(8,128)(2,1)S(1)}, u32[]{:S(2)}, u32[]{:S(2)}) collective-permute-start(bf16[3,512,128]{2,1,0:T(8,128)(2,1)S(1)} %collective-permute-done.8.refs_14_), channel_id=1, source_target_pairs={{0,16},{16,0},{1,17},{17,1},{2,18},{18,2},{3,19},{19,3},{4,20},{20... | collective-permute-start | bytes 1179656 | tf_op jit(solution)/shard_map/ppermute | solution.py:23
  116.6 18.5 %collective-permute-start.28 = (bf16[3,512,128]{2,1,0:T(8,128)(2,1)S(1)}, bf16[3,512,128]{2,1,0:T(8,128)(2,1)S(1)}, u32[]{:S(2)}, u32[]{:S(2)}) collective-permute-start(bf16[3,512,128]{2,1,0:T(8,128)(2,1)S(1)} %collective-permute-done.8.refs_14_), channel_id=1, source_target_pairs={{0,1},{1,0},{2,3},{3,2},{4,5},{5,4},{6,7},{7,6},{8,9},{9,8},{10,11... | collective-permute-start | bytes 1179656 | tf_op jit(solution)/shard_map/ppermute | solution.py:23
  118.1 23.3 %collective-permute-start.12 = (bf16[3,512,128]{2,1,0:T(8,128)(2,1)S(1)}, bf16[3,512,128]{2,1,0:T(8,128)(2,1)S(1)}, u32[]{:S(2)}, u32[]{:S(2)}) collective-permute-start(bf16[3,512,128]{2,1,0:T(8,128)(2,1)S(1)} %collective-permute-done.6.refs_6_.refs_2_), channel_id=1, source_target_pairs={{0,2},{2,0},{1,3},{3,1},{4,6},{6,4},{5,7},{7,5},{8,10},{10,8},{9,1... | collective-permute-start | bytes 1179656 | tf_op jit(solution)/shard_map/ppermute | solution.py:23
  125.0 16.4 %collective-permute-start.14 = (bf16[3,512,128]{2,1,0:T(8,128)(2,1)S(1)}, bf16[3,512,128]{2,1,0:T(8,128)(2,1)S(1)}, u32[]{:S(2)}, u32[]{:S(2)}) collective-permute-start(bf16[3,512,128]{2,1,0:T(8,128)(2,1)S(1)} %collective-permute-done.6.refs_6_.refs_2_), channel_id=1, source_target_pairs={{0,16},{16,0},{1,17},{17,1},{2,18},{18,2},{3,19},{19,3},{4,20},{20... | collective-permute-start | bytes 1179656 | tf_op jit(solution)/shard_map/ppermute | solution.py:23
  145.3 22.8 %collective-permute-start.7 = (bf16[3,512,128]{2,1,0:T(8,128)(2,1)S(1)}, bf16[3,512,128]{2,1,0:T(8,128)(2,1)S(1)}, u32[]{:S(2)}, u32[]{:S(2)}) collective-permute-start(bf16[3,512,128]{2,1,0:T(8,128)(2,1)S(1)} %collective-permute-done.6.refs_6_.refs_2_), channel_id=1, source_target_pairs={{0,1},{1,0},{2,3},{3,2},{4,5},{5,4},{6,7},{7,6},{8,9},{9,8},{10,11... | collective-permute-start | bytes 1179656 | tf_op jit(solution)/shard_map/ppermute | solution.py:23
  145.9 22.2 %collective-permute-start.20 = (bf16[3,512,128]{2,1,0:T(8,128)(2,1)S(1)}, bf16[3,512,128]{2,1,0:T(8,128)(2,1)S(1)}, u32[]{:S(2)}, u32[]{:S(2)}) collective-permute-start(bf16[3,512,128]{2,1,0:T(8,128)(2,1)S(1)} %collective-permute-done.19.refs_16_.refs_12_), channel_id=1, source_target_pairs={{0,1},{1,0},{2,3},{3,2},{4,5},{5,4},{6,7},{7,6},{8,9},{9,8},{10,11... | collective-permute-start | bytes 1179656 | tf_op jit(solution)/shard_map/ppermute | solution.py:23
  146.0 22.1 %collective-permute-start.13 = (bf16[3,512,128]{2,1,0:T(8,128)(2,1)S(1)}, bf16[3,512,128]{2,1,0:T(8,128)(2,1)S(1)}, u32[]{:S(2)}, u32[]{:S(2)}) collective-permute-start(bf16[3,512,128]{2,1,0:T(8,128)(2,1)S(1)} %collective-permute-done.12.refs_8_.refs_4_), channel_id=1, source_target_pairs={{0,1},{1,0},{2,3},{3,2},{4,5},{5,4},{6,7},{7,6},{8,9},{9,8},{10,11... | collective-permute-start | bytes 1179656 | tf_op jit(solution)/shard_map/ppermute | solution.py:23
  153.4 14.7 %collective-permute-start.15 = (bf16[3,512,128]{2,1,0:T(8,128)(2,1)S(1)}, bf16[3,512,128]{2,1,0:T(8,128)(2,1)S(1)}, u32[]{:S(2)}, u32[]{:S(2)}) collective-permute-start(bf16[3,512,128]{2,1,0:T(8,128)(2,1)S(1)} %collective-permute-done.14.refs_10_.refs_6_), channel_id=1, source_target_pairs={{0,1},{1,0},{2,3},{3,2},{4,5},{5,4},{6,7},{7,6},{8,9},{9,8},{10,11... | collective-permute-start | bytes 1179656 | tf_op jit(solution)/shard_map/ppermute | solution.py:23
  180.0 14.8 %collective-permute-start.42 = (bf16[128,2048]{1,0:T(8,128)(2,1)S(1)}, bf16[128,2048]{1,0:T(8,128)(2,1)S(1)}, u32[]{:S(2)}, u32[]{:S(2)}) collective-permute-start(bf16[128,2048]{1,0:T(8,128)(2,1)S(1)} %get-tuple-element.59), channel_id=1, source_target_pairs={{0,4},{4,0},{8,12},{12,8},{1,5},{5,1},{9,13},{13,9},{2,6},{6,2},{1... | collective-permute-start | bytes 1572872 | tf_op jit(solution)/shard_map/ppermute | solution.py:23
  180.4 25.2 %collective-permute-start.41 = (bf16[128,2048]{1,0:T(8,128)(2,1)S(1)}, bf16[128,2048]{1,0:T(8,128)(2,1)S(1)}, u32[]{:S(2)}, u32[]{:S(2)}) collective-permute-start(bf16[128,2048]{1,0:T(8,128)(2,1)S(1)} %get-tuple-element.54), channel_id=1, source_target_pairs={{0,4},{4,0},{8,12},{12,8},{1,5},{5,1},{9,13},{13,9},{2,6},{6,2},{1... | collective-permute-start | bytes 1572872 | tf_op jit(solution)/shard_map/ppermute | solution.py:23
  (64 other events, 1708.9 us)

commit v3 on v1

--- a/solution.py
+++ b/solution.py
@@ -29,6 +29,10 @@
     return lax.ppermute(block, axis, route)
 
 
+def after(block, *others):
+    return lax.optimization_barrier((block, *others))[0]
+
+
 def dot(a, b):
     return jnp.dot(a, b, preferred_element_type=F32)
 
@@ -37,12 +41,17 @@
     return lax.dot_general(a, b, (((1,), (1,)), ((), ())), preferred_element_type=F32)
 
 
+def column(row):
+    tok = row.shape[1]
+    return jnp.broadcast_to(row, (tok, tok)).T[:, 0:1]
+
+
 def routing(ids_ref, here):
-    tok = ids_ref.shape[1]
+    tok = ids_ref.shape[2]
     lane = lax.broadcasted_iota(jnp.int32, (tok, 128), 1)
     row = lax.broadcasted_iota(jnp.int32, (tok, tok), 0)
     col = lax.broadcasted_iota(jnp.int32, (tok, tok), 1)
-    first, second = ids_ref[0, :, 0:1] ^ here, ids_ref[0, :, 1:2] ^ here
+    first, second = column(ids_ref[0, 0:1]) ^ here, column(ids_ref[0, 1:2]) ^ here
     chosen = (first == lane) | (second == lane)
     before = (col < row).astype(BF)
     rank = dot(before, chosen.astype(BF))
@@ -64,10 +73,23 @@
         out[...] = packed[k * slots : (k + 1) * slots]
 
 
-def pack_kernel(slots, ids_ref, rows_ref, *out_refs):
-    here = lax.axis_index("expert")
-    _, _, slot = routing(ids_ref, here)
-    pack(rows_ref[0], slot, slots, out_refs)
+def prepare_kernel(slots, ids_ref, rows_hbm, g_hbm, u_hbm, d_hbm, weight_ref, *refs):
+    out_refs, (rows, down, sems) = refs[:-3], refs[-3:]
+    copies = [
+        pltpu.make_async_copy(rows_hbm.at[0], rows, sems.at[0]),
+        pltpu.make_async_copy(d_hbm.at[0], down, sems.at[1]),
+        pltpu.make_async_copy(g_hbm.at[0], weight_ref.at[0], sems.at[2]),
+        pltpu.make_async_copy(u_hbm.at[0], weight_ref.at[1], sems.at[3]),
+    ]
+    for copy in copies:
+        copy.start()
+    _, _, slot = routing(ids_ref, lax.axis_index("expert"))
+    copies[0].wait()
+    pack(rows[...], slot, slots, out_refs)
+    copies[1].wait()
+    weight_ref[2] = down[...].T
+    copies[2].wait()
+    copies[3].wait()
 
 
 def attend_kernel(
@@ -110,85 +132,69 @@
     pack(normed, slot, slots, out_refs)
 
 
-def load_pieces(piece_refs, whole_ref, sems, axis):
+def load_pieces(piece_refs, whole_ref, sems):
     mine = lax.axis_index("fsdp") * lax.axis_size("ctx") + lax.axis_index("ctx")
-    size = piece_refs[0].shape[1 + axis]
+    size = piece_refs[0].shape[1]
     copies = []
     for j, piece in enumerate(piece_refs):
         at = pl.ds(pl.multiple_of((mine ^ j) * size, size), size)
-        target = whole_ref.at[at, :] if axis == 0 else whole_ref.at[:, at]
-        copies.append(pltpu.make_async_copy(piece.at[0], target, sems.at[j]))
+        copies.append(pltpu.make_async_copy(piece, whole_ref.at[:, at], sems.at[j]))
     for copy in copies:
         copy.start()
     return copies
 
 
-def wait_all(copies):
-    for copy in copies:
-        copy.wait()
-
-
 def forward_kernel(peers, pieces, *refs):
     rows, refs = refs[:peers], refs[peers:]
-    gates, refs = refs[:pieces], refs[pieces:]
-    ups, refs = refs[:pieces], refs[pieces:]
-    downs, refs = refs[:pieces], refs[pieces:]
+    weights, refs = refs[:pieces], refs[pieces:]
     outs, refs = refs[:peers], refs[peers:]
-    slope_ref, silu_ref, gate, up, down, x, hidden, sems = refs
-    copies_g = load_pieces(gates, gate, sems.at[0], 0)
-    copies_u = load_pieces(ups, up, sems.at[1], 0)
-    copies_d = load_pieces(downs, down, sems.at[2], 1)
+    slope_ref, silu_ref, whole, x, hidden, sems = refs
+    copies = load_pieces(weights, whole, sems)
     slots = rows[0].shape[0]
     for k, block in enumerate(rows):
         x[k * slots : (k + 1) * slots] = block[...]
-    wait_all(copies_g)
-    wait_all(copies_u)
+    for copy in copies:
+        copy.wait()
     step = 256
-    for n in range(gate.shape[1] // step):
-        at = slice(n * step, (n + 1) * step)
-        gate_pre = dot(x[...], gate[:, at])
-        up_pre = dot(x[...], up[:, at])
+    for n in range(whole.shape[2] // step):
+        at = slice(n * step, (n + 1) * step)
+        gate_pre = dot(x[...], whole[0, :, at])
+        up_pre = dot(x[...], whole[1, :, at])
         sig = 1.0 / (1.0 + jnp.exp(-gate_pre))
         silu = gate_pre * sig
         hidden[:, at] = (silu * up_pre).astype(BF)
         slope_ref[:, at] = up_pre * sig * (1.0 + gate_pre * (1.0 - sig))
         silu_ref[:, at] = silu
-    wait_all(copies_d)
     step = 512
-    for n in range(down.shape[1] // step):
-        at = slice(n * step, (n + 1) * step)
-        part = dot(hidden[...], down[:, at]).astype(BF)
+    for n in range(whole.shape[1] // step):
+        at = slice(n * step, (n + 1) * step)
+        part = dot_t(hidden[...], whole[2, at]).astype(BF)
         for k, out in enumerate(outs):
             out[:, at] = part[k * slots : (k + 1) * slots]
 
 
 def backward_kernel(peers, pieces, *refs):
     rows, refs = refs[:peers], refs[peers:]
-    gates, refs = refs[:pieces], refs[pieces:]
-    ups, refs = refs[:pieces], refs[pieces:]
-    downs, refs = refs[:pieces], refs[pieces:]
+    weights, refs = refs[:pieces], refs[pieces:]
     slope_ref, silu_ref, refs = refs[0], refs[1], refs[2:]
     outs, refs = refs[:peers], refs[peers:]
-    gate, up, down, x, gate_grad, up_grad, sems = refs
-    copies_d = load_pieces(downs, down, sems.at[2], 1)
-    copies_g = load_pieces(gates, gate, sems.at[0], 0)
-    copies_u = load_pieces(ups, up, sems.at[1], 0)
+    whole, x, gate_grad, up_grad, sems = refs
+    copies = load_pieces(weights, whole, sems)
     slots = rows[0].shape[0]
     for k, block in enumerate(rows):
         x[k * slots : (k + 1) * slots] = block[...]
-    wait_all(copies_d)
+    for copy in copies:
+        copy.wait()
     step = 256
-    for n in range(gate.shape[1] // step):
-        at = slice(n * step, (n + 1) * step)
-        hidden_grad = dot_t(x[...], down[at, :])
+    for n in range(whole.shape[2] // step):
+        at = slice(n * step, (n + 1) * step)
+        hidden_grad = dot(x[...], whole[2, :, at])
         gate_grad[:, at] = (hidden_grad * slope_ref[:, at]).astype(BF)
         up_grad[:, at] = (hidden_grad * silu_ref[:, at]).astype(BF)
-    wait_all(copies_g)
-    wait_all(copies_u)
     step = 512
-    for n in range(gate.shape[0] // step):
-        at = slice(n * step, (n + 1) * step)
-        part = dot_t(gate_grad[...], gate[at, :]) + dot_t(up_grad[...], up[at, :])
+    for n in range(whole.shape[1] // step):
+        at = slice(n * step, (n + 1) * step)
+        part = dot_t(gate_grad[...], whole[0, at]) + dot_t(up_grad[...], whole[1, at])
         part = part.astype(BF)
         for k, out in enumerate(outs):
             out[:, at] = part[k * slots : (k + 1) * slots]
@@ -198,11 +204,10 @@
     if not cache:
         first, second, slot = routing(ids_ref, lax.axis_index("expert"))
         slots = backs[0].shape[0]
+        gates = [column(weight_ref[0, j : j + 1]) for j in range(2)]
         for k in range(len(backs)):
             place = placing(slot, k, slots)[:, :slots].astype(BF)
-            weight = jnp.where(first == k, weight_ref[0, :, 0:1], 0.0) + jnp.where(
-                second == k, weight_ref[0, :, 1:2], 0.0
-            )
+            weight = jnp.where(first == k, gates[0], 0.0) + jnp.where(second == k, gates[1], 0.0)
             cache.append((place, weight))
     total = None
     for back, (place, weight) in zip(backs, cache):
@@ -256,32 +261,29 @@
     slab = jax.ShapeDtypeStruct((slots, width), BF)
     slabs = [slab] * peers
     gain = norm_gain.reshape(1, width)
+    ids, gates = jnp.swapaxes(expert_ids, 1, 2), jnp.swapaxes(gate_weights, 1, 2)
 
     prev_keys = shifted(keys, ("expert", "ctx"), 1)
     prev_values = shifted(values, ("expert", "ctx"), 1)
 
-    def gathered(weight):
-        blocks = []
-        for dx in range(lax.axis_size("fsdp")):
-            block = weight if dx == 0 else swapped(weight, "fsdp", dx)
-            blocks.append(block)
-            blocks.append(swapped(block, "ctx", 1))
-        return blocks
-
-    gates, ups, downs = gathered(w_gate), gathered(w_up), gathered(w_down)
-
     def exchanged(blocks):
         return [block if k == 0 else swapped(block, "expert", k) for k, block in enumerate(blocks)]
 
-    sent_grads = pl.pallas_call(
-        lambda *refs: pack_kernel(slots, *refs),
-        out_shape=slabs,
-        in_specs=[VM] * 2,
-        out_specs=[VM] * peers,
+    own_weights, *sent_grads = pl.pallas_call(
+        lambda *refs: prepare_kernel(slots, *refs),
+        out_shape=[jax.ShapeDtypeStruct((3, w_gate.shape[1], hidden_count), BF)] + slabs,
+        in_specs=[VM] + [ANY] * 4,
+        out_specs=[VM] * (1 + peers),
+        scratch_shapes=[
+            pltpu.VMEM((tok, width), BF),
+            pltpu.VMEM(w_down.shape[1:], BF),
+            pltpu.SemaphoreType.DMA((4,)),
+        ],
         compiler_params=params(32),
-        name="pack_grad",
-    )(expert_ids, out_grad)
-    grads = exchanged(sent_grads)
+        name="prepare",
+    )(ids, out_grad, w_gate, w_up, w_down)
+    early = exchanged(sent_grads[:-1])
+    weights = [own_weights] + [swapped(own_weights, "fsdp", dx) for dx in range(1, lax.axis_size("fsdp"))]
 
     attended, *sent_rows = pl.pallas_call(
         lambda *refs: attend_kernel(slots, *refs),
@@ -290,37 +292,34 @@
         out_specs=[VM] * (1 + peers),
         compiler_params=params(32),
         name="attend",
-    )(queries, keys, values, prev_keys, prev_values, doc_ids, inputs, gain, expert_ids)
-    rows = exchanged(sent_rows)
+    )(after(queries, own_weights), keys, values, prev_keys, prev_values, doc_ids, inputs, gain, ids)
+    grads = early + [swapped(after(sent_grads[-1], attended), "expert", peers - 1)]
+    rows = exchanged([after(block, early[-1]) for block in sent_rows])
+    weights = [part for block in weights for part in (block, swapped(after(block, rows[-2], *early[1:]), "ctx", 1))]
 
     wide = jax.ShapeDtypeStruct((total, hidden_count), F32)
-    weights = [
-        pltpu.VMEM((width, hidden_count), BF),
-        pltpu.VMEM((width, hidden_count), BF),
-        pltpu.VMEM((hidden_count, width), BF),
-        pltpu.VMEM((total, width), BF),
-    ]
-    sems = pltpu.SemaphoreType.DMA((3, pieces))
+    scratch = [pltpu.VMEM((3, width, hidden_count), BF), pltpu.VMEM((total, width), BF)]
+    sems = pltpu.SemaphoreType.DMA((pieces,))
     *served_out, slope, silu = pl.pallas_call(
         lambda *refs: forward_kernel(peers, pieces, *refs),
         out_shape=slabs + [wide] * 2,
-        in_specs=[VM] * peers + [ANY] * (3 * pieces),
+        in_specs=[VM] * peers + [ANY] * pieces,
         out_specs=[VM] * (peers + 2),
-        scratch_shapes=weights + [pltpu.VMEM((total, hidden_count), BF), sems],
+        scratch_shapes=scratch + [pltpu.VMEM((total, hidden_count), BF), sems],
         compiler_params=params(48),
         name="forward",
-    )(*rows, *gates, *ups, *downs)
+    )(*rows, *weights)
     back_out = exchanged(served_out)
 
     served_grad = pl.pallas_call(
         lambda *refs: backward_kernel(peers, pieces, *refs),
         out_shape=slabs,
-        in_specs=[VM] * peers + [ANY] * (3 * pieces) + [VM] * 2,
+        in_specs=[VM] * peers + [ANY] * pieces + [VM] * 2,
         out_specs=[VM] * peers,
-        scratch_shapes=weights + [pltpu.VMEM((total, hidden_count), BF)] * 2 + [sems],
+        scratch_shapes=scratch + [pltpu.VMEM((total, hidden_count), BF)] * 2 + [sems],
         compiler_params=params(48),
         name="backward",
-    )(*grads, *gates, *ups, *downs, slope, silu)
+    )(*grads, *weights, slope, silu)
     back_grad = exchanged(served_grad)
 
     out_block = jax.ShapeDtypeStruct(inputs.shape, BF)
@@ -331,7 +330,7 @@
         out_specs=VM,
         compiler_params=params(32),
         name="layer",
-    )(expert_ids, gate_weights, inputs, attended, *back_out)
+    )(ids, gates, inputs, attended, *back_out)
     input_grad = pl.pallas_call(
         grad_kernel,
         out_shape=out_block,
@@ -340,7 +339,7 @@
         scratch_shapes=[pltpu.VMEM((tok, width), F32)],
         compiler_params=params(32),
         name="grad",
-    )(expert_ids, gate_weights, inputs, attended, gain, out_grad, *back_grad)
+    )(ids, gates, inputs, after(attended, layer_out), gain, out_grad, *back_grad)
     return layer_out, input_grad
 
 

time: 194 us -> 150 us (0.77)
  waiting for transfers between devices: 131 us -> 92.3 us
  local copies, waits for them, and re-layouts: 11.4 us -> 6.61 us
    ppermute x21 -> x15, waiting for transfers between devices: 123 us -> 78.9 us  [swapped(): return lax.ppermute(block, axis, [(i, i ^ distance) for i in range(count)])]
    ppermute x2, waiting for transfers between devices: 8.09 us -> 13.4 us  [shifted(): return lax.ppermute(block, axis, route)]
    unnamed x42 -> x34, local copies, waits for them, and re-layouts: 11.4 us -> 6.61 us
    ppermute x21 -> x15, starting transfers between devices: 17.7 us -> 19 us  [swapped(): return lax.ppermute(block, axis, [(i, i ^ distance) for i in range(count)])]
  transfers between devices with their start and end apart: 23 -> 17, of which waited for: 13 -> 10; matrix products, arithmetic and copies ran while one was open for 0% -> 0% of each run, Pallas kernels for 13% -> 15%
where the time goes in v3:
time: 150 us
  waiting for transfers between devices  92.3 us (62%)
  Pallas kernels  26 us (17%)
  starting transfers between devices  24.5 us (16%)
  local copies, waits for them, and re-layouts  6.61 us (4%)
    ppermute x15, waiting for transfers between devices, swapped(): return lax.ppermute(block, axis, [(i, i ^ distance) for i in range(count)])  78.9 us
    ppermute x15, starting transfers between devices, swapped(): return lax.ppermute(block, axis, [(i, i ^ distance) for i in range(count)])  19 us
    ppermute x2, waiting for transfers between devices, shifted(): return lax.ppermute(block, axis, route)  13.4 us
    pallas_call x1, Pallas kernels, shards(): pl.pallas_call(lambda *refs: backward_kernel(peers, pieces, *refs), out_s...  7.05 us
    pallas_call x1, Pallas kernels, shards(): pl.pallas_call(lambda *refs: forward_kernel(peers, pieces, *refs), out_sh...  7.04 us
    unnamed x34, local copies, waits for them, and re-layouts  6.61 us
    pallas_call x1, Pallas kernels, shards(): pl.pallas_call(lambda *refs: attend_kernel(slots, *refs), out_shape=[jax....  6.32 us
    ppermute x2, starting transfers between devices, shifted(): return lax.ppermute(block, axis, route)  5.5 us
  transfers between devices with their start and end apart: 17, of which 10 were waited for; matrix products, arithmetic and copies ran while one was open for 0% of the time, Pallas kernels for 15%

profile of v3, /device:TPU:10, one launch (start us, length us, event | category | flops | bytes accessed | tf_op | source)
XLA Modules:
  0.0 150.2 jit_solution(9253119261970447070)
XLA Ops:
  5.8 1.4 prepare.1
  7.9 1.9 %collective-permute-start = (bf16[1,128,2048]{2,1,0:T(8,128)(2,1)S(1)}, bf16[1,128,2048]{2,1,0:T(8,128)(2,1)S(1)}, u32[]{:S(2)}, u32[]{:S(2)}) collective-permute-start(bf16[1,128,2048]{2,1,0:T(8,128)(2,1)S(1)} %copy-done.8), channel_id=1, source_target_pairs={{0,1},{1,4},{4,5},{5,8},{8,9},{9,12},{12,13},{2,3},{3,6},{6,7},{7,... | collective-permute-start | bytes 1572872 | tf_op jit(solution)/shard_map/ppermute | solution.py:29
  9.8 3.6 %collective-permute-start.1 = (bf16[1,128,2048]{2,1,0:T(8,128)(2,1)S(1)}, bf16[1,128,2048]{2,1,0:T(8,128)(2,1)S(1)}, u32[]{:S(2)}, u32[]{:S(2)}) collective-permute-start(bf16[1,128,2048]{2,1,0:T(8,128)(2,1)S(1)} %copy-done.9), channel_id=1, source_target_pairs={{0,1},{1,4},{4,5},{5,8},{8,9},{9,12},{12,13},{2,3},{3,6},{6,7},{7,... | collective-permute-start | bytes 1572872 | tf_op jit(solution)/shard_map/ppermute | solution.py:29
  14.4 2.1 %collective-permute-start.6 = (bf16[80,2048]{1,0:T(8,128)(2,1)S(1)}, bf16[80,2048]{1,0:T(8,128)(2,1)S(1)}, u32[]{:S(2)}, u32[]{:S(2)}) collective-permute-start(bf16[80,2048]{1,0:T(8,128)(2,1)S(1)} %get-tuple-element.43), channel_id=1, source_target_pairs={{0,4},{4,0},{8,12},{12,8},{1,5},{5,1},{9,13},{13,9},{2,6},{6,2},{1... | collective-permute-start | bytes 983048 | tf_op jit(solution)/shard_map/ppermute | solution.py:23
  16.5 2.1 %collective-permute-done.refs_3_ = bf16[1,128,2048]{2,1,0:T(8,128)(2,1)S(1)} collective-permute-done((bf16[1,128,2048]{2,1,0:T(8,128)(2,1)S(1)}, bf16[1,128,2048]{2,1,0:T(8,128)(2,1)S(1)}, u32[]{:S(2)}, u32[]{:S(2)}) %collective-permute-start) | collective-permute-done | bytes 524320 | tf_op jit(solution)/shard_map/ppermute | solution.py:29
  18.7 11.2 %collective-permute-done.1.refs_4_ = bf16[1,128,2048]{2,1,0:T(8,128)(2,1)S(1)} collective-permute-done((bf16[1,128,2048]{2,1,0:T(8,128)(2,1)S(1)}, bf16[1,128,2048]{2,1,0:T(8,128)(2,1)S(1)}, u32[]{:S(2)}, u32[]{:S(2)}) %collective-permute-start.1) | collective-permute-done | bytes 524320 | tf_op jit(solution)/shard_map/ppermute | solution.py:29
  29.9 6.3 %attend.1 = (bf16[128,2048]{1,0:T(8,128)(2,1)S(1)}, bf16[80,2048]{1,0:T(8,128)(2,1)S(1)}, bf16[80,2048]{1,0:T(8,128)(2,1)S(1)}, bf16[80,2048]{1,0:T(8,128)(2,1)S(1)}, bf16[80,2048]{1,0:T(8,128)(2,1)S(1)}) custom-call(bf16[1,128,2048]{2,1,0:T(8,128)(2,1)S(1)} %copy-done.7, bf16[1,128,2048]{2,1,0:T(8,128)(2,1)S(1)} %copy-done.8, ...), custom_call_target="tpu_custom_call" | custom-call | tf_op jit(solution)/shard_map/attend/pallas_call | solution.py:288
  36.2 3.8 %collective-permute-start.4 = (bf16[80,2048]{1,0:T(8,128)(2,1)S(1)}, bf16[80,2048]{1,0:T(8,128)(2,1)S(1)}, u32[]{:S(2)}, u32[]{:S(2)}) collective-permute-start(bf16[80,2048]{1,0:T(8,128)(2,1)S(1)} %get-tuple-element.40), channel_id=1, source_target_pairs={{0,8},{4,12},{8,0},{12,4},{1,9},{5,13},{9,1},{13,5},{2,10},{6,14},... | collective-permute-start | bytes 983048 | tf_op jit(solution)/shard_map/ppermute | solution.py:23
  40.1 13.3 %collective-permute-done.4.refs_2_ = bf16[80,2048]{1,0:T(8,128)(2,1)S(1)} collective-permute-done((bf16[80,2048]{1,0:T(8,128)(2,1)S(1)}, bf16[80,2048]{1,0:T(8,128)(2,1)S(1)}, u32[]{:S(2)}, u32[]{:S(2)}) %collective-permute-start.4) | collective-permute-done | bytes 327712 | tf_op jit(solution)/shard_map/ppermute | solution.py:23
  53.4 7.0 %collective-permute-done.8.refs_6_ = bf16[3,512,768]{2,1,0:T(8,128)(2,1)S(1)} collective-permute-done((bf16[3,512,768]{2,1,0:T(8,128)(2,1)S(1)}, bf16[3,512,768]{2,1,0:T(8,128)(2,1)S(1)}, u32[]{:S(2)}, u32[]{:S(2)}) %collective-permute-start.8) | collective-permute-done | bytes 2359328 | tf_op jit(solution)/shard_map/ppermute | solution.py:23
  60.4 1.6 %collective-permute-start.5 = (bf16[80,2048]{1,0:T(8,128)(2,1)S(1)}, bf16[80,2048]{1,0:T(8,128)(2,1)S(1)}, u32[]{:S(2)}, u32[]{:S(2)}) collective-permute-start(bf16[80,2048]{1,0:T(8,128)(2,1)S(1)} %get-tuple-element.42), channel_id=1, source_target_pairs={{0,12},{4,8},{8,4},{12,0},{1,13},{5,9},{9,5},{13,1},{2,14},{6,10},... | collective-permute-start | bytes 983048 | tf_op jit(solution)/shard_map/ppermute | solution.py:23
  61.9 2.5 %collective-permute-start.3 = (bf16[80,2048]{1,0:T(8,128)(2,1)S(1)}, bf16[80,2048]{1,0:T(8,128)(2,1)S(1)}, u32[]{:S(2)}, u32[]{:S(2)}) collective-permute-start(bf16[80,2048]{1,0:T(8,128)(2,1)S(1)} %get-tuple-element.38), channel_id=1, source_target_pairs={{0,4},{4,0},{8,12},{12,8},{1,5},{5,1},{9,13},{13,9},{2,6},{6,2},{1... | collective-permute-start | bytes 983048 | tf_op jit(solution)/shard_map/ppermute | solution.py:23
  64.4 13.5 %collective-permute-done.5.refs_3_ = bf16[80,2048]{1,0:T(8,128)(2,1)S(1)} collective-permute-done((bf16[80,2048]{1,0:T(8,128)(2,1)S(1)}, bf16[80,2048]{1,0:T(8,128)(2,1)S(1)}, u32[]{:S(2)}, u32[]{:S(2)}) %collective-permute-start.5) | collective-permute-done | bytes 327712 | tf_op jit(solution)/shard_map/ppermute | solution.py:23
  77.9 2.1 %collective-permute-done.3.refs_1_ = bf16[80,2048]{1,0:T(8,128)(2,1)S(1)} collective-permute-done((bf16[80,2048]{1,0:T(8,128)(2,1)S(1)}, bf16[80,2048]{1,0:T(8,128)(2,1)S(1)}, u32[]{:S(2)}, u32[]{:S(2)}) %collective-permute-start.3) | collective-permute-done | bytes 327712 | tf_op jit(solution)/shard_map/ppermute | solution.py:23
  81.4 7.0 %forward.1 = (bf16[80,2048]{1,0:T(8,128)(2,1)S(1)}, bf16[80,2048]{1,0:T(8,128)(2,1)S(1)}, bf16[80,2048]{1,0:T(8,128)(2,1)S(1)}, bf16[80,2048]{1,0:T(8,128)(2,1)S...) custom-call(bf16[80,2048]{1,0:T(8,128)(2,1)S(1)} %get-tuple-element.36.refs_0_, ...), custom_call_target="tpu_custom_call" | custom-call | tf_op jit(solution)/shard_map/forward/pallas_call | solution.py:303
  89.5 2.5 %collective-permute-start.12 = (bf16[80,2048]{1,0:T(8,128)(2,1)S(1)}, bf16[80,2048]{1,0:T(8,128)(2,1)S(1)}, u32[]{:S(2)}, u32[]{:S(2)}) collective-permute-start(bf16[80,2048]{1,0:T(8,128)(2,1)S(1)} %get-tuple-element.49), channel_id=1, source_target_pairs={{0,12},{4,8},{8,4},{12,0},{1,13},{5,9},{9,5},{13,1},{2,14},{6,10},... | collective-permute-start | bytes 983048 | tf_op jit(solution)/shard_map/ppermute | solution.py:23
  92.0 7.0 %backward.1 = (bf16[80,2048]{1,0:T(8,128)(2,1)S(1)}, bf16[80,2048]{1,0:T(8,128)(2,1)S(1)}, bf16[80,2048]{1,0:T(8,128)(2,1)S(1)}, bf16[80,2048]{1,0:T(8,128)(2,1)S(1)}) custom-call(bf16[80,2048]{1,0:T(8,128)(2,1)S(1)} %get-tuple-element.51.refs_0_, bf16[80,2048]{1,0:T(8,128)(2,1)S(1)} %collective-permute-done.6.refs_1_, ...), custom_call_target="tpu_custom_call" | custom-call | tf_op jit(solution)/shard_map/backward/pallas_call | solution.py:314
  100.3 1.8 %collective-permute-start.15 = (bf16[80,2048]{1,0:T(8,128)(2,1)S(1)}, bf16[80,2048]{1,0:T(8,128)(2,1)S(1)}, u32[]{:S(2)}, u32[]{:S(2)}) collective-permute-start(bf16[80,2048]{1,0:T(8,128)(2,1)S(1)} %get-tuple-element.58), channel_id=1, source_target_pairs={{0,8},{4,12},{8,0},{12,4},{1,9},{5,13},{9,1},{13,5},{2,10},{6,14},... | collective-permute-start | bytes 983048 | tf_op jit(solution)/shard_map/ppermute | solution.py:23
  102.9 8.7 %collective-permute-done.11.refs_2_ = bf16[80,2048]{1,0:T(8,128)(2,1)S(1)} collective-permute-done((bf16[80,2048]{1,0:T(8,128)(2,1)S(1)}, bf16[80,2048]{1,0:T(8,128)(2,1)S(1)}, u32[]{:S(2)}, u32[]{:S(2)}) %collective-permute-start.11) | collective-permute-done | bytes 327712 | tf_op jit(solution)/shard_map/ppermute | solution.py:23
  111.6 24.2 %collective-permute-done.12.refs_3_ = bf16[80,2048]{1,0:T(8,128)(2,1)S(1)} collective-permute-done((bf16[80,2048]{1,0:T(8,128)(2,1)S(1)}, bf16[80,2048]{1,0:T(8,128)(2,1)S(1)}, u32[]{:S(2)}, u32[]{:S(2)}) %collective-permute-start.12) | collective-permute-done | bytes 327712 | tf_op jit(solution)/shard_map/ppermute | solution.py:23
  135.8 1.9 %layer.1 = bf16[1,128,2048]{2,1,0:T(8,128)(2,1)} custom-call(s32[1,2,128]{2,1,0:T(2,128)S(1)} %bitcast.7, f32[1,2,128]{2,1,0:T(2,128)S(1)} %bitcast.9, bf16[1,128,2048]{2,1,0:T(8,128)(2,1)S(1)} %copy-done.1, bf16[128,2048]{1,0:T(8,128)(2,1)S(1)} %get-tuple-element.50.att_ref, bf16[80,2048]{1,0:T(8,128)(2,1)S(1)} %get-tuple-element.46.refs_0_, ...), custom_call_target="tpu_custom_call" | custom-call | tf_op jit(solution)/shard_map/layer/pallas_call | solution.py:326
  137.7 2.6 %collective-permute-done.15.refs_2_ = bf16[80,2048]{1,0:T(8,128)(2,1)S(1)} collective-permute-done((bf16[80,2048]{1,0:T(8,128)(2,1)S(1)}, bf16[80,2048]{1,0:T(8,128)(2,1)S(1)}, u32[]{:S(2)}, u32[]{:S(2)}) %collective-permute-start.15) | collective-permute-done | bytes 327712 | tf_op jit(solution)/shard_map/ppermute | solution.py:23
  140.3 7.6 %collective-permute-done.16.refs_3_ = bf16[80,2048]{1,0:T(8,128)(2,1)S(1)} collective-permute-done((bf16[80,2048]{1,0:T(8,128)(2,1)S(1)}, bf16[80,2048]{1,0:T(8,128)(2,1)S(1)}, u32[]{:S(2)}, u32[]{:S(2)}) %collective-permute-start.16) | collective-permute-done | bytes 327712 | tf_op jit(solution)/shard_map/ppermute | solution.py:23
  147.9 2.3 %grad.1 = bf16[1,128,2048]{2,1,0:T(8,128)(2,1)} custom-call(s32[1,2,128]{2,1,0:T(2,128)S(1)} %bitcast.8, f32[1,2,128]{2,1,0:T(2,128)S(1)} %bitcast.10, bf16[1,128,2048]{2,1,0:T(8,128)(2,1)S(1)} %copy-done.1, bf16[128,2048]{1,0:T(8,128)(2,1)S(1)} %get-tuple-element.50.att_ref, f32[1,2048]{1,0:T(1,128)S(1)} %bitcast.4, bf16[1,128,2048]{2,1,0:T(8,128)(2,1)S(1)} %copy-done.3, ...), custom_call_target="tpu_custom_call" | custom-call | tf_op jit(solution)/shard_map/grad/pallas_call | solution.py:334
  (50 shorter events, 11.3 us)
Async XLA Ops:
  0.6 29.3 %copy-start.1 = (bf16[1,128,2048]{2,1,0:T(8,128)(2,1)S(1)}, bf16[1,128,2048]{2,1,0:T(8,128)(2,1)}, u32[]{:S(2)}) copy-start(bf16[1,128,2048]{2,1,0:T(8,128)(2,1)} %in_ref.3) | copy-start | bytes 1572868
  5.8 24.1 %copy-start.10 = (f32[2048]{0:T(1024)S(1)}, f32[2048]{0:T(1024)}, u32[]{:S(2)}) copy-start(f32[2048]{0:T(1024)} %param.17) | copy-start | bytes 24580
  5.8 24.1 %copy-start.14 = (s32[1,1024]{1,0:T(1,128)S(1)}, s32[1,1024]{1,0:T(1,128)}, u32[]{:S(2)}) copy-start(s32[1,1024]{1,0:T(1,128)} %refs_5_.1) | copy-start | bytes 12292
  7.3 72.7 %copy-start = (bf16[3,512,768]{2,1,0:T(8,128)(2,1)}, bf16[3,512,768]{2,1,0:T(8,128)(2,1)S(1)}, u32[]{:S(2)}) copy-start(bf16[3,512,768]{2,1,0:T(8,128)(2,1)S(1)} %get-tuple-element.44.refs_4_) | copy-start | bytes 7077892
  7.3 53.1 %collective-permute-start.8 = (bf16[3,512,768]{2,1,0:T(8,128)(2,1)S(1)}, bf16[3,512,768]{2,1,0:T(8,128)(2,1)S(1)}, u32[]{:S(2)}, u32[]{:S(2)}) collective-permute-start(bf16[3,512,768]{2,1,0:T(8,128)(2,1)S(1)} %get-tuple-element.44.refs_4_), channel_id=1, source_target_pairs={{0,2},{2,0},{1,3},{3,1},{4,6},{6,4},{5,7},{7,5},{8,10},{10,8},{9,1... | collective-permute-start | bytes 7077896 | tf_op jit(solution)/shard_map/ppermute | solution.py:23
  7.9 10.7 %collective-permute-start = (bf16[1,128,2048]{2,1,0:T(8,128)(2,1)S(1)}, bf16[1,128,2048]{2,1,0:T(8,128)(2,1)S(1)}, u32[]{:S(2)}, u32[]{:S(2)}) collective-permute-start(bf16[1,128,2048]{2,1,0:T(8,128)(2,1)S(1)} %copy-done.8), channel_id=1, source_target_pairs={{0,1},{1,4},{4,5},{5,8},{8,9},{9,12},{12,13},{2,3},{3,6},{6,7},{7,... | collective-permute-start | bytes 1572872 | tf_op jit(solution)/shard_map/ppermute | solution.py:29
  9.8 20.1 %collective-permute-start.1 = (bf16[1,128,2048]{2,1,0:T(8,128)(2,1)S(1)}, bf16[1,128,2048]{2,1,0:T(8,128)(2,1)S(1)}, u32[]{:S(2)}, u32[]{:S(2)}) collective-permute-start(bf16[1,128,2048]{2,1,0:T(8,128)(2,1)S(1)} %copy-done.9), channel_id=1, source_target_pairs={{0,1},{1,4},{4,5},{5,8},{8,9},{9,12},{12,13},{2,3},{3,6},{6,7},{7,... | collective-permute-start | bytes 1572872 | tf_op jit(solution)/shard_map/ppermute | solution.py:29
  13.4 22.8 %collective-permute-start.2 = (bf16[80,2048]{1,0:T(8,128)(2,1)S(1)}, bf16[80,2048]{1,0:T(8,128)(2,1)S(1)}, u32[]{:S(2)}, u32[]{:S(2)}) collective-permute-start(bf16[80,2048]{1,0:T(8,128)(2,1)S(1)} %get-tuple-element.35), channel_id=1, source_target_pairs={{0,8},{4,12},{8,0},{12,4},{1,9},{5,13},{9,1},{13,5},{2,10},{6,14},... | collective-permute-start | bytes 983048 | tf_op jit(solution)/shard_map/ppermute | solution.py:23
  14.4 25.6 %collective-permute-start.6 = (bf16[80,2048]{1,0:T(8,128)(2,1)S(1)}, bf16[80,2048]{1,0:T(8,128)(2,1)S(1)}, u32[]{:S(2)}, u32[]{:S(2)}) collective-permute-start(bf16[80,2048]{1,0:T(8,128)(2,1)S(1)} %get-tuple-element.43), channel_id=1, source_target_pairs={{0,4},{4,0},{8,12},{12,8},{1,5},{5,1},{9,13},{13,9},{2,6},{6,2},{1... | collective-permute-start | bytes 983048 | tf_op jit(solution)/shard_map/ppermute | solution.py:23
  36.2 17.1 %collective-permute-start.4 = (bf16[80,2048]{1,0:T(8,128)(2,1)S(1)}, bf16[80,2048]{1,0:T(8,128)(2,1)S(1)}, u32[]{:S(2)}, u32[]{:S(2)}) collective-permute-start(bf16[80,2048]{1,0:T(8,128)(2,1)S(1)} %get-tuple-element.40), channel_id=1, source_target_pairs={{0,8},{4,12},{8,0},{12,4},{1,9},{5,13},{9,1},{13,5},{2,10},{6,14},... | collective-permute-start | bytes 983048 | tf_op jit(solution)/shard_map/ppermute | solution.py:23
  53.3 26.6 %collective-permute-start.7 = (bf16[3,512,768]{2,1,0:T(8,128)(2,1)S(1)}, bf16[3,512,768]{2,1,0:T(8,128)(2,1)S(1)}, u32[]{:S(2)}, u32[]{:S(2)}) collective-permute-start(bf16[3,512,768]{2,1,0:T(8,128)(2,1)S(1)} %get-tuple-element.44.refs_4_), channel_id=1, source_target_pairs={{0,1},{1,0},{2,3},{3,2},{4,5},{5,4},{6,7},{7,6},{8,9},{9,8},{10,11... | collective-permute-start | bytes 7077896 | tf_op jit(solution)/shard_map/ppermute | solution.py:23
  60.4 19.6 %collective-permute-start.9 = (bf16[3,512,768]{2,1,0:T(8,128)(2,1)S(1)}, bf16[3,512,768]{2,1,0:T(8,128)(2,1)}, u32[]{:S(2)}, u32[]{:S(2)}) collective-permute-start(bf16[3,512,768]{2,1,0:T(8,128)(2,1)S(1)} %collective-permute-done.8.refs_6_), channel_id=1, source_target_pairs={{0,1},{1,0},{2,3},{3,2},{4,5},{5,4},{6,7},{7,6},{8,9},{9,8},{10,11... | collective-permute-start | bytes 7077896 | tf_op jit(solution)/shard_map/ppermute | solution.py:23
  60.4 17.5 %collective-permute-start.5 = (bf16[80,2048]{1,0:T(8,128)(2,1)S(1)}, bf16[80,2048]{1,0:T(8,128)(2,1)S(1)}, u32[]{:S(2)}, u32[]{:S(2)}) collective-permute-start(bf16[80,2048]{1,0:T(8,128)(2,1)S(1)} %get-tuple-element.42), channel_id=1, source_target_pairs={{0,12},{4,8},{8,4},{12,0},{1,13},{5,9},{9,5},{13,1},{2,14},{6,10},... | collective-permute-start | bytes 983048 | tf_op jit(solution)/shard_map/ppermute | solution.py:23
  61.9 18.0 %collective-permute-start.3 = (bf16[80,2048]{1,0:T(8,128)(2,1)S(1)}, bf16[80,2048]{1,0:T(8,128)(2,1)S(1)}, u32[]{:S(2)}, u32[]{:S(2)}) collective-permute-start(bf16[80,2048]{1,0:T(8,128)(2,1)S(1)} %get-tuple-element.38), channel_id=1, source_target_pairs={{0,4},{4,0},{8,12},{12,8},{1,5},{5,1},{9,13},{13,9},{2,6},{6,2},{1... | collective-permute-start | bytes 983048 | tf_op jit(solution)/shard_map/ppermute | solution.py:23
  64.4 27.6 %collective-permute-start.13 = (bf16[80,2048]{1,0:T(8,128)(2,1)S(1)}, bf16[80,2048]{1,0:T(8,128)(2,1)S(1)}, u32[]{:S(2)}, u32[]{:S(2)}) collective-permute-start(bf16[80,2048]{1,0:T(8,128)(2,1)S(1)} %get-tuple-element.53), channel_id=1, source_target_pairs={{0,12},{4,8},{8,4},{12,0},{1,13},{5,9},{9,5},{13,1},{2,14},{6,10},... | collective-permute-start | bytes 983048 | tf_op jit(solution)/shard_map/ppermute | solution.py:23
  88.4 13.7 %collective-permute-start.10 = (bf16[80,2048]{1,0:T(8,128)(2,1)S(1)}, bf16[80,2048]{1,0:T(8,128)(2,1)S(1)}, u32[]{:S(2)}, u32[]{:S(2)}) collective-permute-start(bf16[80,2048]{1,0:T(8,128)(2,1)S(1)} %get-tuple-element.47), channel_id=1, source_target_pairs={{0,4},{4,0},{8,12},{12,8},{1,5},{5,1},{9,13},{13,9},{2,6},{6,2},{1... | collective-permute-start | bytes 983048 | tf_op jit(solution)/shard_map/ppermute | solution.py:23
  88.8 22.8 %collective-permute-start.11 = (bf16[80,2048]{1,0:T(8,128)(2,1)S(1)}, bf16[80,2048]{1,0:T(8,128)(2,1)S(1)}, u32[]{:S(2)}, u32[]{:S(2)}) collective-permute-start(bf16[80,2048]{1,0:T(8,128)(2,1)S(1)} %get-tuple-element.48), channel_id=1, source_target_pairs={{0,8},{4,12},{8,0},{12,4},{1,9},{5,13},{9,1},{13,5},{2,10},{6,14},... | collective-permute-start | bytes 983048 | tf_op jit(solution)/shard_map/ppermute | solution.py:23
  89.5 46.3 %collective-permute-start.12 = (bf16[80,2048]{1,0:T(8,128)(2,1)S(1)}, bf16[80,2048]{1,0:T(8,128)(2,1)S(1)}, u32[]{:S(2)}, u32[]{:S(2)}) collective-permute-start(bf16[80,2048]{1,0:T(8,128)(2,1)S(1)} %get-tuple-element.49), channel_id=1, source_target_pairs={{0,12},{4,8},{8,4},{12,0},{1,13},{5,9},{9,5},{13,1},{2,14},{6,10},... | collective-permute-start | bytes 983048 | tf_op jit(solution)/shard_map/ppermute | solution.py:23
  92.0 43.8 %copy-start.12 = (s32[1,128,2]{1,2,0:T(2,128)S(1)}, s32[1,128,2]{1,2,0:T(2,128)}, u32[]{:S(2)}) copy-start(s32[1,128,2]{1,2,0:T(2,128)} %param.18) | copy-start | bytes 3076
  92.0 43.8 %copy-start.13 = (f32[1,128,2]{1,2,0:T(2,128)S(1)}, f32[1,128,2]{1,2,0:T(2,128)}, u32[]{:S(2)}) copy-start(f32[1,128,2]{1,2,0:T(2,128)} %param.19) | copy-start | bytes 3076
  99.1 48.8 %copy-start.3 = (bf16[1,128,2048]{2,1,0:T(8,128)(2,1)S(1)}, bf16[1,128,2048]{2,1,0:T(8,128)(2,1)}, u32[]{:S(2)}) copy-start(bf16[1,128,2048]{2,1,0:T(8,128)(2,1)} %up_ref.1) | copy-start | bytes 1572868
  99.1 38.6 %collective-permute-start.14 = (bf16[80,2048]{1,0:T(8,128)(2,1)S(1)}, bf16[80,2048]{1,0:T(8,128)(2,1)S(1)}, u32[]{:S(2)}, u32[]{:S(2)}) collective-permute-start(bf16[80,2048]{1,0:T(8,128)(2,1)S(1)} %get-tuple-element.57), channel_id=1, source_target_pairs={{0,4},{4,0},{8,12},{12,8},{1,5},{5,1},{9,13},{13,9},{2,6},{6,2},{1... | collective-permute-start | bytes 983048 | tf_op jit(solution)/shard_map/ppermute | solution.py:23
  100.3 40.0 %collective-permute-start.15 = (bf16[80,2048]{1,0:T(8,128)(2,1)S(1)}, bf16[80,2048]{1,0:T(8,128)(2,1)S(1)}, u32[]{:S(2)}, u32[]{:S(2)}) collective-permute-start(bf16[80,2048]{1,0:T(8,128)(2,1)S(1)} %get-tuple-element.58), channel_id=1, source_target_pairs={{0,8},{4,12},{8,0},{12,4},{1,9},{5,13},{9,1},{13,5},{2,10},{6,14},... | collective-permute-start | bytes 983048 | tf_op jit(solution)/shard_map/ppermute | solution.py:23
  102.1 45.8 %collective-permute-start.16 = (bf16[80,2048]{1,0:T(8,128)(2,1)S(1)}, bf16[80,2048]{1,0:T(8,128)(2,1)S(1)}, u32[]{:S(2)}, u32[]{:S(2)}) collective-permute-start(bf16[80,2048]{1,0:T(8,128)(2,1)S(1)} %get-tuple-element.59), channel_id=1, source_target_pairs={{0,12},{4,8},{8,4},{12,0},{1,13},{5,9},{9,5},{13,1},{2,14},{6,10},... | collective-permute-start | bytes 983048 | tf_op jit(solution)/shard_map/ppermute | solution.py:23
  (10 other events, 56.4 us)

commit v4 on v3

v4 whole, which is shorter than its diff:
```python
import jax
import jax.numpy as jnp
from jax import lax
from jax.experimental import pallas as pl
from jax.experimental.pallas import tpu as pltpu
from jax.sharding import PartitionSpec as P

HEADS = 16
HD = 128
BF = jnp.bfloat16
F32 = jnp.float32
VM = pl.BlockSpec(memory_space=pltpu.VMEM)
MIB = 1024 * 1024


def params(mib):
    return pltpu.CompilerParams(vmem_limit_bytes=mib * MIB)


def swapped(block, axis, distance):
    count = lax.axis_size(axis)
    return lax.ppermute(block, axis, [(i, i ^ distance) for i in range(count)])


def shifted(block, axis, distance):
    devices = range(lax.axis_size(axis))
    route = [(i - distance, i) for i in devices if i - distance in devices]
    return lax.ppermute(block, axis, route)


def after(block, *others):
    return lax.optimization_barrier((block, *others))[0]


def dot(a, b):
    return jnp.dot(a, b, preferred_element_type=F32)


def dot_t(a, b):
    return lax.dot_general(a, b, (((1,), (1,)), ((), ())), preferred_element_type=F32)


def column(row):
    tok = row.shape[1]
    return jnp.broadcast_to(row, (tok, tok)).T[:, 0:1]


def routing(first, second, here):
    tok = first.shape[1]
    lane = lax.broadcasted_iota(jnp.int32, (tok, 128), 1)
    row = lax.broadcasted_iota(jnp.int32, (tok, tok), 0)
    col = lax.broadcasted_iota(jnp.int32, (tok, tok), 1)
    first, second = column(first) ^ here, column(second) ^ here
    chosen = (first == lane) | (second == lane)
    before = (col < row).astype(BF)
    rank = dot(before, chosen.astype(BF))
    slot = jnp.where(chosen, rank, -1.0)
    return first, second, slot


def placing(slot, k, slots):
    tok = slot.shape[0]
    lane = lax.broadcasted_iota(jnp.int32, (tok, 128), 1)
    return jnp.where(lane == slot[:, k : k + 1].astype(jnp.int32), 1.0, 0.0)


def placing_table(slot, slots, count):
    return jnp.concatenate([placing(slot, k, slots).T[:slots] for k in range(count)], 0).astype(BF)


def pack(rows, slot, slots, out_refs):
    packed = dot(placing_table(slot, slots, len(out_refs)), rows).astype(BF)
    for k, out in enumerate(out_refs):
        out[...] = packed[k * slots : (k + 1) * slots]


def prepare_kernel(slots, ids_ref, k_hbm, v_hbm, rows_hbm, g_hbm, u_hbm, d_hbm, both_hbm, weight_hbm, *refs):
    out_refs, (both, weight, rows, down, sems) = refs[:-5], refs[-5:]
    pairs = [
        (k_hbm.at[0], both.at[0]),
        (v_hbm.at[0], both.at[1]),
        (d_hbm.at[0], down),
        (g_hbm.at[0], weight.at[0]),
        (u_hbm.at[0], weight.at[1]),
        (rows_hbm.at[0], rows),
        (both.at[0], both_hbm.at[0]),
        (both.at[1], both_hbm.at[1]),
        (weight.at[0], weight_hbm.at[0]),
        (weight.at[1], weight_hbm.at[1]),
        (weight.at[2], weight_hbm.at[2]),
    ]
    copies = [pltpu.make_async_copy(source, target, sems.at[n]) for n, (source, target) in enumerate(pairs)]
    for copy in copies[:6]:
        copy.start()
    _, _, slot = routing(ids_ref[0, 0:1], ids_ref[0, 1:2], lax.axis_index("expert"))
    for arrived, leaving in ((0, 6), (1, 7)):
        copies[arrived].wait()
        copies[leaving].start()
    copies[2].wait()
    weight[2] = down[...].T
    copies[10].start()
    for arrived, leaving in ((3, 8), (4, 9)):
        copies[arrived].wait()
        copies[leaving].start()
    copies[5].wait()
    pack(rows[...], slot, slots, out_refs)
    for copy in copies[6:]:
        copy.wait()


def attend_kernel(
    slots, q_ref, k_ref, v_ref, past_ref, doc_ref, in_ref, gain_ref, ids_ref, att_ref, *refs
):
    out_refs, (resid_ref, squares_ref) = refs[:-2], refs[-2:]
    group, groups = pl.program_id(0), pl.num_programs(0)
    tok, part_width = q_ref.shape[1], q_ref.shape[2]
    here = lax.axis_index("expert")
    first = (here * lax.axis_size("ctx") + lax.axis_index("ctx")) * tok
    before = jnp.maximum(first - tok, 0)
    own_docs = doc_ref[:, pl.ds(pl.multiple_of(first, tok), tok)]
    past_docs = doc_ref[:, pl.ds(pl.multiple_of(before, tok), tok)]
    row = lax.broadcasted_iota(jnp.int32, (tok, tok), 0)
    col = lax.broadcasted_iota(jnp.int32, (tok, tok), 1)
    own_all = jnp.broadcast_to(own_docs, (tok, tok))
    query_docs = own_all.T
    see_own = (query_docs == own_all) & (col <= row)
    see_past = (query_docs == past_docs) & (first > 0)
    scale = HD ** (-0.5)
    squares = jnp.zeros((tok, HD), F32)
    for h in range(part_width // HD):
        at = slice(h * HD, (h + 1) * HD)
        q = q_ref[0, :, at]
        own = jnp.where(see_own, dot_t(q, k_ref[0, :, at]) * scale, -jnp.inf)
        past = jnp.where(see_past, dot_t(q, past_ref[0, :, at]) * scale, -jnp.inf)
        top = jnp.maximum(own, past).max(axis=1, keepdims=True)
        own, past = jnp.exp(own - top), jnp.exp(past - top)
        total = (own + past).sum(axis=1, keepdims=True)
        inverse = 1.0 / total
        own, past = (own * inverse).astype(BF), (past * inverse).astype(BF)
        part = dot(own, v_ref[0, :, at]) + dot(past, past_ref[1, :, at])
        part = part.astype(BF)
        att_ref[:, at] = part
        resid = in_ref[0, :, at].astype(F32) + part.astype(F32)
        resid_ref[group, :, at] = resid
        squares = squares + resid * resid

    @pl.when(group == 0)
    def _():
        squares_ref[...] = squares

    @pl.when(group > 0)
    def _():
        squares_ref[...] += squares

    @pl.when(group == groups - 1)
    def _():
        parts = resid_ref.shape[0]
        width = parts * part_width
        inv_rms = lax.rsqrt(squares_ref[...].sum(axis=1, keepdims=True) / width + 1e-06)
        _, _, slot = routing(ids_ref[0, 0:1], ids_ref[0, 1:2], here)
        table = placing_table(slot, slots, len(out_refs))
        for n in range(parts):
            at = slice(n * part_width, (n + 1) * part_width)
            normed = (resid_ref[n] * inv_rms * gain_ref[:, at]).astype(BF)
            packed = dot(table, normed).astype(BF)
            for k, out in enumerate(out_refs):
                out[:, at] = packed[k * slots : (k + 1) * slots]


def quarter(j, size):
    mine = lax.axis_index("fsdp") * lax.axis_size("ctx") + lax.axis_index("ctx")
    return pl.ds(pl.multiple_of((mine ^ j) * size, size), size)


def gather_rows(rows, slots, x):
    for j in range(x.shape[0]):
        at = quarter(j, x.shape[2])
        for k, block in enumerate(rows):
            x[j, k * slots : (k + 1) * slots] = block[:, at]


def summed(terms):
    total = terms[0]
    for term in terms[1:]:
        total = total + term
    return total


def hidden_kernel(count, pieces, *refs):
    rows, weights, refs = refs[:count], refs[count : count + pieces], refs[count + pieces :]
    hidden_ref, slope_ref, silu_ref, x = refs
    gather_rows(rows, rows[0].shape[0], x)
    step = 256
    for n in range(hidden_ref.shape[1] // step):
        at = slice(n * step, (n + 1) * step)
        gate_pre = summed([dot(x[j], weight[0, :, at]) for j, weight in enumerate(weights)])
        up_pre = summed([dot(x[j], weight[1, :, at]) for j, weight in enumerate(weights)])
        sig = 1.0 / (1.0 + jnp.exp(-gate_pre))
        silu = gate_pre * sig
        hidden_ref[:, at] = (silu * up_pre).astype(BF)
        slope_ref[:, at] = up_pre * sig * (1.0 + gate_pre * (1.0 - sig))
        silu_ref[:, at] = silu


def out_kernel(pieces, hidden_ref, *refs):
    weights, outs = refs[:pieces], refs[pieces:]
    slots = outs[0].shape[0]
    for j, weight in enumerate(weights):
        part = dot_t(hidden_ref[...], weight[2]).astype(BF)
        for k, out in enumerate(outs):
            out[:, quarter(j, weight.shape[1])] = part[k * slots : (k + 1) * slots]


def backward_kernel(rows_count, pieces, slots, *refs):
    rows, weights, refs = refs[:rows_count], refs[rows_count : rows_count + pieces], refs[rows_count + pieces :]
    slope_ref, silu_ref, refs = refs[0], refs[1], refs[2:]
    outs, (x, gate_grad, up_grad) = refs[:-3], refs[-3:]
    gather_rows(rows, slots, x)
    step = 256
    for n in range(gate_grad.shape[1] // step):
        at = slice(n * step, (n + 1) * step)
        hidden_grad = summed([dot(x[j], weight[2, :, at]) for j, weight in enumerate(weights)])
        gate_grad[:, at] = (hidden_grad * slope_ref[:, at]).astype(BF)
        up_grad[:, at] = (hidden_grad * silu_ref[:, at]).astype(BF)
    for j, weight in enumerate(weights):
        part = dot_t(gate_grad[...], weight[0]) + dot_t(up_grad[...], weight[1])
        part = part.astype(BF)
        for k, out in enumerate(outs):
            out[:, quarter(j, weight.shape[1])] = part[k * slots : (k + 1) * slots]


def mixed(ids_ref, weight_ref, backs, at, cache):
    if not cache:
        first, second, slot = routing(ids_ref[0, 0:1], ids_ref[0, 1:2], lax.axis_index("expert"))
        slots = backs[0].shape[0]
        gates = [column(weight_ref[0, j : j + 1]) for j in range(2)]
        for k in range(len(backs)):
            place = placing(slot, k, slots)[:, :slots].astype(BF)
            weight = jnp.where(first == k, gates[0], 0.0) + jnp.where(second == k, gates[1], 0.0)
            cache.append((place, weight))
    total = None
    for back, (place, weight) in zip(backs, cache):
        term = weight * dot(place, back[:, at])
        total = term if total is None else total + term
    return total


def layer_kernel(ids_ref, weight_ref, in_ref, att_ref, *refs):
    backs, out_ref = refs[:-1], refs[-1]
    step, cache = 512, []
    for n in range(in_ref.shape[2] // step):
        at = slice(n * step, (n + 1) * step)
        resid = in_ref[0, :, at].astype(F32) + att_ref[:, at].astype(F32)
        out_ref[0, :, at] = (resid + mixed(ids_ref, weight_ref, backs, at, cache)).astype(BF)


def grad_kernel(ids_ref, weight_ref, in_ref, att_ref, gain_ref, up_ref, *refs):
    backs, out_ref, gained_ref = refs[:-2], refs[-2], refs[-1]
    tok, width = in_ref.shape[1], in_ref.shape[2]
    step, cache = 512, []
    squares = jnp.zeros((tok, 1), F32)
    cross = jnp.zeros((tok, 1), F32)
    for n in range(width // step):
        at = slice(n * step, (n + 1) * step)
        resid = in_ref[0, :, at].astype(F32) + att_ref[:, at].astype(F32)
        gained = gain_ref[:, at] * mixed(ids_ref, weight_ref, backs, at, cache)
        gained_ref[:, at] = gained
        squares = squares + (resid * resid).sum(axis=1, keepdims=True)
        cross = cross + (resid * gained).sum(axis=1, keepdims=True)
    inv_rms = lax.rsqrt(squares / width + 1e-06)
    pull = inv_rms * inv_rms * inv_rms * (cross / width)
    for n in range(width // step):
        at = slice(n * step, (n + 1) * step)
        resid = in_ref[0, :, at].astype(F32) + att_ref[:, at].astype(F32)
        out_ref[0, :, at] = (
            up_ref[0, :, at].astype(F32) + inv_rms * gained_ref[:, at] - resid * pull
        ).astype(BF)


def shards(
    inputs, queries, keys, values, doc_ids, norm_gain, expert_ids, gate_weights, w_gate, w_up, w_down, out_grad
):
    tok, width = inputs.shape[1], inputs.shape[2]
    hidden_count = w_gate.shape[2]
    peers = lax.axis_size("expert")
    slots = 5 * tok // (2 * peers)
    slots = -(-slots // 16) * 16
    pieces = lax.axis_size("fsdp") * lax.axis_size("ctx")
    total = peers * slots
    slab = jax.ShapeDtypeStruct((slots, width), BF)
    slabs = [slab] * peers
    gain = norm_gain.reshape(1, width)
    ids, gates = jnp.swapaxes(expert_ids, 1, 2), jnp.swapaxes(gate_weights, 1, 2)


    def call(kernel, name, out_shape, count, scratch=(), mib=24):
        return pl.pallas_call(
            kernel,
            out_shape=out_shape,
            in_specs=[VM] * count,
            out_specs=[VM] * len(out_shape) if isinstance(out_shape, list) else VM,
            scratch_shapes=list(scratch),
            compiler_params=params(mib),
            name=name,
        )

    def exchanged(blocks):
        return [block if k == 0 else swapped(block, "expert", k) for k, block in enumerate(blocks)]

    def over_core(block):
        return swapped(block, "ctx", 1)

    def over_x(block):
        return [swapped(block, "fsdp", dx) for dx in range(1, lax.axis_size("fsdp"))]

    both, own_weights, *sent_grads = pl.pallas_call(
        lambda *refs: prepare_kernel(slots, *refs),
        out_shape=[
            jax.ShapeDtypeStruct((2, tok, width), BF),
            jax.ShapeDtypeStruct((3, w_gate.shape[1], hidden_count), BF),
        ]
        + slabs,
        in_specs=[VM] + [pl.BlockSpec(memory_space=pl.ANY)] * 6,
        out_specs=[pl.BlockSpec(memory_space=pl.ANY)] * 2 + [VM] * peers,
        scratch_shapes=[
            pltpu.VMEM((2, tok, width), BF),
            pltpu.VMEM((3, w_gate.shape[1], hidden_count), BF),
            pltpu.VMEM((tok, width), BF),
            pltpu.VMEM(w_down.shape[1:], BF),
            pltpu.SemaphoreType.DMA((11,)),
        ],
        compiler_params=params(56),
        name="prepare",
    )(ids, keys, values, out_grad, w_gate, w_up, w_down)
    previous = shifted(both, ("expert", "ctx"), 1)
    grads = exchanged([after(block, previous) for block in sent_grads[:-1]])
    weights_x = over_x(own_weights)

    parts = 4
    cut = width // parts

    def by_part(*dims):
        return pl.BlockSpec((*dims, cut), lambda n: (0,) * len(dims) + (n,))

    def fixed(*dims):
        return pl.BlockSpec(dims, lambda n: (0,) * len(dims))

    attended, *sent_rows = pl.pallas_call(
        lambda *refs: attend_kernel(slots, *refs),
        out_shape=[jax.ShapeDtypeStruct((tok, width), BF)] + slabs,
        grid=(parts,),
        in_specs=[by_part(1, tok)] * 3
        + [by_part(2, tok), fixed(*doc_ids.shape), by_part(1, tok), fixed(1, width), fixed(*ids.shape)],
        out_specs=[by_part(tok)] + [fixed(slots, width)] * peers,
        scratch_shapes=[pltpu.VMEM((parts, tok, cut), F32), pltpu.VMEM((tok, HD), F32)],
        compiler_params=params(16),
        name="attend",
    )(queries, keys, values, previous, doc_ids, inputs, gain, ids)
    rows = exchanged([after(block, grads[-1]) for block in sent_rows])

    weights = [own_weights, over_core(after(own_weights, attended))]
    for block in weights_x:
        weights += [block, over_core(after(block, *rows[1:]))]
    grads.append(swapped(after(sent_grads[-1], *rows[2:]), "expert", peers - 1))

    wide = jax.ShapeDtypeStruct((total, hidden_count), F32)
    x_scratch = pltpu.VMEM((pieces, total, w_gate.shape[1]), BF)
    hidden, slope, silu = call(
        lambda *refs: hidden_kernel(peers, pieces, *refs),
        "hidden",
        [jax.ShapeDtypeStruct((total, hidden_count), BF), wide, wide],
        peers + pieces,
        [x_scratch],
    )(*rows, *weights)
    served_out = call(lambda *refs: out_kernel(pieces, *refs), "served", slabs, 1 + pieces)(hidden, *weights)
    back_out = exchanged(served_out)

    served_grad = call(
        lambda *refs: backward_kernel(len(grads), pieces, slots, *refs),
        "backward",
        slabs,
        len(grads) + pieces + 2,
        [x_scratch] + [pltpu.VMEM((total, hidden_count), BF)] * 2,
    )(*grads, *weights, slope, silu)
    back_grad = exchanged(served_grad)

    out_block = jax.ShapeDtypeStruct(inputs.shape, BF)
    layer_out = pl.pallas_call(
        layer_kernel,
        out_shape=out_block,
        in_specs=[VM] * (4 + peers),
        out_specs=VM,
        compiler_params=params(32),
        name="layer",
    )(ids, gates, inputs, attended, *back_out)
    input_grad = pl.pallas_call(
        grad_kernel,
        out_shape=out_block,
        in_specs=[VM] * (6 + peers),
        out_specs=VM,
        scratch_shapes=[pltpu.VMEM((tok, width), F32)],
        compiler_params=params(32),
        name="grad",
    )(ids, gates, inputs, after(attended, layer_out), gain, out_grad, *back_grad)
    return layer_out, input_grad


def solution(mesh):
    rows = P(("groups", "fsdp"), ("expert", "ctx"), None)
    in_specs = (
        rows,
        rows,
        rows,
        rows,
        P(("groups", "fsdp"), None),
        P(),
        rows,
        rows,
        P("expert", ("fsdp", "ctx"), None),
        P("expert", ("fsdp", "ctx"), None),
        P("expert", None, ("fsdp", "ctx")),
        rows,
    )
    return jax.shard_map(shards, mesh=mesh, in_specs=in_specs, out_specs=(rows, rows), check_vma=False)
```

time: 150 us -> 145 us (0.967)
  local copies, waits for them, and re-layouts: 6.61 us -> 0.06 us
  waiting for transfers between devices: 92.3 us -> 96.4 us
  Pallas kernels: 26 us -> 23.5 us
    pallas_call x2 -> x3, Pallas kernels: 14.1 us -> 6.74 us  [the longest x1 3.23 us: shards(): call(lambda *refs: backward_kernel(len(grads), pieces, slots, *refs), 'ba...]
    unnamed x34 -> x26, local copies, waits for them, and re-layouts: 6.61 us -> 0.06 us
    pallas_call x1, Pallas kernels: 1.44 us -> 5.09 us  [shards(): pl.pallas_call(lambda *refs: prepare_kernel(slots, *refs), out_shape=[jax...]
    ppermute x2 -> x1, starting transfers between devices: 5.5 us -> 2.04 us  [shifted(): return lax.ppermute(block, axis, route)]
    ppermute x15, waiting for transfers between devices: 78.9 us -> 82 us  [swapped(): return lax.ppermute(block, axis, [(i, i ^ distance) for i in range(count)])]
    ppermute x15, starting transfers between devices: 19 us -> 21.1 us  [swapped(): return lax.ppermute(block, axis, [(i, i ^ distance) for i in range(count)])]
    ppermute x2 -> x1, waiting for transfers between devices: 13.4 us -> 14.4 us  [shifted(): return lax.ppermute(block, axis, route)]
  transfers between devices with their start and end apart: 17 -> 16, of which waited for: 10 -> 11; matrix products, arithmetic and copies ran while one was open for 0% -> 0% of each run, Pallas kernels for 15% -> 11%
where the time goes in v4:
time: 145 us; the launch traced here: 144 us
  waiting for transfers between devices  96.4 us (66%)
  Pallas kernels  23.5 us (16%)
  starting transfers between devices  23.1 us (16%)
    ppermute x15, waiting for transfers between devices, swapped(): return lax.ppermute(block, axis, [(i, i ^ distance) for i in range(count)])  82 us
    ppermute x15, starting transfers between devices, swapped(): return lax.ppermute(block, axis, [(i, i ^ distance) for i in range(count)])  21.1 us
    ppermute x1, waiting for transfers between devices, shifted(): return lax.ppermute(block, axis, route)  14.4 us
    pallas_call x1, Pallas kernels, shards(): pl.pallas_call(lambda *refs: attend_kernel(slots, *refs), out_shape=[jax....  7.47 us
    pallas_call x1, Pallas kernels, shards(): pl.pallas_call(lambda *refs: prepare_kernel(slots, *refs), out_shape=[jax...  5.09 us
    pallas_call x1, Pallas kernels, shards(): call(lambda *refs: backward_kernel(len(grads), pieces, slots, *refs), 'ba...  3.23 us
  transfers between devices with their start and end apart: 16, of which 11 were waited for; matrix products, arithmetic and copies ran while one was open for 0% of the time, Pallas kernels for 11%

profile of v4, /device:TPU:10, one launch (start us, length us, event | category | flops | bytes accessed | tf_op | source)
XLA Modules:
  0.0 143.9 jit_solution(911623391408647675)
XLA Ops:
  0.7 5.1 %prepare.1 = (bf16[2,128,2048]{2,1,0:T(8,128)(2,1)}, bf16[3,512,768]{2,1,0:T(8,128)(2,1)}, bf16[80,2048]{1,0:T(8,128)(2,1)}, bf16[80,2048]{1,0:T(8,128)(2,1)}, b...) custom-call(s32[1,2,128]{2,1,0:T(2,128)} %bitcast.5, bf16[1,128,2048]{2,1,0:T(8,128)(2,1)} %refs_1_.3, ...), custom_call_target="tpu_custom_call" | custom-call | tf_op jit(solution)/shard_map/prepare/pallas_call | solution.py:316
  6.4 2.0 %collective-permute-start = (bf16[2,128,2048]{2,1,0:T(8,128)(2,1)}, bf16[2,128,2048]{2,1,0:T(8,128)(2,1)S(1)}, u32[]{:S(2)}, u32[]{:S(2)}) collective-permute-start(bf16[2,128,2048]{2,1,0:T(8,128)(2,1)} %get-tuple-element.35), channel_id=1, source_target_pairs={{0,1},{1,4},{4,5},{5,8},{8,9},{9,12},{12,13},{2,3},{3,6},{6,7},{7,... | collective-permute-start | bytes 3145736 | tf_op jit(solution)/shard_map/ppermute | solution.py:28
  8.5 14.4 %collective-permute-done.refs_3_ = bf16[2,128,2048]{2,1,0:T(8,128)(2,1)S(1)} collective-permute-done((bf16[2,128,2048]{2,1,0:T(8,128)(2,1)}, bf16[2,128,2048]{2,1,0:T(8,128)(2,1)S(1)}, u32[]{:S(2)}, u32[]{:S(2)}) %collective-permute-start) | collective-permute-done | bytes 1048608 | tf_op jit(solution)/shard_map/ppermute | solution.py:28
  22.9 2.6 %collective-permute-start.1 = (bf16[80,2048]{1,0:T(8,128)(2,1)}, bf16[80,2048]{1,0:T(8,128)(2,1)S(1)}, u32[]{:S(2)}, u32[]{:S(2)}) collective-permute-start(bf16[80,2048]{1,0:T(8,128)(2,1)} %get-tuple-element.39), channel_id=1, source_target_pairs={{0,8},{4,12},{8,0},{12,4},{1,9},{5,13},{9,1},{13,5},{2,10},{6,14},... | collective-permute-start | bytes 983048 | tf_op jit(solution)/shard_map/ppermute | solution.py:22
  25.5 7.5 %attend.1 = (bf16[128,2048]{1,0:T(8,128)(2,1)S(1)}, bf16[80,2048]{1,0:T(8,128)(2,1)S(1)}, bf16[80,2048]{1,0:T(8,128)(2,1)S(1)}, bf16[80,2048]{1,0:T(8,128)(2,1)S(1)}, bf16[80,2048]{1,0:T(8,128)(2,1)S(1)}) custom-call(bf16[1,128,2048]{2,1,0:T(8,128)(2,1)S(1)} %copy-done.5, bf16[1,128,2048]{2,1,0:T(8,128)(2,1)S(1)} %copy-done.2, ...), custom_call_target="tpu_custom_call" | custom-call | tf_op jit(solution)/shard_map/attend/pallas_call | solution.py:348
  33.0 4.0 %collective-permute-done.1.refs_2_ = bf16[80,2048]{1,0:T(8,128)(2,1)S(1)} collective-permute-done((bf16[80,2048]{1,0:T(8,128)(2,1)}, bf16[80,2048]{1,0:T(8,128)(2,1)S(1)}, u32[]{:S(2)}, u32[]{:S(2)}) %collective-permute-start.1) | collective-permute-done | bytes 327712 | tf_op jit(solution)/shard_map/ppermute | solution.py:22
  37.0 2.1 %collective-permute-start.4 = (bf16[80,2048]{1,0:T(8,128)(2,1)S(1)}, bf16[80,2048]{1,0:T(8,128)(2,1)S(1)}, u32[]{:S(2)}, u32[]{:S(2)}) collective-permute-start(bf16[80,2048]{1,0:T(8,128)(2,1)S(1)} %get-tuple-element.46), channel_id=1, source_target_pairs={{0,12},{4,8},{8,4},{12,0},{1,13},{5,9},{9,5},{13,1},{2,14},{6,10},... | collective-permute-start | bytes 983048 | tf_op jit(solution)/shard_map/ppermute | solution.py:22
  39.1 4.2 %collective-permute-start.3 = (bf16[80,2048]{1,0:T(8,128)(2,1)S(1)}, bf16[80,2048]{1,0:T(8,128)(2,1)S(1)}, u32[]{:S(2)}, u32[]{:S(2)}) collective-permute-start(bf16[80,2048]{1,0:T(8,128)(2,1)S(1)} %get-tuple-element.44), channel_id=1, source_target_pairs={{0,8},{4,12},{8,0},{12,4},{1,9},{5,13},{9,1},{13,5},{2,10},{6,14},... | collective-permute-start | bytes 983048 | tf_op jit(solution)/shard_map/ppermute | solution.py:22
  43.2 18.5 %collective-permute-done.4.refs_3_ = bf16[80,2048]{1,0:T(8,128)(2,1)S(1)} collective-permute-done((bf16[80,2048]{1,0:T(8,128)(2,1)S(1)}, bf16[80,2048]{1,0:T(8,128)(2,1)S(1)}, u32[]{:S(2)}, u32[]{:S(2)}) %collective-permute-start.4) | collective-permute-done | bytes 327712 | tf_op jit(solution)/shard_map/ppermute | solution.py:22
  61.7 4.0 %collective-permute-done.3.refs_2_ = bf16[80,2048]{1,0:T(8,128)(2,1)S(1)} collective-permute-done((bf16[80,2048]{1,0:T(8,128)(2,1)S(1)}, bf16[80,2048]{1,0:T(8,128)(2,1)S(1)}, u32[]{:S(2)}, u32[]{:S(2)}) %collective-permute-start.3) | collective-permute-done | bytes 327712 | tf_op jit(solution)/shard_map/ppermute | solution.py:22
  65.8 2.8 %collective-permute-start.11 = (bf16[80,2048]{1,0:T(8,128)(2,1)S(1)}, bf16[80,2048]{1,0:T(8,128)(2,1)S(1)}, u32[]{:S(2)}, u32[]{:S(2)}) collective-permute-start(bf16[80,2048]{1,0:T(8,128)(2,1)S(1)} %copy-done.12), channel_id=1, source_target_pairs={{0,4},{4,0},{8,12},{12,8},{1,5},{5,1},{9,13},{13,9},{2,6},{6,2},{1... | collective-permute-start | bytes 983048 | tf_op jit(solution)/shard_map/ppermute | solution.py:22
  70.3 2.3 %hidden.1 = (bf16[320,768]{1,0:T(8,128)(2,1)S(1)}, f32[320,768]{1,0:T(8,128)S(1)}, f32[320,768]{1,0:T(8,128)S(1)}) custom-call(bf16[80,2048]{1,0:T(8,128)(2,1)S(1)} %get-tuple-element.40.refs_0_, bf16[80,2048]{1,0:T(8,128)(2,1)S(1)} %collective-permute-done.2.refs_1_, bf16[80,2048]{1,0:T(8,128)(2,1)S(1)} %collective-permute-done.3.refs_2_, ...), custom_call_target="tpu_custom_call" | custom-call | tf_op jit(solution)/shard_map/hidden/pallas_call | solution.py:368
  72.6 1.2 served.1
  73.8 2.8 %collective-permute-start.8 = (bf16[80,2048]{1,0:T(8,128)(2,1)S(1)}, bf16[80,2048]{1,0:T(8,128)(2,1)S(1)}, u32[]{:S(2)}, u32[]{:S(2)}) collective-permute-start(bf16[80,2048]{1,0:T(8,128)(2,1)S(1)} %get-tuple-element.52), channel_id=1, source_target_pairs={{0,4},{4,0},{8,12},{12,8},{1,5},{5,1},{9,13},{13,9},{2,6},{6,2},{1... | collective-permute-start | bytes 983048 | tf_op jit(solution)/shard_map/ppermute | solution.py:22
  78.2 7.9 %collective-permute-done.12.refs_3_ = bf16[80,2048]{1,0:T(8,128)(2,1)S(1)} collective-permute-done((bf16[80,2048]{1,0:T(8,128)(2,1)S(1)}, bf16[80,2048]{1,0:T(8,128)(2,1)S(1)}, u32[]{:S(2)}, u32[]{:S(2)}) %collective-permute-start.12) | collective-permute-done | bytes 327712 | tf_op jit(solution)/shard_map/ppermute | solution.py:22
  86.1 3.2 %backward.1 = (bf16[80,2048]{1,0:T(8,128)(2,1)S(1)}, bf16[80,2048]{1,0:T(8,128)(2,1)S(1)}, bf16[80,2048]{1,0:T(8,128)(2,1)S(1)}, bf16[80,2048]{1,0:T(8,128)(2,1)S(1)}) custom-call(bf16[80,2048]{1,0:T(8,128)(2,1)S(1)} %copy-done.6, bf16[80,2048]{1,0:T(8,128)(2,1)S(1)} %collective-permute-done.11.refs_1_, bf16[80,2048]{1,0:T(8,128)(2,1)S(1)} %collective-permute-done.1.refs_2_, ...), custom_call_target="tpu_custom_call" | custom-call | tf_op jit(solution)/shard_map/backward/pallas_call | solution.py:378
  89.7 2.5 %collective-permute-start.14 = (bf16[80,2048]{1,0:T(8,128)(2,1)S(1)}, bf16[80,2048]{1,0:T(8,128)(2,1)S(1)}, u32[]{:S(2)}, u32[]{:S(2)}) collective-permute-start(bf16[80,2048]{1,0:T(8,128)(2,1)S(1)} %get-tuple-element.66), channel_id=1, source_target_pairs={{0,8},{4,12},{8,0},{12,4},{1,9},{5,13},{9,1},{13,5},{2,10},{6,14},... | collective-permute-start | bytes 983048 | tf_op jit(solution)/shard_map/ppermute | solution.py:22
  92.1 4.9 %collective-permute-done.8.refs_1_ = bf16[80,2048]{1,0:T(8,128)(2,1)S(1)} collective-permute-done((bf16[80,2048]{1,0:T(8,128)(2,1)S(1)}, bf16[80,2048]{1,0:T(8,128)(2,1)S(1)}, u32[]{:S(2)}, u32[]{:S(2)}) %collective-permute-start.8) | collective-permute-done | bytes 327712 | tf_op jit(solution)/shard_map/ppermute | solution.py:22
  97.5 8.5 %collective-permute-done.9.refs_2_ = bf16[80,2048]{1,0:T(8,128)(2,1)S(1)} collective-permute-done((bf16[80,2048]{1,0:T(8,128)(2,1)S(1)}, bf16[80,2048]{1,0:T(8,128)(2,1)S(1)}, u32[]{:S(2)}, u32[]{:S(2)}) %collective-permute-start.9) | collective-permute-done | bytes 327712 | tf_op jit(solution)/shard_map/ppermute | solution.py:22
  106.0 22.2 %collective-permute-done.10.refs_3_ = bf16[80,2048]{1,0:T(8,128)(2,1)S(1)} collective-permute-done((bf16[80,2048]{1,0:T(8,128)(2,1)S(1)}, bf16[80,2048]{1,0:T(8,128)(2,1)S(1)}, u32[]{:S(2)}, u32[]{:S(2)}) %collective-permute-start.10) | collective-permute-done | bytes 327712 | tf_op jit(solution)/shard_map/ppermute | solution.py:22
  128.2 1.9 %layer.1 = bf16[1,128,2048]{2,1,0:T(8,128)(2,1)} custom-call(s32[1,2,128]{2,1,0:T(2,128)S(1)} %bitcast.7, f32[1,2,128]{2,1,0:T(2,128)S(1)} %bitcast.9, bf16[1,128,2048]{2,1,0:T(8,128)(2,1)S(1)} %copy-done.1, bf16[128,2048]{1,0:T(8,128)(2,1)S(1)} %get-tuple-element.55.att_ref, bf16[80,2048]{1,0:T(8,128)(2,1)S(1)} %get-tuple-element.51.refs_0_, ...), custom_call_target="tpu_custom_call" | custom-call | tf_op jit(solution)/shard_map/layer/pallas_call | solution.py:388
  130.1 3.9 %collective-permute-done.14.refs_2_ = bf16[80,2048]{1,0:T(8,128)(2,1)S(1)} collective-permute-done((bf16[80,2048]{1,0:T(8,128)(2,1)S(1)}, bf16[80,2048]{1,0:T(8,128)(2,1)S(1)}, u32[]{:S(2)}, u32[]{:S(2)}) %collective-permute-start.14) | collective-permute-done | bytes 327712 | tf_op jit(solution)/shard_map/ppermute | solution.py:22
  134.1 7.5 %collective-permute-done.15.refs_3_ = bf16[80,2048]{1,0:T(8,128)(2,1)S(1)} collective-permute-done((bf16[80,2048]{1,0:T(8,128)(2,1)S(1)}, bf16[80,2048]{1,0:T(8,128)(2,1)S(1)}, u32[]{:S(2)}, u32[]{:S(2)}) %collective-permute-start.15) | collective-permute-done | bytes 327712 | tf_op jit(solution)/shard_map/ppermute | solution.py:22
  141.6 2.3 %grad.1 = bf16[1,128,2048]{2,1,0:T(8,128)(2,1)} custom-call(s32[1,2,128]{2,1,0:T(2,128)S(1)} %bitcast.8, f32[1,2,128]{2,1,0:T(2,128)S(1)} %bitcast.10, bf16[1,128,2048]{2,1,0:T(8,128)(2,1)S(1)} %copy-done.1, bf16[128,2048]{1,0:T(8,128)(2,1)S(1)} %get-tuple-element.55.att_ref, f32[1,2048]{1,0:T(1,128)S(1)} %bitcast.4, bf16[1,128,2048]{2,1,0:T(8,128)(2,1)S(1)} %copy-done.4, ...), custom_call_target="tpu_custom_call" | custom-call | tf_op jit(solution)/shard_map/grad/pallas_call | solution.py:396
  (41 shorter events, 4.7 us)
Async XLA Ops:
  0.6 24.8 %copy-start.3 = (bf16[1,128,2048]{2,1,0:T(8,128)(2,1)S(1)}, bf16[1,128,2048]{2,1,0:T(8,128)(2,1)}, u32[]{:S(2)}) copy-start(bf16[1,128,2048]{2,1,0:T(8,128)(2,1)} %refs_2_.3) | copy-start | bytes 1572868
  0.6 24.8 %copy-start.2 = (bf16[1,128,2048]{2,1,0:T(8,128)(2,1)S(1)}, bf16[1,128,2048]{2,1,0:T(8,128)(2,1)}, u32[]{:S(2)}) copy-start(bf16[1,128,2048]{2,1,0:T(8,128)(2,1)} %refs_1_.3) | copy-start | bytes 1572868
  0.7 24.8 %copy-start.8 = (s32[1,128,2]{1,2,0:T(2,128)S(1)}, s32[1,128,2]{1,2,0:T(2,128)}, u32[]{:S(2)}) copy-start(s32[1,128,2]{1,2,0:T(2,128)} %param.18) | copy-start | bytes 3076
  5.8 37.4 %copy-start = (bf16[3,512,768]{2,1,0:T(8,128)(2,1)S(1)}, bf16[3,512,768]{2,1,0:T(8,128)(2,1)}, u32[]{:S(2)}) copy-start(bf16[3,512,768]{2,1,0:T(8,128)(2,1)} %get-tuple-element.48.refs_4_.refs_1_) | copy-start | bytes 7077892
  5.8 59.9 %copy-start.12 = (bf16[80,2048]{1,0:T(8,128)(2,1)S(1)}, bf16[80,2048]{1,0:T(8,128)(2,1)}, u32[]{:S(2)}) copy-start(bf16[80,2048]{1,0:T(8,128)(2,1)} %get-tuple-element.59) | copy-start | bytes 983044
  5.8 62.8 %copy-start.11 = (bf16[80,2048]{1,0:T(8,128)(2,1)S(1)}, bf16[80,2048]{1,0:T(8,128)(2,1)}, u32[]{:S(2)}) copy-start(bf16[80,2048]{1,0:T(8,128)(2,1)} %get-tuple-element.61) | copy-start | bytes 983044
  5.8 59.9 %collective-permute-start.6 = (bf16[3,512,768]{2,1,0:T(8,128)(2,1)}, bf16[3,512,768]{2,1,0:T(8,128)(2,1)S(1)}, u32[]{:S(2)}, u32[]{:S(2)}) collective-permute-start(bf16[3,512,768]{2,1,0:T(8,128)(2,1)} %get-tuple-element.48.refs_4_.refs_1_), channel_id=1, source_target_pairs={{0,2},{2,0},{1,3},{3,1},{4,6},{6,4},{5,7},{7,5},{8,10},{10,8},{9,1... | collective-permute-start | bytes 7077896 | tf_op jit(solution)/shard_map/ppermute | solution.py:22
  6.4 16.4 %collective-permute-start = (bf16[2,128,2048]{2,1,0:T(8,128)(2,1)}, bf16[2,128,2048]{2,1,0:T(8,128)(2,1)S(1)}, u32[]{:S(2)}, u32[]{:S(2)}) collective-permute-start(bf16[2,128,2048]{2,1,0:T(8,128)(2,1)} %get-tuple-element.35), channel_id=1, source_target_pairs={{0,1},{1,4},{4,5},{5,8},{8,9},{9,12},{12,13},{2,3},{3,6},{6,7},{7,... | collective-permute-start | bytes 3145736 | tf_op jit(solution)/shard_map/ppermute | solution.py:28
  22.9 14.1 %collective-permute-start.1 = (bf16[80,2048]{1,0:T(8,128)(2,1)}, bf16[80,2048]{1,0:T(8,128)(2,1)S(1)}, u32[]{:S(2)}, u32[]{:S(2)}) collective-permute-start(bf16[80,2048]{1,0:T(8,128)(2,1)} %get-tuple-element.39), channel_id=1, source_target_pairs={{0,8},{4,12},{8,0},{12,4},{1,9},{5,13},{9,1},{13,5},{2,10},{6,14},... | collective-permute-start | bytes 983048 | tf_op jit(solution)/shard_map/ppermute | solution.py:22
  37.0 24.8 %collective-permute-start.4 = (bf16[80,2048]{1,0:T(8,128)(2,1)S(1)}, bf16[80,2048]{1,0:T(8,128)(2,1)S(1)}, u32[]{:S(2)}, u32[]{:S(2)}) collective-permute-start(bf16[80,2048]{1,0:T(8,128)(2,1)S(1)} %get-tuple-element.46), channel_id=1, source_target_pairs={{0,12},{4,8},{8,4},{12,0},{1,13},{5,9},{9,5},{13,1},{2,14},{6,10},... | collective-permute-start | bytes 983048 | tf_op jit(solution)/shard_map/ppermute | solution.py:22
  39.1 26.7 %collective-permute-start.3 = (bf16[80,2048]{1,0:T(8,128)(2,1)S(1)}, bf16[80,2048]{1,0:T(8,128)(2,1)S(1)}, u32[]{:S(2)}, u32[]{:S(2)}) collective-permute-start(bf16[80,2048]{1,0:T(8,128)(2,1)S(1)} %get-tuple-element.44), channel_id=1, source_target_pairs={{0,8},{4,12},{8,0},{12,4},{1,9},{5,13},{9,1},{13,5},{2,10},{6,14},... | collective-permute-start | bytes 983048 | tf_op jit(solution)/shard_map/ppermute | solution.py:22
  43.2 22.5 %collective-permute-start.2 = (bf16[80,2048]{1,0:T(8,128)(2,1)S(1)}, bf16[80,2048]{1,0:T(8,128)(2,1)S(1)}, u32[]{:S(2)}, u32[]{:S(2)}) collective-permute-start(bf16[80,2048]{1,0:T(8,128)(2,1)S(1)} %get-tuple-element.42), channel_id=1, source_target_pairs={{0,4},{4,0},{8,12},{12,8},{1,5},{5,1},{9,13},{13,9},{2,6},{6,2},{1... | collective-permute-start | bytes 983048 | tf_op jit(solution)/shard_map/ppermute | solution.py:22
  43.2 26.5 %collective-permute-start.5 = (bf16[3,512,768]{2,1,0:T(8,128)(2,1)S(1)}, bf16[3,512,768]{2,1,0:T(8,128)(2,1)S(1)}, u32[]{:S(2)}, u32[]{:S(2)}) collective-permute-start(bf16[3,512,768]{2,1,0:T(8,128)(2,1)S(1)} %copy-done), channel_id=1, source_target_pairs={{0,1},{1,0},{2,3},{3,2},{4,5},{5,4},{6,7},{7,6},{8,9},{9,8},{10,11... | collective-permute-start | bytes 7077896 | tf_op jit(solution)/shard_map/ppermute | solution.py:22
  65.8 4.5 %collective-permute-start.7 = (bf16[3,512,768]{2,1,0:T(8,128)(2,1)S(1)}, bf16[3,512,768]{2,1,0:T(8,128)(2,1)S(1)}, u32[]{:S(2)}, u32[]{:S(2)}) collective-permute-start(bf16[3,512,768]{2,1,0:T(8,128)(2,1)S(1)} %collective-permute-done.6.refs_6_.refs_3_), channel_id=1, source_target_pairs={{0,1},{1,0},{2,3},{3,2},{4,5},{5,4},{6,7},{7,6},{8,9},{9,8},{10,11... | collective-permute-start | bytes 7077896 | tf_op jit(solution)/shard_map/ppermute | solution.py:22
  65.8 12.4 %collective-permute-start.11 = (bf16[80,2048]{1,0:T(8,128)(2,1)S(1)}, bf16[80,2048]{1,0:T(8,128)(2,1)S(1)}, u32[]{:S(2)}, u32[]{:S(2)}) collective-permute-start(bf16[80,2048]{1,0:T(8,128)(2,1)S(1)} %copy-done.12), channel_id=1, source_target_pairs={{0,4},{4,0},{8,12},{12,8},{1,5},{5,1},{9,13},{13,9},{2,6},{6,2},{1... | collective-permute-start | bytes 983048 | tf_op jit(solution)/shard_map/ppermute | solution.py:22
  68.6 17.5 %collective-permute-start.12 = (bf16[80,2048]{1,0:T(8,128)(2,1)S(1)}, bf16[80,2048]{1,0:T(8,128)(2,1)S(1)}, u32[]{:S(2)}, u32[]{:S(2)}) collective-permute-start(bf16[80,2048]{1,0:T(8,128)(2,1)S(1)} %copy-done.11), channel_id=1, source_target_pairs={{0,12},{4,8},{8,4},{12,0},{1,13},{5,9},{9,5},{13,1},{2,14},{6,10},... | collective-permute-start | bytes 983048 | tf_op jit(solution)/shard_map/ppermute | solution.py:22
  73.8 23.3 %collective-permute-start.8 = (bf16[80,2048]{1,0:T(8,128)(2,1)S(1)}, bf16[80,2048]{1,0:T(8,128)(2,1)S(1)}, u32[]{:S(2)}, u32[]{:S(2)}) collective-permute-start(bf16[80,2048]{1,0:T(8,128)(2,1)S(1)} %get-tuple-element.52), channel_id=1, source_target_pairs={{0,4},{4,0},{8,12},{12,8},{1,5},{5,1},{9,13},{13,9},{2,6},{6,2},{1... | collective-permute-start | bytes 983048 | tf_op jit(solution)/shard_map/ppermute | solution.py:22
  76.6 29.4 %collective-permute-start.9 = (bf16[80,2048]{1,0:T(8,128)(2,1)S(1)}, bf16[80,2048]{1,0:T(8,128)(2,1)S(1)}, u32[]{:S(2)}, u32[]{:S(2)}) collective-permute-start(bf16[80,2048]{1,0:T(8,128)(2,1)S(1)} %get-tuple-element.53), channel_id=1, source_target_pairs={{0,8},{4,12},{8,0},{12,4},{1,9},{5,13},{9,1},{13,5},{2,10},{6,14},... | collective-permute-start | bytes 983048 | tf_op jit(solution)/shard_map/ppermute | solution.py:22
  77.4 50.9 %collective-permute-start.10 = (bf16[80,2048]{1,0:T(8,128)(2,1)S(1)}, bf16[80,2048]{1,0:T(8,128)(2,1)S(1)}, u32[]{:S(2)}, u32[]{:S(2)}) collective-permute-start(bf16[80,2048]{1,0:T(8,128)(2,1)S(1)} %get-tuple-element.54), channel_id=1, source_target_pairs={{0,12},{4,8},{8,4},{12,0},{1,13},{5,9},{9,5},{13,1},{2,14},{6,10},... | collective-permute-start | bytes 983048 | tf_op jit(solution)/shard_map/ppermute | solution.py:22
  86.1 42.2 %copy-start.9 = (f32[1,128,2]{1,2,0:T(2,128)S(1)}, f32[1,128,2]{1,2,0:T(2,128)}, u32[]{:S(2)}) copy-start(f32[1,128,2]{1,2,0:T(2,128)} %param.19) | copy-start | bytes 3076
  89.3 52.3 %copy-start.4 = (bf16[1,128,2048]{2,1,0:T(8,128)(2,1)S(1)}, bf16[1,128,2048]{2,1,0:T(8,128)(2,1)}, u32[]{:S(2)}) copy-start(bf16[1,128,2048]{2,1,0:T(8,128)(2,1)} %up_ref.1) | copy-start | bytes 1572868
  89.3 40.8 %collective-permute-start.13 = (bf16[80,2048]{1,0:T(8,128)(2,1)S(1)}, bf16[80,2048]{1,0:T(8,128)(2,1)S(1)}, u32[]{:S(2)}, u32[]{:S(2)}) collective-permute-start(bf16[80,2048]{1,0:T(8,128)(2,1)S(1)} %get-tuple-element.65), channel_id=1, source_target_pairs={{0,4},{4,0},{8,12},{12,8},{1,5},{5,1},{9,13},{13,9},{2,6},{6,2},{1... | collective-permute-start | bytes 983048 | tf_op jit(solution)/shard_map/ppermute | solution.py:22
  89.7 44.4 %collective-permute-start.14 = (bf16[80,2048]{1,0:T(8,128)(2,1)S(1)}, bf16[80,2048]{1,0:T(8,128)(2,1)S(1)}, u32[]{:S(2)}, u32[]{:S(2)}) collective-permute-start(bf16[80,2048]{1,0:T(8,128)(2,1)S(1)} %get-tuple-element.66), channel_id=1, source_target_pairs={{0,8},{4,12},{8,0},{12,4},{1,9},{5,13},{9,1},{13,5},{2,10},{6,14},... | collective-permute-start | bytes 983048 | tf_op jit(solution)/shard_map/ppermute | solution.py:22
  97.1 44.5 %collective-permute-start.15 = (bf16[80,2048]{1,0:T(8,128)(2,1)S(1)}, bf16[80,2048]{1,0:T(8,128)(2,1)S(1)}, u32[]{:S(2)}, u32[]{:S(2)}) collective-permute-start(bf16[80,2048]{1,0:T(8,128)(2,1)S(1)} %get-tuple-element.67), channel_id=1, source_target_pairs={{0,12},{4,8},{8,4},{12,0},{1,13},{5,9},{9,5},{13,1},{2,14},{6,10},... | collective-permute-start | bytes 983048 | tf_op jit(solution)/shard_map/ppermute | solution.py:22
  (5 other events, 112.7 us)

commit v5 on v4

--- a/solution.py
+++ b/solution.py
@@ -74,38 +74,28 @@
         out[...] = packed[k * slots : (k + 1) * slots]
 
 
-def prepare_kernel(slots, ids_ref, k_hbm, v_hbm, rows_hbm, g_hbm, u_hbm, d_hbm, both_hbm, weight_hbm, *refs):
-    out_refs, (both, weight, rows, down, sems) = refs[:-5], refs[-5:]
+def prepare_kernel(u_hbm, d_hbm, weight_hbm, weight, down, sems):
     pairs = [
-        (k_hbm.at[0], both.at[0]),
-        (v_hbm.at[0], both.at[1]),
         (d_hbm.at[0], down),
-        (g_hbm.at[0], weight.at[0]),
-        (u_hbm.at[0], weight.at[1]),
-        (rows_hbm.at[0], rows),
-        (both.at[0], both_hbm.at[0]),
-        (both.at[1], both_hbm.at[1]),
+        (u_hbm.at[0], weight.at[0]),
         (weight.at[0], weight_hbm.at[0]),
         (weight.at[1], weight_hbm.at[1]),
-        (weight.at[2], weight_hbm.at[2]),
     ]
     copies = [pltpu.make_async_copy(source, target, sems.at[n]) for n, (source, target) in enumerate(pairs)]
-    for copy in copies[:6]:
-        copy.start()
+    copies[0].start()
+    copies[1].start()
+    copies[1].wait()
+    copies[2].start()
+    copies[0].wait()
+    weight[1] = down[...].T
+    copies[3].start()
+    copies[2].wait()
+    copies[3].wait()
+
+
+def pack_kernel(slots, ids_ref, rows_ref, *out_refs):
     _, _, slot = routing(ids_ref[0, 0:1], ids_ref[0, 1:2], lax.axis_index("expert"))
-    for arrived, leaving in ((0, 6), (1, 7)):
-        copies[arrived].wait()
-        copies[leaving].start()
-    copies[2].wait()
-    weight[2] = down[...].T
-    copies[10].start()
-    for arrived, leaving in ((3, 8), (4, 9)):
-        copies[arrived].wait()
-        copies[leaving].start()
-    copies[5].wait()
-    pack(rows[...], slot, slots, out_refs)
-    for copy in copies[6:]:
-        copy.wait()
+    pack(rows_ref[0], slot, slots, out_refs)
 
 
 def attend_kernel(
@@ -187,14 +177,15 @@
 
 
 def hidden_kernel(count, pieces, *refs):
-    rows, weights, refs = refs[:count], refs[count : count + pieces], refs[count + pieces :]
+    rows, gates, refs = refs[:count], refs[count : count + pieces], refs[count + pieces :]
+    others, refs = refs[:pieces], refs[pieces:]
     hidden_ref, slope_ref, silu_ref, x = refs
     gather_rows(rows, rows[0].shape[0], x)
     step = 256
     for n in range(hidden_ref.shape[1] // step):
         at = slice(n * step, (n + 1) * step)
-        gate_pre = summed([dot(x[j], weight[0, :, at]) for j, weight in enumerate(weights)])
-        up_pre = summed([dot(x[j], weight[1, :, at]) for j, weight in enumerate(weights)])
+        gate_pre = summed([dot(x[j], gate[0, :, at]) for j, gate in enumerate(gates)])
+        up_pre = summed([dot(x[j], other[0, :, at]) for j, other in enumerate(others)])
         sig = 1.0 / (1.0 + jnp.exp(-gate_pre))
         silu = gate_pre * sig
         hidden_ref[:, at] = (silu * up_pre).astype(BF)
@@ -203,30 +194,30 @@
 
 
 def out_kernel(pieces, hidden_ref, *refs):
-    weights, outs = refs[:pieces], refs[pieces:]
+    others, outs = refs[:pieces], refs[pieces:]
     slots = outs[0].shape[0]
-    for j, weight in enumerate(weights):
-        part = dot_t(hidden_ref[...], weight[2]).astype(BF)
+    for j, other in enumerate(others):
+        part = dot_t(hidden_ref[...], other[1]).astype(BF)
         for k, out in enumerate(outs):
-            out[:, quarter(j, weight.shape[1])] = part[k * slots : (k + 1) * slots]
+            out[:, quarter(j, other.shape[1])] = part[k * slots : (k + 1) * slots]
 
 
 def backward_kernel(rows_count, pieces, slots, *refs):
-    rows, weights, refs = refs[:rows_count], refs[rows_count : rows_count + pieces], refs[rows_count + pieces :]
-    slope_ref, silu_ref, refs = refs[0], refs[1], refs[2:]
+    rows, gates, refs = refs[:rows_count], refs[rows_count : rows_count + pieces], refs[rows_count + pieces :]
+    others, slope_ref, silu_ref, refs = refs[:pieces], refs[pieces], refs[pieces + 1], refs[pieces + 2 :]
     outs, (x, gate_grad, up_grad) = refs[:-3], refs[-3:]
     gather_rows(rows, slots, x)
     step = 256
     for n in range(gate_grad.shape[1] // step):
         at = slice(n * step, (n + 1) * step)
-        hidden_grad = summed([dot(x[j], weight[2, :, at]) for j, weight in enumerate(weights)])
+        hidden_grad = summed([dot(x[j], other[1, :, at]) for j, other in enumerate(others)])
         gate_grad[:, at] = (hidden_grad * slope_ref[:, at]).astype(BF)
         up_grad[:, at] = (hidden_grad * silu_ref[:, at]).astype(BF)
-    for j, weight in enumerate(weights):
-        part = dot_t(gate_grad[...], weight[0]) + dot_t(up_grad[...], weight[1])
+    for j, (gate, other) in enumerate(zip(gates, others)):
+        part = dot_t(gate_grad[...], gate[0]) + dot_t(up_grad[...], other[0])
         part = part.astype(BF)
         for k, out in enumerate(outs):
-            out[:, quarter(j, weight.shape[1])] = part[k * slots : (k + 1) * slots]
+            out[:, quarter(j, gate.shape[1])] = part[k * slots : (k + 1) * slots]
 
 
 def mixed(ids_ref, weight_ref, backs, at, cache):
@@ -313,28 +304,26 @@
     def over_x(block):
         return [swapped(block, "fsdp", dx) for dx in range(1, lax.axis_size("fsdp"))]
 
-    both, own_weights, *sent_grads = pl.pallas_call(
-        lambda *refs: prepare_kernel(slots, *refs),
-        out_shape=[
-            jax.ShapeDtypeStruct((2, tok, width), BF),
-            jax.ShapeDtypeStruct((3, w_gate.shape[1], hidden_count), BF),
-        ]
-        + slabs,
-        in_specs=[VM] + [pl.BlockSpec(memory_space=pl.ANY)] * 6,
-        out_specs=[pl.BlockSpec(memory_space=pl.ANY)] * 2 + [VM] * peers,
+    both = jnp.concatenate([keys, values], 0)
+    previous = shifted(both, ("expert", "ctx"), 1)
+    own_others = pl.pallas_call(
+        prepare_kernel,
+        out_shape=jax.ShapeDtypeStruct((2, w_gate.shape[1], hidden_count), BF),
+        in_specs=[pl.BlockSpec(memory_space=pl.ANY)] * 2,
+        out_specs=pl.BlockSpec(memory_space=pl.ANY),
         scratch_shapes=[
-            pltpu.VMEM((2, tok, width), BF),
-            pltpu.VMEM((3, w_gate.shape[1], hidden_count), BF),
-            pltpu.VMEM((tok, width), BF),
+            pltpu.VMEM((2, w_gate.shape[1], hidden_count), BF),
             pltpu.VMEM(w_down.shape[1:], BF),
-            pltpu.SemaphoreType.DMA((11,)),
+            pltpu.SemaphoreType.DMA((4,)),
         ],
         compiler_params=params(56),
         name="prepare",
-    )(ids, keys, values, out_grad, w_gate, w_up, w_down)
-    previous = shifted(both, ("expert", "ctx"), 1)
-    grads = exchanged([after(block, previous) for block in sent_grads[:-1]])
-    weights_x = over_x(own_weights)
+    )(w_up, after(w_down, both))
+    sent_grads = call(lambda *refs: pack_kernel(slots, *refs), "pack_grad", slabs, 2)(ids, after(out_grad, own_others))
+    grads = [
+        block if k < 2 else swapped(after(block, previous), "expert", k) for k, block in enumerate(sent_grads[:-1])
+    ]
+    gates_x, others_x = over_x(w_gate), over_x(own_others)
 
     parts = 4
     cut = width // parts
@@ -358,9 +347,10 @@
     )(queries, keys, values, previous, doc_ids, inputs, gain, ids)
     rows = exchanged([after(block, grads[-1]) for block in sent_rows])
 
-    weights = [own_weights, over_core(after(own_weights, attended))]
-    for block in weights_x:
-        weights += [block, over_core(after(block, *rows[1:]))]
+    all_gates, all_others = [w_gate, over_core(after(w_gate, attended))], [own_others, over_core(after(own_others, attended))]
+    for gate, other in zip(gates_x, others_x):
+        all_gates += [gate, over_core(after(gate, *rows[1:]))]
+        all_others += [other, over_core(after(other, *rows[1:]))]
     grads.append(swapped(after(sent_grads[-1], *rows[2:]), "expert", peers - 1))
 
     wide = jax.ShapeDtypeStruct((total, hidden_count), F32)
@@ -369,19 +359,20 @@
         lambda *refs: hidden_kernel(peers, pieces, *refs),
         "hidden",
         [jax.ShapeDtypeStruct((total, hidden_count), BF), wide, wide],
-        peers + pieces,
+        peers + 2 * pieces,
         [x_scratch],
-    )(*rows, *weights)
-    served_out = call(lambda *refs: out_kernel(pieces, *refs), "served", slabs, 1 + pieces)(hidden, *weights)
+    )(*rows, *all_gates, *all_others)
+    grads[1] = swapped(after(grads[1], hidden), "expert", 1)
+    served_out = call(lambda *refs: out_kernel(pieces, *refs), "served", slabs, 1 + pieces)(hidden, *all_others)
     back_out = exchanged(served_out)
 
     served_grad = call(
         lambda *refs: backward_kernel(len(grads), pieces, slots, *refs),
         "backward",
         slabs,
-        len(grads) + pieces + 2,
+        len(grads) + 2 * pieces + 2,
         [x_scratch] + [pltpu.VMEM((total, hidden_count), BF)] * 2,
-    )(*grads, *weights, slope, silu)
+    )(*grads, *all_gates, *all_others, slope, silu)
     back_grad = exchanged(served_grad)
 
     out_block = jax.ShapeDtypeStruct(inputs.shape, BF)

time: 145 us -> 138 us (0.952)
  waiting for transfers between devices: 96.4 us -> 86.7 us
  starting transfers between devices: 23.1 us -> 26.2 us
  local copies, waits for them, and re-layouts: 0.06 us -> 2.22 us
  Pallas kernels: 23.5 us -> 21.9 us
    ppermute x15 -> x18, waiting for transfers between devices: 82 us -> 76.6 us  [swapped(): return lax.ppermute(block, axis, [(i, i ^ distance) for i in range(count)])]
    ppermute x1, waiting for transfers between devices: 14.4 us -> 10 us  [shifted(): return lax.ppermute(block, axis, route)]
    ppermute x15 -> x18, starting transfers between devices: 21.1 us -> 24.1 us  [swapped(): return lax.ppermute(block, axis, [(i, i ^ distance) for i in range(count)])]
    pallas_call x1 -> x2, Pallas kernels: 5.09 us -> 3.52 us  [the longest x1 2.59 us: shards(): pl.pallas_call(prepare_kernel, out_shape=jax.ShapeDtypeStruct((2, w_gate....]
  transfers between devices with their start and end apart: 16 -> 19, of which waited for: 11 -> 15; matrix products, arithmetic and copies ran while one was open for 0% -> 0% of each run, Pallas kernels for 11% -> 14%
where the time goes in v5:
time: 138 us
  waiting for transfers between devices  86.7 us (63%)
  starting transfers between devices  26.2 us (19%)
  Pallas kernels  21.9 us (16%)
  local copies, waits for them, and re-layouts  2.22 us (2%)
    ppermute x18, waiting for transfers between devices, swapped(): return lax.ppermute(block, axis, [(i, i ^ distance) for i in range(count)])  76.6 us
    ppermute x18, starting transfers between devices, swapped(): return lax.ppermute(block, axis, [(i, i ^ distance) for i in range(count)])  24.1 us
    ppermute x1, waiting for transfers between devices, shifted(): return lax.ppermute(block, axis, route)  10 us
    pallas_call x1, Pallas kernels, shards(): pl.pallas_call(lambda *refs: attend_kernel(slots, *refs), out_shape=[jax....  7.46 us
    pallas_call x1, Pallas kernels, shards(): call(lambda *refs: backward_kernel(len(grads), pieces, slots, *refs), 'ba...  3.23 us
  transfers between devices with their start and end apart: 19, of which 15 were waited for; matrix products, arithmetic and copies ran while one was open for 0% of the time, Pallas kernels for 14%

profile of v5, /device:TPU:10, one launch (start us, length us, event | category | flops | bytes accessed | tf_op | source)
XLA Modules:
  0.0 137.8 jit_solution(15869201208891334057)
XLA Ops:
  2.9 2.1 %collective-permute-start = (bf16[2,128,2048]{2,1,0:T(8,128)(2,1)S(1)}, bf16[2,128,2048]{2,1,0:T(8,128)(2,1)S(1)}, u32[]{:S(2)}, u32[]{:S(2)}) collective-permute-start(bf16[2,128,2048]{2,1,0:T(8,128)(2,1)S(1)} %constant_dynamic-update-slice_fusion), channel_id=1, source_target_pairs={{0,1},{1,4},{4,5},{5,8},{8,9},{9,12},{12,13},{2,3},{3,6},{6,7},{7,... | collective-permute-start | bytes 3145736 | tf_op jit(solution)/shard_map/ppermute | solution.py:28
  4.9 2.6 %prepare.1.refs_8_.refs_1_ = bf16[2,512,768]{2,1,0:T(8,128)(2,1)} custom-call(bf16[1,512,768]{2,1,0:T(8,128)(2,1)} %u_hbm.1, bf16[1,768,512]{2,1,0:T(8,128)(2,1)} %d_hbm), custom_call_target="tpu_custom_call" | custom-call | tf_op jit(solution)/shard_map/prepare/pallas_call | solution.py:309
  9.1 10.0 %collective-permute-done.refs_3_ = bf16[2,128,2048]{2,1,0:T(8,128)(2,1)S(1)} collective-permute-done((bf16[2,128,2048]{2,1,0:T(8,128)(2,1)S(1)}, bf16[2,128,2048]{2,1,0:T(8,128)(2,1)S(1)}, u32[]{:S(2)}, u32[]{:S(2)}) %collective-permute-start) | collective-permute-done | bytes 1048608 | tf_op jit(solution)/shard_map/ppermute | solution.py:28
  19.1 2.6 %collective-permute-start.1 = (bf16[80,2048]{1,0:T(8,128)(2,1)S(1)}, bf16[80,2048]{1,0:T(8,128)(2,1)S(1)}, u32[]{:S(2)}, u32[]{:S(2)}) collective-permute-start(bf16[80,2048]{1,0:T(8,128)(2,1)S(1)} %get-tuple-element.41), channel_id=1, source_target_pairs={{0,8},{4,12},{8,0},{12,4},{1,9},{5,13},{9,1},{13,5},{2,10},{6,14},... | collective-permute-start | bytes 983048 | tf_op jit(solution)/shard_map/ppermute | solution.py:22
  21.8 7.5 %attend.1 = (bf16[128,2048]{1,0:T(8,128)(2,1)S(1)}, bf16[80,2048]{1,0:T(8,128)(2,1)S(1)}, bf16[80,2048]{1,0:T(8,128)(2,1)S(1)}, bf16[80,2048]{1,0:T(8,128)(2,1)S(1)}, bf16[80,2048]{1,0:T(8,128)(2,1)S(1)}) custom-call(bf16[1,128,2048]{2,1,0:T(8,128)(2,1)S(1)} %copy-done.6, bf16[1,128,2048]{2,1,0:T(8,128)(2,1)S(1)} %copy-done.3, ...), custom_call_target="tpu_custom_call" | custom-call | tf_op jit(solution)/shard_map/attend/pallas_call | solution.py:337
  29.3 3.5 %collective-permute-done.1.refs_2_ = bf16[80,2048]{1,0:T(8,128)(2,1)S(1)} collective-permute-done((bf16[80,2048]{1,0:T(8,128)(2,1)S(1)}, bf16[80,2048]{1,0:T(8,128)(2,1)S(1)}, u32[]{:S(2)}, u32[]{:S(2)}) %collective-permute-start.1) | collective-permute-done | bytes 327712 | tf_op jit(solution)/shard_map/ppermute | solution.py:22
  32.8 2.2 %collective-permute-start.4 = (bf16[80,2048]{1,0:T(8,128)(2,1)S(1)}, bf16[80,2048]{1,0:T(8,128)(2,1)S(1)}, u32[]{:S(2)}, u32[]{:S(2)}) collective-permute-start(bf16[80,2048]{1,0:T(8,128)(2,1)S(1)} %get-tuple-element.48), channel_id=1, source_target_pairs={{0,12},{4,8},{8,4},{12,0},{1,13},{5,9},{9,5},{13,1},{2,14},{6,10},... | collective-permute-start | bytes 983048 | tf_op jit(solution)/shard_map/ppermute | solution.py:22
  35.0 4.3 %collective-permute-start.3 = (bf16[80,2048]{1,0:T(8,128)(2,1)S(1)}, bf16[80,2048]{1,0:T(8,128)(2,1)S(1)}, u32[]{:S(2)}, u32[]{:S(2)}) collective-permute-start(bf16[80,2048]{1,0:T(8,128)(2,1)S(1)} %get-tuple-element.46), channel_id=1, source_target_pairs={{0,8},{4,12},{8,0},{12,4},{1,9},{5,13},{9,1},{13,5},{2,10},{6,14},... | collective-permute-start | bytes 983048 | tf_op jit(solution)/shard_map/ppermute | solution.py:22
  39.8 4.6 %collective-permute-done.9.refs_10_.refs_3_ = bf16[2,512,768]{2,1,0:T(8,128)(2,1)S(1)} collective-permute-done((bf16[2,512,768]{2,1,0:T(8,128)(2,1)}, bf16[2,512,768]{2,1,0:T(8,128)(2,1)S(1)}, u32[]{:S(2)}, u32[]{:S(2)}) %collective-permute-start.9) | collective-permute-done | bytes 1572896 | tf_op jit(solution)/shard_map/ppermute | solution.py:22
  45.9 11.8 %collective-permute-done.4.refs_3_ = bf16[80,2048]{1,0:T(8,128)(2,1)S(1)} collective-permute-done((bf16[80,2048]{1,0:T(8,128)(2,1)S(1)}, bf16[80,2048]{1,0:T(8,128)(2,1)S(1)}, u32[]{:S(2)}, u32[]{:S(2)}) %collective-permute-start.4) | collective-permute-done | bytes 327712 | tf_op jit(solution)/shard_map/ppermute | solution.py:22
  57.7 3.9 %collective-permute-done.3.refs_2_ = bf16[80,2048]{1,0:T(8,128)(2,1)S(1)} collective-permute-done((bf16[80,2048]{1,0:T(8,128)(2,1)S(1)}, bf16[80,2048]{1,0:T(8,128)(2,1)S(1)}, u32[]{:S(2)}, u32[]{:S(2)}) %collective-permute-start.3) | collective-permute-done | bytes 327712 | tf_op jit(solution)/shard_map/ppermute | solution.py:22
  63.3 2.8 %collective-permute-done.5.refs_5_ = bf16[1,512,768]{2,1,0:T(8,128)(2,1)S(1)} collective-permute-done((bf16[1,512,768]{2,1,0:T(8,128)(2,1)S(1)}, bf16[1,512,768]{2,1,0:T(8,128)(2,1)S(1)}, u32[]{:S(2)}, u32[]{:S(2)}) %collective-permute-start.5) | collective-permute-done | bytes 786464 | tf_op jit(solution)/shard_map/ppermute | solution.py:22
  67.2 2.3 %hidden.1 = (bf16[320,768]{1,0:T(8,128)(2,1)S(1)}, f32[320,768]{1,0:T(8,128)S(1)}, f32[320,768]{1,0:T(8,128)S(1)}) custom-call(bf16[80,2048]{1,0:T(8,128)(2,1)S(1)} %get-tuple-element.42.refs_0_, bf16[80,2048]{1,0:T(8,128)(2,1)S(1)} %collective-permute-done.2.refs_1_, bf16[80,2048]{1,0:T(8,128)(2,1)S(1)} %collective-permute-done.3.refs_2_, ...), custom_call_target="tpu_custom_call" | custom-call | tf_op jit(solution)/shard_map/hidden/pallas_call | solution.py:358
  69.5 2.9 %collective-permute-start.14 = (bf16[80,2048]{1,0:T(8,128)(2,1)S(1)}, bf16[80,2048]{1,0:T(8,128)(2,1)S(1)}, u32[]{:S(2)}, u32[]{:S(2)}) collective-permute-start(bf16[80,2048]{1,0:T(8,128)(2,1)S(1)} %get-tuple-element.61), channel_id=1, source_target_pairs={{0,4},{4,0},{8,12},{12,8},{1,5},{5,1},{9,13},{13,9},{2,6},{6,2},{1... | collective-permute-start | bytes 983048 | tf_op jit(solution)/shard_map/ppermute | solution.py:22
  73.8 2.5 %collective-permute-start.12 = (bf16[80,2048]{1,0:T(8,128)(2,1)S(1)}, bf16[80,2048]{1,0:T(8,128)(2,1)S(1)}, u32[]{:S(2)}, u32[]{:S(2)}) collective-permute-start(bf16[80,2048]{1,0:T(8,128)(2,1)S(1)} %get-tuple-element.56), channel_id=1, source_target_pairs={{0,8},{4,12},{8,0},{12,4},{1,9},{5,13},{9,1},{13,5},{2,10},{6,14},... | collective-permute-start | bytes 983048 | tf_op jit(solution)/shard_map/ppermute | solution.py:22
  77.2 2.4 %collective-permute-done.15.refs_3_ = bf16[80,2048]{1,0:T(8,128)(2,1)S(1)} collective-permute-done((bf16[80,2048]{1,0:T(8,128)(2,1)S(1)}, bf16[80,2048]{1,0:T(8,128)(2,1)S(1)}, u32[]{:S(2)}, u32[]{:S(2)}) %collective-permute-start.15) | collective-permute-done | bytes 327712 | tf_op jit(solution)/shard_map/ppermute | solution.py:22
  79.6 9.0 %collective-permute-done.14.refs_1_ = bf16[80,2048]{1,0:T(8,128)(2,1)S(1)} collective-permute-done((bf16[80,2048]{1,0:T(8,128)(2,1)S(1)}, bf16[80,2048]{1,0:T(8,128)(2,1)S(1)}, u32[]{:S(2)}, u32[]{:S(2)}) %collective-permute-start.14) | collective-permute-done | bytes 327712 | tf_op jit(solution)/shard_map/ppermute | solution.py:22
  88.6 3.2 %backward.1 = (bf16[80,2048]{1,0:T(8,128)(2,1)S(1)}, bf16[80,2048]{1,0:T(8,128)(2,1)S(1)}, bf16[80,2048]{1,0:T(8,128)(2,1)S(1)}, bf16[80,2048]{1,0:T(8,128)(2,1)S(1)}) custom-call(bf16[80,2048]{1,0:T(8,128)(2,1)S(1)} %get-tuple-element.59.refs_0_, bf16[80,2048]{1,0:T(8,128)(2,1)S(1)} %collective-permute-done.14.refs_1_, ...), custom_call_target="tpu_custom_call" | custom-call | tf_op jit(solution)/shard_map/backward/pallas_call | solution.py:369
  91.9 2.5 %collective-permute-start.16 = (bf16[80,2048]{1,0:T(8,128)(2,1)S(1)}, bf16[80,2048]{1,0:T(8,128)(2,1)S(1)}, u32[]{:S(2)}, u32[]{:S(2)}) collective-permute-start(bf16[80,2048]{1,0:T(8,128)(2,1)S(1)} %get-tuple-element.67), channel_id=1, source_target_pairs={{0,4},{4,0},{8,12},{12,8},{1,5},{5,1},{9,13},{13,9},{2,6},{6,2},{1... | collective-permute-start | bytes 983048 | tf_op jit(solution)/shard_map/ppermute | solution.py:22
  97.0 10.7 %collective-permute-done.13.refs_3_ = bf16[80,2048]{1,0:T(8,128)(2,1)S(1)} collective-permute-done((bf16[80,2048]{1,0:T(8,128)(2,1)S(1)}, bf16[80,2048]{1,0:T(8,128)(2,1)S(1)}, u32[]{:S(2)}, u32[]{:S(2)}) %collective-permute-start.13) | collective-permute-done | bytes 327712 | tf_op jit(solution)/shard_map/ppermute | solution.py:22
  109.6 3.3 %collective-permute-done.16.refs_1_ = bf16[80,2048]{1,0:T(8,128)(2,1)S(1)} collective-permute-done((bf16[80,2048]{1,0:T(8,128)(2,1)S(1)}, bf16[80,2048]{1,0:T(8,128)(2,1)S(1)}, u32[]{:S(2)}, u32[]{:S(2)}) %collective-permute-start.16) | collective-permute-done | bytes 327712 | tf_op jit(solution)/shard_map/ppermute | solution.py:22
  112.9 14.7 %collective-permute-done.17.refs_2_ = bf16[80,2048]{1,0:T(8,128)(2,1)S(1)} collective-permute-done((bf16[80,2048]{1,0:T(8,128)(2,1)S(1)}, bf16[80,2048]{1,0:T(8,128)(2,1)S(1)}, u32[]{:S(2)}, u32[]{:S(2)}) %collective-permute-start.17) | collective-permute-done | bytes 327712 | tf_op jit(solution)/shard_map/ppermute | solution.py:22
  127.7 7.8 %collective-permute-done.18.refs_3_ = bf16[80,2048]{1,0:T(8,128)(2,1)S(1)} collective-permute-done((bf16[80,2048]{1,0:T(8,128)(2,1)S(1)}, bf16[80,2048]{1,0:T(8,128)(2,1)S(1)}, u32[]{:S(2)}, u32[]{:S(2)}) %collective-permute-start.18) | collective-permute-done | bytes 327712 | tf_op jit(solution)/shard_map/ppermute | solution.py:22
  135.5 2.3 %grad.1 = bf16[1,128,2048]{2,1,0:T(8,128)(2,1)} custom-call(s32[1,2,128]{2,1,0:T(2,128)S(1)} %bitcast.8, f32[1,2,128]{2,1,0:T(2,128)S(1)} %bitcast.10, bf16[1,128,2048]{2,1,0:T(8,128)(2,1)S(1)} %copy-done.1, bf16[128,2048]{1,0:T(8,128)(2,1)S(1)} %get-tuple-element.58.att_ref, f32[1,2048]{1,0:T(1,128)S(1)} %bitcast.4, bf16[1,128,2048]{2,1,0:T(8,128)(2,1)S(1)} %copy-done.5, ...), custom_call_target="tpu_custom_call" | custom-call | tf_op jit(solution)/shard_map/grad/pallas_call | solution.py:387
  (46 shorter events, 15.4 us)
Async XLA Ops:
  2.8 18.9 %copy-start.1 = (bf16[1,128,2048]{2,1,0:T(8,128)(2,1)S(1)}, bf16[1,128,2048]{2,1,0:T(8,128)(2,1)}, u32[]{:S(2)}) copy-start(bf16[1,128,2048]{2,1,0:T(8,128)(2,1)} %in_ref.3) | copy-start | bytes 1572868
  2.8 18.9 %copy-start.3 = (bf16[1,128,2048]{2,1,0:T(8,128)(2,1)S(1)}, bf16[1,128,2048]{2,1,0:T(8,128)(2,1)}, u32[]{:S(2)}) copy-start(bf16[1,128,2048]{2,1,0:T(8,128)(2,1)} %refs_1_.1) | copy-start | bytes 1572868
  2.8 18.9 %copy-start.4 = (bf16[1,128,2048]{2,1,0:T(8,128)(2,1)S(1)}, bf16[1,128,2048]{2,1,0:T(8,128)(2,1)}, u32[]{:S(2)}) copy-start(bf16[1,128,2048]{2,1,0:T(8,128)(2,1)} %refs_2_.1) | copy-start | bytes 1572868
  2.9 16.2 %collective-permute-start = (bf16[2,128,2048]{2,1,0:T(8,128)(2,1)S(1)}, bf16[2,128,2048]{2,1,0:T(8,128)(2,1)S(1)}, u32[]{:S(2)}, u32[]{:S(2)}) collective-permute-start(bf16[2,128,2048]{2,1,0:T(8,128)(2,1)S(1)} %constant_dynamic-update-slice_fusion), channel_id=1, source_target_pairs={{0,1},{1,4},{4,5},{5,8},{8,9},{9,12},{12,13},{2,3},{3,6},{6,7},{7,... | collective-permute-start | bytes 3145736 | tf_op jit(solution)/shard_map/ppermute | solution.py:28
  7.5 36.9 %collective-permute-start.9 = (bf16[2,512,768]{2,1,0:T(8,128)(2,1)}, bf16[2,512,768]{2,1,0:T(8,128)(2,1)S(1)}, u32[]{:S(2)}, u32[]{:S(2)}) collective-permute-start(bf16[2,512,768]{2,1,0:T(8,128)(2,1)} %prepare.1.refs_8_.refs_1_), channel_id=1, source_target_pairs={{0,2},{2,0},{1,3},{3,1},{4,6},{6,4},{5,7},{7,5},{8,10},{10,8},{9,1... | collective-permute-start | bytes 4718600 | tf_op jit(solution)/shard_map/ppermute | solution.py:22
  19.1 13.7 %collective-permute-start.1 = (bf16[80,2048]{1,0:T(8,128)(2,1)S(1)}, bf16[80,2048]{1,0:T(8,128)(2,1)S(1)}, u32[]{:S(2)}, u32[]{:S(2)}) collective-permute-start(bf16[80,2048]{1,0:T(8,128)(2,1)S(1)} %get-tuple-element.41), channel_id=1, source_target_pairs={{0,8},{4,12},{8,0},{12,4},{1,9},{5,13},{9,1},{13,5},{2,10},{6,14},... | collective-permute-start | bytes 983048 | tf_op jit(solution)/shard_map/ppermute | solution.py:22
  21.8 22.7 %copy-start = (bf16[2,512,768]{2,1,0:T(8,128)(2,1)S(1)}, bf16[2,512,768]{2,1,0:T(8,128)(2,1)}, u32[]{:S(2)}) copy-start(bf16[2,512,768]{2,1,0:T(8,128)(2,1)} %prepare.1.refs_8_.refs_1_) | copy-start | bytes 4718596
  32.8 24.9 %collective-permute-start.4 = (bf16[80,2048]{1,0:T(8,128)(2,1)S(1)}, bf16[80,2048]{1,0:T(8,128)(2,1)S(1)}, u32[]{:S(2)}, u32[]{:S(2)}) collective-permute-start(bf16[80,2048]{1,0:T(8,128)(2,1)S(1)} %get-tuple-element.48), channel_id=1, source_target_pairs={{0,12},{4,8},{8,4},{12,0},{1,13},{5,9},{9,5},{13,1},{2,14},{6,10},... | collective-permute-start | bytes 983048 | tf_op jit(solution)/shard_map/ppermute | solution.py:22
  35.0 26.6 %collective-permute-start.3 = (bf16[80,2048]{1,0:T(8,128)(2,1)S(1)}, bf16[80,2048]{1,0:T(8,128)(2,1)S(1)}, u32[]{:S(2)}, u32[]{:S(2)}) collective-permute-start(bf16[80,2048]{1,0:T(8,128)(2,1)S(1)} %get-tuple-element.46), channel_id=1, source_target_pairs={{0,8},{4,12},{8,0},{12,4},{1,9},{5,13},{9,1},{13,5},{2,10},{6,14},... | collective-permute-start | bytes 983048 | tf_op jit(solution)/shard_map/ppermute | solution.py:22
  39.3 22.3 %collective-permute-start.2 = (bf16[80,2048]{1,0:T(8,128)(2,1)S(1)}, bf16[80,2048]{1,0:T(8,128)(2,1)S(1)}, u32[]{:S(2)}, u32[]{:S(2)}) collective-permute-start(bf16[80,2048]{1,0:T(8,128)(2,1)S(1)} %get-tuple-element.44), channel_id=1, source_target_pairs={{0,4},{4,0},{8,12},{12,8},{1,5},{5,1},{9,13},{13,9},{2,6},{6,2},{1... | collective-permute-start | bytes 983048 | tf_op jit(solution)/shard_map/ppermute | solution.py:22
  39.3 22.8 %collective-permute-start.6 = (bf16[1,512,768]{2,1,0:T(8,128)(2,1)S(1)}, bf16[1,512,768]{2,1,0:T(8,128)(2,1)S(1)}, u32[]{:S(2)}, u32[]{:S(2)}) collective-permute-start(bf16[1,512,768]{2,1,0:T(8,128)(2,1)S(1)} %copy-done.2), channel_id=1, source_target_pairs={{0,2},{2,0},{1,3},{3,1},{4,6},{6,4},{5,7},{7,5},{8,10},{10,8},{9,1... | collective-permute-start | bytes 2359304 | tf_op jit(solution)/shard_map/ppermute | solution.py:22
  44.4 22.8 %collective-permute-start.8 = (bf16[2,512,768]{2,1,0:T(8,128)(2,1)S(1)}, bf16[2,512,768]{2,1,0:T(8,128)(2,1)S(1)}, u32[]{:S(2)}, u32[]{:S(2)}) collective-permute-start(bf16[2,512,768]{2,1,0:T(8,128)(2,1)S(1)} %copy-done), channel_id=1, source_target_pairs={{0,1},{1,0},{2,3},{3,2},{4,5},{5,4},{6,7},{7,6},{8,9},{9,8},{10,11... | collective-permute-start | bytes 4718600 | tf_op jit(solution)/shard_map/ppermute | solution.py:22
  61.6 5.7 %collective-permute-start.10 = (bf16[2,512,768]{2,1,0:T(8,128)(2,1)S(1)}, bf16[2,512,768]{2,1,0:T(8,128)(2,1)S(1)}, u32[]{:S(2)}, u32[]{:S(2)}) collective-permute-start(bf16[2,512,768]{2,1,0:T(8,128)(2,1)S(1)} %collective-permute-done.9.refs_10_.refs_3_), channel_id=1, source_target_pairs={{0,1},{1,0},{2,3},{3,2},{4,5},{5,4},{6,7},{7,6},{8,9},{9,8},{10,11... | collective-permute-start | bytes 4718600 | tf_op jit(solution)/shard_map/ppermute | solution.py:22
  61.6 4.5 %collective-permute-start.5 = (bf16[1,512,768]{2,1,0:T(8,128)(2,1)S(1)}, bf16[1,512,768]{2,1,0:T(8,128)(2,1)S(1)}, u32[]{:S(2)}, u32[]{:S(2)}) collective-permute-start(bf16[1,512,768]{2,1,0:T(8,128)(2,1)S(1)} %copy-done.2), channel_id=1, source_target_pairs={{0,1},{1,0},{2,3},{3,2},{4,5},{5,4},{6,7},{7,6},{8,9},{9,8},{10,11... | collective-permute-start | bytes 2359304 | tf_op jit(solution)/shard_map/ppermute | solution.py:22
  62.1 5.1 %collective-permute-start.7 = (bf16[1,512,768]{2,1,0:T(8,128)(2,1)S(1)}, bf16[1,512,768]{2,1,0:T(8,128)(2,1)S(1)}, u32[]{:S(2)}, u32[]{:S(2)}) collective-permute-start(bf16[1,512,768]{2,1,0:T(8,128)(2,1)S(1)} %collective-permute-done.6.refs_6_), channel_id=1, source_target_pairs={{0,1},{1,0},{2,3},{3,2},{4,5},{5,4},{6,7},{7,6},{8,9},{9,8},{10,11... | collective-permute-start | bytes 2359304 | tf_op jit(solution)/shard_map/ppermute | solution.py:22
  62.1 17.5 %collective-permute-start.15 = (bf16[80,2048]{1,0:T(8,128)(2,1)S(1)}, bf16[80,2048]{1,0:T(8,128)(2,1)S(1)}, u32[]{:S(2)}, u32[]{:S(2)}) collective-permute-start(bf16[80,2048]{1,0:T(8,128)(2,1)S(1)} %get-tuple-element.63), channel_id=1, source_target_pairs={{0,12},{4,8},{8,4},{12,0},{1,13},{5,9},{9,5},{13,1},{2,14},{6,10},... | collective-permute-start | bytes 983048 | tf_op jit(solution)/shard_map/ppermute | solution.py:22
  69.5 19.1 %collective-permute-start.14 = (bf16[80,2048]{1,0:T(8,128)(2,1)S(1)}, bf16[80,2048]{1,0:T(8,128)(2,1)S(1)}, u32[]{:S(2)}, u32[]{:S(2)}) collective-permute-start(bf16[80,2048]{1,0:T(8,128)(2,1)S(1)} %get-tuple-element.61), channel_id=1, source_target_pairs={{0,4},{4,0},{8,12},{12,8},{1,5},{5,1},{9,13},{13,9},{2,6},{6,2},{1... | collective-permute-start | bytes 983048 | tf_op jit(solution)/shard_map/ppermute | solution.py:22
  73.7 22.1 %collective-permute-start.11 = (bf16[80,2048]{1,0:T(8,128)(2,1)S(1)}, bf16[80,2048]{1,0:T(8,128)(2,1)S(1)}, u32[]{:S(2)}, u32[]{:S(2)}) collective-permute-start(bf16[80,2048]{1,0:T(8,128)(2,1)S(1)} %get-tuple-element.55), channel_id=1, source_target_pairs={{0,4},{4,0},{8,12},{12,8},{1,5},{5,1},{9,13},{13,9},{2,6},{6,2},{1... | collective-permute-start | bytes 983048 | tf_op jit(solution)/shard_map/ppermute | solution.py:22
  73.8 23.2 %collective-permute-start.12 = (bf16[80,2048]{1,0:T(8,128)(2,1)S(1)}, bf16[80,2048]{1,0:T(8,128)(2,1)S(1)}, u32[]{:S(2)}, u32[]{:S(2)}) collective-permute-start(bf16[80,2048]{1,0:T(8,128)(2,1)S(1)} %get-tuple-element.56), channel_id=1, source_target_pairs={{0,8},{4,12},{8,0},{12,4},{1,9},{5,13},{9,1},{13,5},{2,10},{6,14},... | collective-permute-start | bytes 983048 | tf_op jit(solution)/shard_map/ppermute | solution.py:22
  76.3 31.5 %collective-permute-start.13 = (bf16[80,2048]{1,0:T(8,128)(2,1)S(1)}, bf16[80,2048]{1,0:T(8,128)(2,1)S(1)}, u32[]{:S(2)}, u32[]{:S(2)}) collective-permute-start(bf16[80,2048]{1,0:T(8,128)(2,1)S(1)} %get-tuple-element.57), channel_id=1, source_target_pairs={{0,12},{4,8},{8,4},{12,0},{1,13},{5,9},{9,5},{13,1},{2,14},{6,10},... | collective-permute-start | bytes 983048 | tf_op jit(solution)/shard_map/ppermute | solution.py:22
  88.6 19.1 %copy-start.9 = (f32[1,128,2]{1,2,0:T(2,128)S(1)}, f32[1,128,2]{1,2,0:T(2,128)}, u32[]{:S(2)}) copy-start(f32[1,128,2]{1,2,0:T(2,128)} %param.19) | copy-start | bytes 3076
  91.9 21.1 %collective-permute-start.16 = (bf16[80,2048]{1,0:T(8,128)(2,1)S(1)}, bf16[80,2048]{1,0:T(8,128)(2,1)S(1)}, u32[]{:S(2)}, u32[]{:S(2)}) collective-permute-start(bf16[80,2048]{1,0:T(8,128)(2,1)S(1)} %get-tuple-element.67), channel_id=1, source_target_pairs={{0,4},{4,0},{8,12},{12,8},{1,5},{5,1},{9,13},{13,9},{2,6},{6,2},{1... | collective-permute-start | bytes 983048 | tf_op jit(solution)/shard_map/ppermute | solution.py:22
  94.4 33.3 %collective-permute-start.17 = (bf16[80,2048]{1,0:T(8,128)(2,1)S(1)}, bf16[80,2048]{1,0:T(8,128)(2,1)S(1)}, u32[]{:S(2)}, u32[]{:S(2)}) collective-permute-start(bf16[80,2048]{1,0:T(8,128)(2,1)S(1)} %get-tuple-element.68), channel_id=1, source_target_pairs={{0,8},{4,12},{8,0},{12,4},{1,9},{5,13},{9,1},{13,5},{2,10},{6,14},... | collective-permute-start | bytes 983048 | tf_op jit(solution)/shard_map/ppermute | solution.py:22
  95.8 39.7 %collective-permute-start.18 = (bf16[80,2048]{1,0:T(8,128)(2,1)S(1)}, bf16[80,2048]{1,0:T(8,128)(2,1)S(1)}, u32[]{:S(2)}, u32[]{:S(2)}) collective-permute-start(bf16[80,2048]{1,0:T(8,128)(2,1)S(1)} %get-tuple-element.69), channel_id=1, source_target_pairs={{0,12},{4,8},{8,4},{12,0},{1,13},{5,9},{9,5},{13,1},{2,14},{6,10},... | collective-permute-start | bytes 983048 | tf_op jit(solution)/shard_map/ppermute | solution.py:22
  (6 other events, 84.9 us)

commit v6 on v5

--- a/solution.py
+++ b/solution.py
@@ -99,7 +99,7 @@
 
 
 def attend_kernel(
-    slots, q_ref, k_ref, v_ref, past_ref, doc_ref, in_ref, gain_ref, ids_ref, att_ref, *refs
+    slots, q_ref, k_ref, v_ref, kp_ref, vp_ref, doc_ref, in_ref, gain_ref, ids_ref, att_ref, *refs
 ):
     out_refs, (resid_ref, squares_ref) = refs[:-2], refs[-2:]
     group, groups = pl.program_id(0), pl.num_programs(0)
@@ -121,13 +121,13 @@
         at = slice(h * HD, (h + 1) * HD)
         q = q_ref[0, :, at]
         own = jnp.where(see_own, dot_t(q, k_ref[0, :, at]) * scale, -jnp.inf)
-        past = jnp.where(see_past, dot_t(q, past_ref[0, :, at]) * scale, -jnp.inf)
+        past = jnp.where(see_past, dot_t(q, kp_ref[0, :, at]) * scale, -jnp.inf)
         top = jnp.maximum(own, past).max(axis=1, keepdims=True)
         own, past = jnp.exp(own - top), jnp.exp(past - top)
         total = (own + past).sum(axis=1, keepdims=True)
         inverse = 1.0 / total
         own, past = (own * inverse).astype(BF), (past * inverse).astype(BF)
-        part = dot(own, v_ref[0, :, at]) + dot(past, past_ref[1, :, at])
+        part = dot(own, v_ref[0, :, at]) + dot(past, vp_ref[0, :, at])
         part = part.astype(BF)
         att_ref[:, at] = part
         resid = in_ref[0, :, at].astype(F32) + part.astype(F32)
@@ -220,20 +220,16 @@
             out[:, quarter(j, gate.shape[1])] = part[k * slots : (k + 1) * slots]
 
 
-def mixed(ids_ref, weight_ref, backs, at, cache):
+def mixed(ids_ref, weight_ref, backs, kinds, at, cache):
     if not cache:
         first, second, slot = routing(ids_ref[0, 0:1], ids_ref[0, 1:2], lax.axis_index("expert"))
         slots = backs[0].shape[0]
         gates = [column(weight_ref[0, j : j + 1]) for j in range(2)]
-        for k in range(len(backs)):
+        for k in kinds:
             place = placing(slot, k, slots)[:, :slots].astype(BF)
             weight = jnp.where(first == k, gates[0], 0.0) + jnp.where(second == k, gates[1], 0.0)
             cache.append((place, weight))
-    total = None
-    for back, (place, weight) in zip(backs, cache):
-        term = weight * dot(place, back[:, at])
-        total = term if total is None else total + term
-    return total
+    return summed([weight * dot(place, back[:, at]) for back, (place, weight) in zip(backs, cache)])
 
 
 def layer_kernel(ids_ref, weight_ref, in_ref, att_ref, *refs):
@@ -242,23 +238,35 @@
     for n in range(in_ref.shape[2] // step):
         at = slice(n * step, (n + 1) * step)
         resid = in_ref[0, :, at].astype(F32) + att_ref[:, at].astype(F32)
-        out_ref[0, :, at] = (resid + mixed(ids_ref, weight_ref, backs, at, cache)).astype(BF)
-
-
-def grad_kernel(ids_ref, weight_ref, in_ref, att_ref, gain_ref, up_ref, *refs):
+        out_ref[0, :, at] = (resid + mixed(ids_ref, weight_ref, backs, range(len(backs)), at, cache)).astype(BF)
+
+
+def near_grad_kernel(ids_ref, weight_ref, in_ref, att_ref, *refs):
+    backs, sum_ref, rms_ref = refs[:-2], refs[-2], refs[-1]
+    tok, width = in_ref.shape[1], in_ref.shape[2]
+    step, cache = 512, []
+    squares = jnp.zeros((tok, 1), F32)
+    for n in range(width // step):
+        at = slice(n * step, (n + 1) * step)
+        resid = in_ref[0, :, at].astype(F32) + att_ref[:, at].astype(F32)
+        sum_ref[:, at] = mixed(ids_ref, weight_ref, backs, range(len(backs)), at, cache)
+        squares = squares + (resid * resid).sum(axis=1, keepdims=True)
+    rms_ref[...] = jnp.broadcast_to(lax.rsqrt(squares / width + 1e-06), rms_ref.shape)
+
+
+def grad_kernel(ids_ref, weight_ref, in_ref, att_ref, gain_ref, up_ref, sum_ref, rms_ref, *refs):
     backs, out_ref, gained_ref = refs[:-2], refs[-2], refs[-1]
     tok, width = in_ref.shape[1], in_ref.shape[2]
     step, cache = 512, []
-    squares = jnp.zeros((tok, 1), F32)
+    kinds = range(lax.axis_size("expert") - len(backs), lax.axis_size("expert"))
     cross = jnp.zeros((tok, 1), F32)
     for n in range(width // step):
         at = slice(n * step, (n + 1) * step)
         resid = in_ref[0, :, at].astype(F32) + att_ref[:, at].astype(F32)
-        gained = gain_ref[:, at] * mixed(ids_ref, weight_ref, backs, at, cache)
+        gained = gain_ref[:, at] * (sum_ref[:, at] + mixed(ids_ref, weight_ref, backs, kinds, at, cache))
         gained_ref[:, at] = gained
-        squares = squares + (resid * resid).sum(axis=1, keepdims=True)
         cross = cross + (resid * gained).sum(axis=1, keepdims=True)
-    inv_rms = lax.rsqrt(squares / width + 1e-06)
+    inv_rms = rms_ref[:, 0:1]
     pull = inv_rms * inv_rms * inv_rms * (cross / width)
     for n in range(width // step):
         at = slice(n * step, (n + 1) * step)
@@ -304,7 +312,7 @@
     def over_x(block):
         return [swapped(block, "fsdp", dx) for dx in range(1, lax.axis_size("fsdp"))]
 
-    both = jnp.concatenate([keys, values], 0)
+    both = jnp.concatenate([keys, values], 2)
     previous = shifted(both, ("expert", "ctx"), 1)
     own_others = pl.pallas_call(
         prepare_kernel,
@@ -339,12 +347,12 @@
         out_shape=[jax.ShapeDtypeStruct((tok, width), BF)] + slabs,
         grid=(parts,),
         in_specs=[by_part(1, tok)] * 3
-        + [by_part(2, tok), fixed(*doc_ids.shape), by_part(1, tok), fixed(1, width), fixed(*ids.shape)],
+        + [by_part(1, tok), pl.BlockSpec((1, tok, cut), lambda n: (0, 0, n + parts)), fixed(*doc_ids.shape), by_part(1, tok), fixed(1, width), fixed(*ids.shape)],
         out_specs=[by_part(tok)] + [fixed(slots, width)] * peers,
         scratch_shapes=[pltpu.VMEM((parts, tok, cut), F32), pltpu.VMEM((tok, HD), F32)],
         compiler_params=params(16),
         name="attend",
-    )(queries, keys, values, previous, doc_ids, inputs, gain, ids)
+    )(queries, keys, values, previous, previous, doc_ids, inputs, gain, ids)
     rows = exchanged([after(block, grads[-1]) for block in sent_rows])
 
     all_gates, all_others = [w_gate, over_core(after(w_gate, attended))], [own_others, over_core(after(own_others, attended))]
@@ -384,15 +392,16 @@
         compiler_params=params(32),
         name="layer",
     )(ids, gates, inputs, attended, *back_out)
-    input_grad = pl.pallas_call(
-        grad_kernel,
-        out_shape=out_block,
-        in_specs=[VM] * (6 + peers),
-        out_specs=VM,
-        scratch_shapes=[pltpu.VMEM((tok, width), F32)],
-        compiler_params=params(32),
-        name="grad",
-    )(ids, gates, inputs, after(attended, layer_out), gain, out_grad, *back_grad)
+    near = peers - 1
+    near_sum, inv_rms = call(
+        near_grad_kernel,
+        "near_grad",
+        [jax.ShapeDtypeStruct((tok, width), F32), jax.ShapeDtypeStruct((tok, 128), F32)],
+        4 + near,
+    )(ids, gates, inputs, after(attended, layer_out), *back_grad[:near])
+    input_grad = call(
+        grad_kernel, "grad", out_block, 8 + peers - near, [pltpu.VMEM((tok, width), F32)]
+    )(ids, gates, inputs, attended, gain, out_grad, near_sum, inv_rms, *back_grad[near:])
     return layer_out, input_grad
 
 

time: 138 us -> 138 us (level)
    pallas_call x1 -> x2, Pallas kernels: 2.29 us -> 2.85 us  [the longest x1 1.87 us: shards(): call(grad_kernel, 'grad', out_block, 8 + peers - near, [pltpu.VMEM((tok,...]
  transfers between devices with their start and end apart: 19 -> 19, of which waited for: 15 -> 15; matrix products, arithmetic and copies ran while one was open for 0% -> 0% of each run, Pallas kernels for 14% -> 15%
where the time goes in v6:
time: 138 us; the launch traced here: 137 us
  waiting for transfers between devices  85.6 us (62%)
  starting transfers between devices  26.2 us (19%)
  Pallas kernels  22.5 us (16%)
  local copies, waits for them, and re-layouts  2.22 us (2%)
    ppermute x18, waiting for transfers between devices, swapped(): return lax.ppermute(block, axis, [(i, i ^ distance) for i in range(count)])  75.6 us
    ppermute x18, starting transfers between devices, swapped(): return lax.ppermute(block, axis, [(i, i ^ distance) for i in range(count)])  24.1 us
    ppermute x1, waiting for transfers between devices, shifted(): return lax.ppermute(block, axis, route)  10.1 us
    pallas_call x1, Pallas kernels, shards(): pl.pallas_call(lambda *refs: attend_kernel(slots, *refs), out_shape=[jax....  7.52 us
    pallas_call x1, Pallas kernels, shards(): call(lambda *refs: backward_kernel(len(grads), pieces, slots, *refs), 'ba...  3.23 us
  transfers between devices with their start and end apart: 19, of which 15 were waited for; matrix products, arithmetic and copies ran while one was open for 0% of the time, Pallas kernels for 15%

profile of v6, /device:TPU:10, one launch (start us, length us, event | category | flops | bytes accessed | tf_op | source)
XLA Modules:
  0.0 137.4 jit_solution(8651412628622704153)
XLA Ops:
  2.9 2.1 %collective-permute-start = (bf16[1,128,4096]{2,1,0:T(8,128)(2,1)S(1)}, bf16[1,128,4096]{2,1,0:T(8,128)(2,1)S(1)}, u32[]{:S(2)}, u32[]{:S(2)}) collective-permute-start(bf16[1,128,4096]{2,1,0:T(8,128)(2,1)S(1)} %constant_dynamic-update-slice_fusion), channel_id=1, source_target_pairs={{0,1},{1,4},{4,5},{5,8},{8,9},{9,12},{12,13},{2,3},{3,6},{6,7},{7,... | collective-permute-start | bytes 3145736 | tf_op jit(solution)/shard_map/ppermute | solution.py:28
  4.9 2.6 %prepare.1.refs_8_.refs_1_ = bf16[2,512,768]{2,1,0:T(8,128)(2,1)} custom-call(bf16[1,512,768]{2,1,0:T(8,128)(2,1)} %u_hbm.1, bf16[1,768,512]{2,1,0:T(8,128)(2,1)} %d_hbm), custom_call_target="tpu_custom_call" | custom-call | tf_op jit(solution)/shard_map/prepare/pallas_call | solution.py:317
  9.1 10.1 %collective-permute-done.refs_3_.refs_4_ = bf16[1,128,4096]{2,1,0:T(8,128)(2,1)S(1)} collective-permute-done((bf16[1,128,4096]{2,1,0:T(8,128)(2,1)S(1)}, bf16[1,128,4096]{2,1,0:T(8,128)(2,1)S(1)}, u32[]{:S(2)}, u32[]{:S(2)}) %collective-permute-start) | collective-permute-done | bytes 1048608 | tf_op jit(solution)/shard_map/ppermute | solution.py:28
  19.1 2.6 %collective-permute-start.1 = (bf16[80,2048]{1,0:T(8,128)(2,1)S(1)}, bf16[80,2048]{1,0:T(8,128)(2,1)S(1)}, u32[]{:S(2)}, u32[]{:S(2)}) collective-permute-start(bf16[80,2048]{1,0:T(8,128)(2,1)S(1)} %get-tuple-element.43), channel_id=1, source_target_pairs={{0,8},{4,12},{8,0},{12,4},{1,9},{5,13},{9,1},{13,5},{2,10},{6,14},... | collective-permute-start | bytes 983048 | tf_op jit(solution)/shard_map/ppermute | solution.py:22
  21.8 7.5 %attend.1 = (bf16[128,2048]{1,0:T(8,128)(2,1)S(1)}, bf16[80,2048]{1,0:T(8,128)(2,1)S(1)}, bf16[80,2048]{1,0:T(8,128)(2,1)S(1)}, bf16[80,2048]{1,0:T(8,128)(2,1)S(1)}, bf16[80,2048]{1,0:T(8,128)(2,1)S(1)}) custom-call(bf16[1,128,2048]{2,1,0:T(8,128)(2,1)S(1)} %copy-done.6, bf16[1,128,2048]{2,1,0:T(8,128)(2,1)S(1)} %copy-done.4, ...), custom_call_target="tpu_custom_call" | custom-call | tf_op jit(solution)/shard_map/attend/pallas_call | solution.py:345
  29.3 3.5 %collective-permute-done.1.refs_2_ = bf16[80,2048]{1,0:T(8,128)(2,1)S(1)} collective-permute-done((bf16[80,2048]{1,0:T(8,128)(2,1)S(1)}, bf16[80,2048]{1,0:T(8,128)(2,1)S(1)}, u32[]{:S(2)}, u32[]{:S(2)}) %collective-permute-start.1) | collective-permute-done | bytes 327712 | tf_op jit(solution)/shard_map/ppermute | solution.py:22
  32.8 2.2 %collective-permute-start.4 = (bf16[80,2048]{1,0:T(8,128)(2,1)S(1)}, bf16[80,2048]{1,0:T(8,128)(2,1)S(1)}, u32[]{:S(2)}, u32[]{:S(2)}) collective-permute-start(bf16[80,2048]{1,0:T(8,128)(2,1)S(1)} %get-tuple-element.50), channel_id=1, source_target_pairs={{0,12},{4,8},{8,4},{12,0},{1,13},{5,9},{9,5},{13,1},{2,14},{6,10},... | collective-permute-start | bytes 983048 | tf_op jit(solution)/shard_map/ppermute | solution.py:22
  35.0 4.3 %collective-permute-start.3 = (bf16[80,2048]{1,0:T(8,128)(2,1)S(1)}, bf16[80,2048]{1,0:T(8,128)(2,1)S(1)}, u32[]{:S(2)}, u32[]{:S(2)}) collective-permute-start(bf16[80,2048]{1,0:T(8,128)(2,1)S(1)} %get-tuple-element.48), channel_id=1, source_target_pairs={{0,8},{4,12},{8,0},{12,4},{1,9},{5,13},{9,1},{13,5},{2,10},{6,14},... | collective-permute-start | bytes 983048 | tf_op jit(solution)/shard_map/ppermute | solution.py:22
  39.8 4.6 %collective-permute-done.9.refs_10_.refs_3_ = bf16[2,512,768]{2,1,0:T(8,128)(2,1)S(1)} collective-permute-done((bf16[2,512,768]{2,1,0:T(8,128)(2,1)}, bf16[2,512,768]{2,1,0:T(8,128)(2,1)S(1)}, u32[]{:S(2)}, u32[]{:S(2)}) %collective-permute-start.9) | collective-permute-done | bytes 1572896 | tf_op jit(solution)/shard_map/ppermute | solution.py:22
  45.9 11.8 %collective-permute-done.4.refs_3_ = bf16[80,2048]{1,0:T(8,128)(2,1)S(1)} collective-permute-done((bf16[80,2048]{1,0:T(8,128)(2,1)S(1)}, bf16[80,2048]{1,0:T(8,128)(2,1)S(1)}, u32[]{:S(2)}, u32[]{:S(2)}) %collective-permute-start.4) | collective-permute-done | bytes 327712 | tf_op jit(solution)/shard_map/ppermute | solution.py:22
  57.7 3.9 %collective-permute-done.3.refs_2_ = bf16[80,2048]{1,0:T(8,128)(2,1)S(1)} collective-permute-done((bf16[80,2048]{1,0:T(8,128)(2,1)S(1)}, bf16[80,2048]{1,0:T(8,128)(2,1)S(1)}, u32[]{:S(2)}, u32[]{:S(2)}) %collective-permute-start.3) | collective-permute-done | bytes 327712 | tf_op jit(solution)/shard_map/ppermute | solution.py:22
  63.3 2.8 %collective-permute-done.5.refs_5_ = bf16[1,512,768]{2,1,0:T(8,128)(2,1)S(1)} collective-permute-done((bf16[1,512,768]{2,1,0:T(8,128)(2,1)S(1)}, bf16[1,512,768]{2,1,0:T(8,128)(2,1)S(1)}, u32[]{:S(2)}, u32[]{:S(2)}) %collective-permute-start.5) | collective-permute-done | bytes 786464 | tf_op jit(solution)/shard_map/ppermute | solution.py:22
  67.2 2.3 %hidden.1 = (bf16[320,768]{1,0:T(8,128)(2,1)S(1)}, f32[320,768]{1,0:T(8,128)S(1)}, f32[320,768]{1,0:T(8,128)S(1)}) custom-call(bf16[80,2048]{1,0:T(8,128)(2,1)S(1)} %get-tuple-element.44.refs_0_, bf16[80,2048]{1,0:T(8,128)(2,1)S(1)} %collective-permute-done.2.refs_1_, bf16[80,2048]{1,0:T(8,128)(2,1)S(1)} %collective-permute-done.3.refs_2_, ...), custom_call_target="tpu_custom_call" | custom-call | tf_op jit(solution)/shard_map/hidden/pallas_call | solution.py:366
  69.5 2.9 %collective-permute-start.14 = (bf16[80,2048]{1,0:T(8,128)(2,1)S(1)}, bf16[80,2048]{1,0:T(8,128)(2,1)S(1)}, u32[]{:S(2)}, u32[]{:S(2)}) collective-permute-start(bf16[80,2048]{1,0:T(8,128)(2,1)S(1)} %get-tuple-element.63), channel_id=1, source_target_pairs={{0,4},{4,0},{8,12},{12,8},{1,5},{5,1},{9,13},{13,9},{2,6},{6,2},{1... | collective-permute-start | bytes 983048 | tf_op jit(solution)/shard_map/ppermute | solution.py:22
  73.8 2.5 %collective-permute-start.12 = (bf16[80,2048]{1,0:T(8,128)(2,1)S(1)}, bf16[80,2048]{1,0:T(8,128)(2,1)S(1)}, u32[]{:S(2)}, u32[]{:S(2)}) collective-permute-start(bf16[80,2048]{1,0:T(8,128)(2,1)S(1)} %get-tuple-element.58), channel_id=1, source_target_pairs={{0,8},{4,12},{8,0},{12,4},{1,9},{5,13},{9,1},{13,5},{2,10},{6,14},... | collective-permute-start | bytes 983048 | tf_op jit(solution)/shard_map/ppermute | solution.py:22
  77.2 2.4 %collective-permute-done.15.refs_3_ = bf16[80,2048]{1,0:T(8,128)(2,1)S(1)} collective-permute-done((bf16[80,2048]{1,0:T(8,128)(2,1)S(1)}, bf16[80,2048]{1,0:T(8,128)(2,1)S(1)}, u32[]{:S(2)}, u32[]{:S(2)}) %collective-permute-start.15) | collective-permute-done | bytes 327712 | tf_op jit(solution)/shard_map/ppermute | solution.py:22
  79.6 9.0 %collective-permute-done.14.refs_1_ = bf16[80,2048]{1,0:T(8,128)(2,1)S(1)} collective-permute-done((bf16[80,2048]{1,0:T(8,128)(2,1)S(1)}, bf16[80,2048]{1,0:T(8,128)(2,1)S(1)}, u32[]{:S(2)}, u32[]{:S(2)}) %collective-permute-start.14) | collective-permute-done | bytes 327712 | tf_op jit(solution)/shard_map/ppermute | solution.py:22
  88.6 3.2 %backward.1 = (bf16[80,2048]{1,0:T(8,128)(2,1)S(1)}, bf16[80,2048]{1,0:T(8,128)(2,1)S(1)}, bf16[80,2048]{1,0:T(8,128)(2,1)S(1)}, bf16[80,2048]{1,0:T(8,128)(2,1)S(1)}) custom-call(bf16[80,2048]{1,0:T(8,128)(2,1)S(1)} %get-tuple-element.61.refs_0_, bf16[80,2048]{1,0:T(8,128)(2,1)S(1)} %collective-permute-done.14.refs_1_, ...), custom_call_target="tpu_custom_call" | custom-call | tf_op jit(solution)/shard_map/backward/pallas_call | solution.py:377
  91.9 2.5 %collective-permute-start.16 = (bf16[80,2048]{1,0:T(8,128)(2,1)S(1)}, bf16[80,2048]{1,0:T(8,128)(2,1)S(1)}, u32[]{:S(2)}, u32[]{:S(2)}) collective-permute-start(bf16[80,2048]{1,0:T(8,128)(2,1)S(1)} %get-tuple-element.69), channel_id=1, source_target_pairs={{0,4},{4,0},{8,12},{12,8},{1,5},{5,1},{9,13},{13,9},{2,6},{6,2},{1... | collective-permute-start | bytes 983048 | tf_op jit(solution)/shard_map/ppermute | solution.py:22
  97.0 10.7 %collective-permute-done.13.refs_3_ = bf16[80,2048]{1,0:T(8,128)(2,1)S(1)} collective-permute-done((bf16[80,2048]{1,0:T(8,128)(2,1)S(1)}, bf16[80,2048]{1,0:T(8,128)(2,1)S(1)}, u32[]{:S(2)}, u32[]{:S(2)}) %collective-permute-start.13) | collective-permute-done | bytes 327712 | tf_op jit(solution)/shard_map/ppermute | solution.py:22
  107.8 1.9 %layer.1 = bf16[1,128,2048]{2,1,0:T(8,128)(2,1)} custom-call(s32[1,2,128]{2,1,0:T(2,128)S(1)} %bitcast.7, f32[1,2,128]{2,1,0:T(2,128)S(1)} %bitcast.10, bf16[1,128,2048]{2,1,0:T(8,128)(2,1)S(1)} %copy-done.1, bf16[128,2048]{1,0:T(8,128)(2,1)S(1)} %get-tuple-element.60.att_ref, bf16[80,2048]{1,0:T(8,128)(2,1)S(1)} %get-tuple-element.56.refs_0_, ...), custom_call_target="tpu_custom_call" | custom-call | tf_op jit(solution)/shard_map/layer/pallas_call | solution.py:387
  109.6 3.3 %collective-permute-done.16.refs_1_ = bf16[80,2048]{1,0:T(8,128)(2,1)S(1)} collective-permute-done((bf16[80,2048]{1,0:T(8,128)(2,1)S(1)}, bf16[80,2048]{1,0:T(8,128)(2,1)S(1)}, u32[]{:S(2)}, u32[]{:S(2)}) %collective-permute-start.16) | collective-permute-done | bytes 327712 | tf_op jit(solution)/shard_map/ppermute | solution.py:22
  112.9 14.7 %collective-permute-done.17.refs_2_ = bf16[80,2048]{1,0:T(8,128)(2,1)S(1)} collective-permute-done((bf16[80,2048]{1,0:T(8,128)(2,1)S(1)}, bf16[80,2048]{1,0:T(8,128)(2,1)S(1)}, u32[]{:S(2)}, u32[]{:S(2)}) %collective-permute-start.17) | collective-permute-done | bytes 327712 | tf_op jit(solution)/shard_map/ppermute | solution.py:22
  128.7 6.8 %collective-permute-done.18.refs_0_ = bf16[80,2048]{1,0:T(8,128)(2,1)S(1)} collective-permute-done((bf16[80,2048]{1,0:T(8,128)(2,1)S(1)}, bf16[80,2048]{1,0:T(8,128)(2,1)S(1)}, u32[]{:S(2)}, u32[]{:S(2)}) %collective-permute-start.18) | collective-permute-done | bytes 327712 | tf_op jit(solution)/shard_map/ppermute | solution.py:22
  (47 shorter events, 16.3 us)
Async XLA Ops:
  2.8 18.9 %copy-start.1 = (bf16[1,128,2048]{2,1,0:T(8,128)(2,1)S(1)}, bf16[1,128,2048]{2,1,0:T(8,128)(2,1)}, u32[]{:S(2)}) copy-start(bf16[1,128,2048]{2,1,0:T(8,128)(2,1)} %in_ref.5) | copy-start | bytes 1572868
  2.8 18.9 %copy-start.4 = (bf16[1,128,2048]{2,1,0:T(8,128)(2,1)S(1)}, bf16[1,128,2048]{2,1,0:T(8,128)(2,1)}, u32[]{:S(2)}) copy-start(bf16[1,128,2048]{2,1,0:T(8,128)(2,1)} %refs_1_.1) | copy-start | bytes 1572868
  2.8 18.9 %copy-start.5 = (bf16[1,128,2048]{2,1,0:T(8,128)(2,1)S(1)}, bf16[1,128,2048]{2,1,0:T(8,128)(2,1)}, u32[]{:S(2)}) copy-start(bf16[1,128,2048]{2,1,0:T(8,128)(2,1)} %refs_2_.1) | copy-start | bytes 1572868
  2.9 16.2 %collective-permute-start = (bf16[1,128,4096]{2,1,0:T(8,128)(2,1)S(1)}, bf16[1,128,4096]{2,1,0:T(8,128)(2,1)S(1)}, u32[]{:S(2)}, u32[]{:S(2)}) collective-permute-start(bf16[1,128,4096]{2,1,0:T(8,128)(2,1)S(1)} %constant_dynamic-update-slice_fusion), channel_id=1, source_target_pairs={{0,1},{1,4},{4,5},{5,8},{8,9},{9,12},{12,13},{2,3},{3,6},{6,7},{7,... | collective-permute-start | bytes 3145736 | tf_op jit(solution)/shard_map/ppermute | solution.py:28
  7.5 36.9 %collective-permute-start.9 = (bf16[2,512,768]{2,1,0:T(8,128)(2,1)}, bf16[2,512,768]{2,1,0:T(8,128)(2,1)S(1)}, u32[]{:S(2)}, u32[]{:S(2)}) collective-permute-start(bf16[2,512,768]{2,1,0:T(8,128)(2,1)} %prepare.1.refs_8_.refs_1_), channel_id=1, source_target_pairs={{0,2},{2,0},{1,3},{3,1},{4,6},{6,4},{5,7},{7,5},{8,10},{10,8},{9,1... | collective-permute-start | bytes 4718600 | tf_op jit(solution)/shard_map/ppermute | solution.py:22
  19.1 13.7 %collective-permute-start.1 = (bf16[80,2048]{1,0:T(8,128)(2,1)S(1)}, bf16[80,2048]{1,0:T(8,128)(2,1)S(1)}, u32[]{:S(2)}, u32[]{:S(2)}) collective-permute-start(bf16[80,2048]{1,0:T(8,128)(2,1)S(1)} %get-tuple-element.43), channel_id=1, source_target_pairs={{0,8},{4,12},{8,0},{12,4},{1,9},{5,13},{9,1},{13,5},{2,10},{6,14},... | collective-permute-start | bytes 983048 | tf_op jit(solution)/shard_map/ppermute | solution.py:22
  21.8 22.6 %copy-start = (bf16[2,512,768]{2,1,0:T(8,128)(2,1)S(1)}, bf16[2,512,768]{2,1,0:T(8,128)(2,1)}, u32[]{:S(2)}) copy-start(bf16[2,512,768]{2,1,0:T(8,128)(2,1)} %prepare.1.refs_8_.refs_1_) | copy-start | bytes 4718596
  32.8 24.9 %collective-permute-start.4 = (bf16[80,2048]{1,0:T(8,128)(2,1)S(1)}, bf16[80,2048]{1,0:T(8,128)(2,1)S(1)}, u32[]{:S(2)}, u32[]{:S(2)}) collective-permute-start(bf16[80,2048]{1,0:T(8,128)(2,1)S(1)} %get-tuple-element.50), channel_id=1, source_target_pairs={{0,12},{4,8},{8,4},{12,0},{1,13},{5,9},{9,5},{13,1},{2,14},{6,10},... | collective-permute-start | bytes 983048 | tf_op jit(solution)/shard_map/ppermute | solution.py:22
  35.0 26.6 %collective-permute-start.3 = (bf16[80,2048]{1,0:T(8,128)(2,1)S(1)}, bf16[80,2048]{1,0:T(8,128)(2,1)S(1)}, u32[]{:S(2)}, u32[]{:S(2)}) collective-permute-start(bf16[80,2048]{1,0:T(8,128)(2,1)S(1)} %get-tuple-element.48), channel_id=1, source_target_pairs={{0,8},{4,12},{8,0},{12,4},{1,9},{5,13},{9,1},{13,5},{2,10},{6,14},... | collective-permute-start | bytes 983048 | tf_op jit(solution)/shard_map/ppermute | solution.py:22
  39.3 22.3 %collective-permute-start.2 = (bf16[80,2048]{1,0:T(8,128)(2,1)S(1)}, bf16[80,2048]{1,0:T(8,128)(2,1)S(1)}, u32[]{:S(2)}, u32[]{:S(2)}) collective-permute-start(bf16[80,2048]{1,0:T(8,128)(2,1)S(1)} %get-tuple-element.46), channel_id=1, source_target_pairs={{0,4},{4,0},{8,12},{12,8},{1,5},{5,1},{9,13},{13,9},{2,6},{6,2},{1... | collective-permute-start | bytes 983048 | tf_op jit(solution)/shard_map/ppermute | solution.py:22
  39.3 22.8 %collective-permute-start.6 = (bf16[1,512,768]{2,1,0:T(8,128)(2,1)S(1)}, bf16[1,512,768]{2,1,0:T(8,128)(2,1)S(1)}, u32[]{:S(2)}, u32[]{:S(2)}) collective-permute-start(bf16[1,512,768]{2,1,0:T(8,128)(2,1)S(1)} %copy-done.2), channel_id=1, source_target_pairs={{0,2},{2,0},{1,3},{3,1},{4,6},{6,4},{5,7},{7,5},{8,10},{10,8},{9,1... | collective-permute-start | bytes 2359304 | tf_op jit(solution)/shard_map/ppermute | solution.py:22
  44.4 22.8 %collective-permute-start.8 = (bf16[2,512,768]{2,1,0:T(8,128)(2,1)S(1)}, bf16[2,512,768]{2,1,0:T(8,128)(2,1)S(1)}, u32[]{:S(2)}, u32[]{:S(2)}) collective-permute-start(bf16[2,512,768]{2,1,0:T(8,128)(2,1)S(1)} %copy-done), channel_id=1, source_target_pairs={{0,1},{1,0},{2,3},{3,2},{4,5},{5,4},{6,7},{7,6},{8,9},{9,8},{10,11... | collective-permute-start | bytes 4718600 | tf_op jit(solution)/shard_map/ppermute | solution.py:22
  61.6 5.7 %collective-permute-start.10 = (bf16[2,512,768]{2,1,0:T(8,128)(2,1)S(1)}, bf16[2,512,768]{2,1,0:T(8,128)(2,1)S(1)}, u32[]{:S(2)}, u32[]{:S(2)}) collective-permute-start(bf16[2,512,768]{2,1,0:T(8,128)(2,1)S(1)} %collective-permute-done.9.refs_10_.refs_3_), channel_id=1, source_target_pairs={{0,1},{1,0},{2,3},{3,2},{4,5},{5,4},{6,7},{7,6},{8,9},{9,8},{10,11... | collective-permute-start | bytes 4718600 | tf_op jit(solution)/shard_map/ppermute | solution.py:22
  61.6 4.5 %collective-permute-start.5 = (bf16[1,512,768]{2,1,0:T(8,128)(2,1)S(1)}, bf16[1,512,768]{2,1,0:T(8,128)(2,1)S(1)}, u32[]{:S(2)}, u32[]{:S(2)}) collective-permute-start(bf16[1,512,768]{2,1,0:T(8,128)(2,1)S(1)} %copy-done.2), channel_id=1, source_target_pairs={{0,1},{1,0},{2,3},{3,2},{4,5},{5,4},{6,7},{7,6},{8,9},{9,8},{10,11... | collective-permute-start | bytes 2359304 | tf_op jit(solution)/shard_map/ppermute | solution.py:22
  62.1 5.1 %collective-permute-start.7 = (bf16[1,512,768]{2,1,0:T(8,128)(2,1)S(1)}, bf16[1,512,768]{2,1,0:T(8,128)(2,1)S(1)}, u32[]{:S(2)}, u32[]{:S(2)}) collective-permute-start(bf16[1,512,768]{2,1,0:T(8,128)(2,1)S(1)} %collective-permute-done.6.refs_6_), channel_id=1, source_target_pairs={{0,1},{1,0},{2,3},{3,2},{4,5},{5,4},{6,7},{7,6},{8,9},{9,8},{10,11... | collective-permute-start | bytes 2359304 | tf_op jit(solution)/shard_map/ppermute | solution.py:22
  62.1 17.5 %collective-permute-start.15 = (bf16[80,2048]{1,0:T(8,128)(2,1)S(1)}, bf16[80,2048]{1,0:T(8,128)(2,1)S(1)}, u32[]{:S(2)}, u32[]{:S(2)}) collective-permute-start(bf16[80,2048]{1,0:T(8,128)(2,1)S(1)} %get-tuple-element.65), channel_id=1, source_target_pairs={{0,12},{4,8},{8,4},{12,0},{1,13},{5,9},{9,5},{13,1},{2,14},{6,10},... | collective-permute-start | bytes 983048 | tf_op jit(solution)/shard_map/ppermute | solution.py:22
  69.5 19.1 %collective-permute-start.14 = (bf16[80,2048]{1,0:T(8,128)(2,1)S(1)}, bf16[80,2048]{1,0:T(8,128)(2,1)S(1)}, u32[]{:S(2)}, u32[]{:S(2)}) collective-permute-start(bf16[80,2048]{1,0:T(8,128)(2,1)S(1)} %get-tuple-element.63), channel_id=1, source_target_pairs={{0,4},{4,0},{8,12},{12,8},{1,5},{5,1},{9,13},{13,9},{2,6},{6,2},{1... | collective-permute-start | bytes 983048 | tf_op jit(solution)/shard_map/ppermute | solution.py:22
  73.7 22.1 %collective-permute-start.11 = (bf16[80,2048]{1,0:T(8,128)(2,1)S(1)}, bf16[80,2048]{1,0:T(8,128)(2,1)S(1)}, u32[]{:S(2)}, u32[]{:S(2)}) collective-permute-start(bf16[80,2048]{1,0:T(8,128)(2,1)S(1)} %get-tuple-element.57), channel_id=1, source_target_pairs={{0,4},{4,0},{8,12},{12,8},{1,5},{5,1},{9,13},{13,9},{2,6},{6,2},{1... | collective-permute-start | bytes 983048 | tf_op jit(solution)/shard_map/ppermute | solution.py:22
  73.8 23.2 %collective-permute-start.12 = (bf16[80,2048]{1,0:T(8,128)(2,1)S(1)}, bf16[80,2048]{1,0:T(8,128)(2,1)S(1)}, u32[]{:S(2)}, u32[]{:S(2)}) collective-permute-start(bf16[80,2048]{1,0:T(8,128)(2,1)S(1)} %get-tuple-element.58), channel_id=1, source_target_pairs={{0,8},{4,12},{8,0},{12,4},{1,9},{5,13},{9,1},{13,5},{2,10},{6,14},... | collective-permute-start | bytes 983048 | tf_op jit(solution)/shard_map/ppermute | solution.py:22
  76.3 31.5 %collective-permute-start.13 = (bf16[80,2048]{1,0:T(8,128)(2,1)S(1)}, bf16[80,2048]{1,0:T(8,128)(2,1)S(1)}, u32[]{:S(2)}, u32[]{:S(2)}) collective-permute-start(bf16[80,2048]{1,0:T(8,128)(2,1)S(1)} %get-tuple-element.59), channel_id=1, source_target_pairs={{0,12},{4,8},{8,4},{12,0},{1,13},{5,9},{9,5},{13,1},{2,14},{6,10},... | collective-permute-start | bytes 983048 | tf_op jit(solution)/shard_map/ppermute | solution.py:22
  88.6 19.1 %copy-start.9 = (f32[1,128,2]{1,2,0:T(2,128)S(1)}, f32[1,128,2]{1,2,0:T(2,128)}, u32[]{:S(2)}) copy-start(f32[1,128,2]{1,2,0:T(2,128)} %param.19) | copy-start | bytes 3076
  91.9 21.1 %collective-permute-start.16 = (bf16[80,2048]{1,0:T(8,128)(2,1)S(1)}, bf16[80,2048]{1,0:T(8,128)(2,1)S(1)}, u32[]{:S(2)}, u32[]{:S(2)}) collective-permute-start(bf16[80,2048]{1,0:T(8,128)(2,1)S(1)} %get-tuple-element.69), channel_id=1, source_target_pairs={{0,4},{4,0},{8,12},{12,8},{1,5},{5,1},{9,13},{13,9},{2,6},{6,2},{1... | collective-permute-start | bytes 983048 | tf_op jit(solution)/shard_map/ppermute | solution.py:22
  94.4 33.3 %collective-permute-start.17 = (bf16[80,2048]{1,0:T(8,128)(2,1)S(1)}, bf16[80,2048]{1,0:T(8,128)(2,1)S(1)}, u32[]{:S(2)}, u32[]{:S(2)}) collective-permute-start(bf16[80,2048]{1,0:T(8,128)(2,1)S(1)} %get-tuple-element.70), channel_id=1, source_target_pairs={{0,8},{4,12},{8,0},{12,4},{1,9},{5,13},{9,1},{13,5},{2,10},{6,14},... | collective-permute-start | bytes 983048 | tf_op jit(solution)/shard_map/ppermute | solution.py:22
  95.8 39.7 %collective-permute-start.18 = (bf16[80,2048]{1,0:T(8,128)(2,1)S(1)}, bf16[80,2048]{1,0:T(8,128)(2,1)S(1)}, u32[]{:S(2)}, u32[]{:S(2)}) collective-permute-start(bf16[80,2048]{1,0:T(8,128)(2,1)S(1)} %get-tuple-element.73), channel_id=1, source_target_pairs={{0,12},{4,8},{8,4},{12,0},{1,13},{5,9},{9,5},{13,1},{2,14},{6,10},... | collective-permute-start | bytes 983048 | tf_op jit(solution)/shard_map/ppermute | solution.py:22
  (6 other events, 84.9 us)

commit v7 on v6

--- a/solution.py
+++ b/solution.py
@@ -242,7 +242,7 @@
 
 
 def near_grad_kernel(ids_ref, weight_ref, in_ref, att_ref, *refs):
-    backs, sum_ref, rms_ref = refs[:-2], refs[-2], refs[-1]
+    backs, sum_ref, rms_ref, place_ref, share_ref = refs[:-4], refs[-4], refs[-3], refs[-2], refs[-1]
     tok, width = in_ref.shape[1], in_ref.shape[2]
     step, cache = 512, []
     squares = jnp.zeros((tok, 1), F32)
@@ -252,28 +252,37 @@
         sum_ref[:, at] = mixed(ids_ref, weight_ref, backs, range(len(backs)), at, cache)
         squares = squares + (resid * resid).sum(axis=1, keepdims=True)
     rms_ref[...] = jnp.broadcast_to(lax.rsqrt(squares / width + 1e-06), rms_ref.shape)
-
-
-def grad_kernel(ids_ref, weight_ref, in_ref, att_ref, gain_ref, up_ref, sum_ref, rms_ref, *refs):
-    backs, out_ref, gained_ref = refs[:-2], refs[-2], refs[-1]
+    first, second, slot = routing(ids_ref[0, 0:1], ids_ref[0, 1:2], lax.axis_index("expert"))
+    last = len(backs)
+    place_ref[...] = placing(slot, last, 0).astype(BF)
+    gates = [column(weight_ref[0, j : j + 1]) for j in range(2)]
+    share = jnp.where(first == last, gates[0], 0.0) + jnp.where(second == last, gates[1], 0.0)
+    share_ref[...] = jnp.broadcast_to(share, share_ref.shape)
+
+
+def grad_kernel(in_ref, att_ref, gain_ref, up_ref, sum_ref, rms_ref, place_ref, share_ref, back_ref, out_hbm, *refs):
+    gained_ref, out_ref, sems = refs
     tok, width = in_ref.shape[1], in_ref.shape[2]
-    step, cache = 512, []
-    kinds = range(lax.axis_size("expert") - len(backs), lax.axis_size("expert"))
+    step = 512
+    place, share = place_ref[:, : back_ref.shape[0]], share_ref[:, 0:1]
     cross = jnp.zeros((tok, 1), F32)
     for n in range(width // step):
         at = slice(n * step, (n + 1) * step)
         resid = in_ref[0, :, at].astype(F32) + att_ref[:, at].astype(F32)
-        gained = gain_ref[:, at] * (sum_ref[:, at] + mixed(ids_ref, weight_ref, backs, kinds, at, cache))
+        gained = gain_ref[:, at] * (sum_ref[:, at] + share * dot(place, back_ref[:, at]))
         gained_ref[:, at] = gained
         cross = cross + (resid * gained).sum(axis=1, keepdims=True)
     inv_rms = rms_ref[:, 0:1]
     pull = inv_rms * inv_rms * inv_rms * (cross / width)
+    copies = []
     for n in range(width // step):
         at = slice(n * step, (n + 1) * step)
         resid = in_ref[0, :, at].astype(F32) + att_ref[:, at].astype(F32)
-        out_ref[0, :, at] = (
-            up_ref[0, :, at].astype(F32) + inv_rms * gained_ref[:, at] - resid * pull
-        ).astype(BF)
+        out_ref[:, at] = (up_ref[0, :, at].astype(F32) + inv_rms * gained_ref[:, at] - resid * pull).astype(BF)
+        copies.append(pltpu.make_async_copy(out_ref.at[:, at], out_hbm.at[0, :, at], sems.at[n]))
+        copies[-1].start()
+    for copy in copies:
+        copy.wait()
 
 
 def shards(
@@ -353,13 +362,13 @@
         compiler_params=params(16),
         name="attend",
     )(queries, keys, values, previous, previous, doc_ids, inputs, gain, ids)
-    rows = exchanged([after(block, grads[-1]) for block in sent_rows])
+    rows = exchanged([after(block, grads[-1]) if k != peers - 1 else block for k, block in enumerate(sent_rows)])
 
     all_gates, all_others = [w_gate, over_core(after(w_gate, attended))], [own_others, over_core(after(own_others, attended))]
     for gate, other in zip(gates_x, others_x):
         all_gates += [gate, over_core(after(gate, *rows[1:]))]
         all_others += [other, over_core(after(other, *rows[1:]))]
-    grads.append(swapped(after(sent_grads[-1], *rows[2:]), "expert", peers - 1))
+    grads.append(swapped(after(sent_grads[-1], rows[1]), "expert", peers - 1))
 
     wide = jax.ShapeDtypeStruct((total, hidden_count), F32)
     x_scratch = pltpu.VMEM((pieces, total, w_gate.shape[1]), BF)
@@ -392,16 +401,26 @@
         compiler_params=params(32),
         name="layer",
     )(ids, gates, inputs, attended, *back_out)
-    near = peers - 1
-    near_sum, inv_rms = call(
+    flat = jax.ShapeDtypeStruct((tok, 128), F32)
+    near_sum, inv_rms, place, share = call(
         near_grad_kernel,
         "near_grad",
-        [jax.ShapeDtypeStruct((tok, width), F32), jax.ShapeDtypeStruct((tok, 128), F32)],
-        4 + near,
-    )(ids, gates, inputs, after(attended, layer_out), *back_grad[:near])
-    input_grad = call(
-        grad_kernel, "grad", out_block, 8 + peers - near, [pltpu.VMEM((tok, width), F32)]
-    )(ids, gates, inputs, attended, gain, out_grad, near_sum, inv_rms, *back_grad[near:])
+        [jax.ShapeDtypeStruct((tok, width), F32), flat, jax.ShapeDtypeStruct((tok, 128), BF), flat],
+        3 + peers,
+    )(ids, gates, inputs, after(attended, layer_out), *back_grad[:-1])
+    input_grad = pl.pallas_call(
+        grad_kernel,
+        out_shape=out_block,
+        in_specs=[VM] * 9,
+        out_specs=pl.BlockSpec(memory_space=pl.ANY),
+        scratch_shapes=[
+            pltpu.VMEM((tok, width), F32),
+            pltpu.VMEM((tok, width), BF),
+            pltpu.SemaphoreType.DMA((width // 512,)),
+        ],
+        compiler_params=params(16),
+        name="grad",
+    )(inputs, attended, gain, out_grad, near_sum, inv_rms, place, share, back_grad[-1])
     return layer_out, input_grad
 
 

time: 138 us -> 137 us (level)
  starting transfers between devices: 26.2 us -> 23.9 us
  waiting for transfers between devices: 85.6 us -> 87.5 us
    ppermute x18, starting transfers between devices: 24.1 us -> 21.9 us  [swapped(): return lax.ppermute(block, axis, [(i, i ^ distance) for i in range(count)])]
    ppermute x18, waiting for transfers between devices: 75.6 us -> 77.4 us  [swapped(): return lax.ppermute(block, axis, [(i, i ^ distance) for i in range(count)])]
where the time goes in v7:
time: 137 us
  waiting for transfers between devices  87.5 us (64%)
  starting transfers between devices  23.9 us (17%)
  Pallas kernels  22.4 us (16%)
  local copies, waits for them, and re-layouts  2.22 us (2%)
    ppermute x18, waiting for transfers between devices, swapped(): return lax.ppermute(block, axis, [(i, i ^ distance) for i in range(count)])  77.4 us
    ppermute x18, starting transfers between devices, swapped(): return lax.ppermute(block, axis, [(i, i ^ distance) for i in range(count)])  21.9 us
    ppermute x1, waiting for transfers between devices, shifted(): return lax.ppermute(block, axis, route)  10.1 us
    pallas_call x1, Pallas kernels, shards(): pl.pallas_call(lambda *refs: attend_kernel(slots, *refs), out_shape=[jax....  7.52 us
    pallas_call x1, Pallas kernels, shards(): call(lambda *refs: backward_kernel(len(grads), pieces, slots, *refs), 'ba...  3.22 us
  transfers between devices with their start and end apart: 19, of which 15 were waited for; matrix products, arithmetic and copies ran while one was open for 0% of the time, Pallas kernels for 15%

profile of v7, /device:TPU:10, one launch (start us, length us, event | category | flops | bytes accessed | tf_op | source)
XLA Modules:
  0.0 136.9 jit_solution(9387299612467661331)
XLA Ops:
  2.9 2.1 %collective-permute-start = (bf16[1,128,4096]{2,1,0:T(8,128)(2,1)S(1)}, bf16[1,128,4096]{2,1,0:T(8,128)(2,1)S(1)}, u32[]{:S(2)}, u32[]{:S(2)}) collective-permute-start(bf16[1,128,4096]{2,1,0:T(8,128)(2,1)S(1)} %constant_dynamic-update-slice_fusion), channel_id=1, source_target_pairs={{0,1},{1,4},{4,5},{5,8},{8,9},{9,12},{12,13},{2,3},{3,6},{6,7},{7,... | collective-permute-start | bytes 3145736 | tf_op jit(solution)/shard_map/ppermute | solution.py:28
  4.9 2.6 %prepare.1.refs_8_.refs_1_ = bf16[2,512,768]{2,1,0:T(8,128)(2,1)} custom-call(bf16[1,512,768]{2,1,0:T(8,128)(2,1)} %u_hbm.1, bf16[1,768,512]{2,1,0:T(8,128)(2,1)} %d_hbm), custom_call_target="tpu_custom_call" | custom-call | tf_op jit(solution)/shard_map/prepare/pallas_call | solution.py:326
  9.1 10.1 %collective-permute-done.refs_3_.refs_4_ = bf16[1,128,4096]{2,1,0:T(8,128)(2,1)S(1)} collective-permute-done((bf16[1,128,4096]{2,1,0:T(8,128)(2,1)S(1)}, bf16[1,128,4096]{2,1,0:T(8,128)(2,1)S(1)}, u32[]{:S(2)}, u32[]{:S(2)}) %collective-permute-start) | collective-permute-done | bytes 1048608 | tf_op jit(solution)/shard_map/ppermute | solution.py:28
  19.1 2.6 %collective-permute-start.1 = (bf16[80,2048]{1,0:T(8,128)(2,1)S(1)}, bf16[80,2048]{1,0:T(8,128)(2,1)S(1)}, u32[]{:S(2)}, u32[]{:S(2)}) collective-permute-start(bf16[80,2048]{1,0:T(8,128)(2,1)S(1)} %get-tuple-element.44), channel_id=1, source_target_pairs={{0,8},{4,12},{8,0},{12,4},{1,9},{5,13},{9,1},{13,5},{2,10},{6,14},... | collective-permute-start | bytes 983048 | tf_op jit(solution)/shard_map/ppermute | solution.py:22
  21.8 7.5 %attend.1 = (bf16[128,2048]{1,0:T(8,128)(2,1)S(1)}, bf16[80,2048]{1,0:T(8,128)(2,1)S(1)}, bf16[80,2048]{1,0:T(8,128)(2,1)S(1)}, bf16[80,2048]{1,0:T(8,128)(2,1)S(1)}, bf16[80,2048]{1,0:T(8,128)(2,1)S(1)}) custom-call(bf16[1,128,2048]{2,1,0:T(8,128)(2,1)S(1)} %copy-done.6, bf16[1,128,2048]{2,1,0:T(8,128)(2,1)S(1)} %copy-done.4, ...), custom_call_target="tpu_custom_call" | custom-call | tf_op jit(solution)/shard_map/attend/pallas_call | solution.py:354
  29.4 12.8 %collective-permute-done.1.refs_2_ = bf16[80,2048]{1,0:T(8,128)(2,1)S(1)} collective-permute-done((bf16[80,2048]{1,0:T(8,128)(2,1)S(1)}, bf16[80,2048]{1,0:T(8,128)(2,1)S(1)}, u32[]{:S(2)}, u32[]{:S(2)}) %collective-permute-start.1) | collective-permute-done | bytes 327712 | tf_op jit(solution)/shard_map/ppermute | solution.py:22
  42.2 3.4 %collective-permute-start.3 = (bf16[80,2048]{1,0:T(8,128)(2,1)S(1)}, bf16[80,2048]{1,0:T(8,128)(2,1)S(1)}, u32[]{:S(2)}, u32[]{:S(2)}) collective-permute-start(bf16[80,2048]{1,0:T(8,128)(2,1)S(1)} %get-tuple-element.49), channel_id=1, source_target_pairs={{0,8},{4,12},{8,0},{12,4},{1,9},{5,13},{9,1},{13,5},{2,10},{6,14},... | collective-permute-start | bytes 983048 | tf_op jit(solution)/shard_map/ppermute | solution.py:22
  45.6 2.5 %collective-permute-start.2 = (bf16[80,2048]{1,0:T(8,128)(2,1)S(1)}, bf16[80,2048]{1,0:T(8,128)(2,1)S(1)}, u32[]{:S(2)}, u32[]{:S(2)}) collective-permute-start(bf16[80,2048]{1,0:T(8,128)(2,1)S(1)} %get-tuple-element.47), channel_id=1, source_target_pairs={{0,4},{4,0},{8,12},{12,8},{1,5},{5,1},{9,13},{13,9},{2,6},{6,2},{1... | collective-permute-start | bytes 983048 | tf_op jit(solution)/shard_map/ppermute | solution.py:22
  48.6 8.5 %collective-permute-done.4.refs_3_ = bf16[80,2048]{1,0:T(8,128)(2,1)S(1)} collective-permute-done((bf16[80,2048]{1,0:T(8,128)(2,1)S(1)}, bf16[80,2048]{1,0:T(8,128)(2,1)S(1)}, u32[]{:S(2)}, u32[]{:S(2)}) %collective-permute-start.4) | collective-permute-done | bytes 327712 | tf_op jit(solution)/shard_map/ppermute | solution.py:22
  57.1 3.8 %collective-permute-done.3.refs_2_ = bf16[80,2048]{1,0:T(8,128)(2,1)S(1)} collective-permute-done((bf16[80,2048]{1,0:T(8,128)(2,1)S(1)}, bf16[80,2048]{1,0:T(8,128)(2,1)S(1)}, u32[]{:S(2)}, u32[]{:S(2)}) %collective-permute-start.3) | collective-permute-done | bytes 327712 | tf_op jit(solution)/shard_map/ppermute | solution.py:22
  63.5 1.9 %collective-permute-done.5.refs_5_ = bf16[1,512,768]{2,1,0:T(8,128)(2,1)S(1)} collective-permute-done((bf16[1,512,768]{2,1,0:T(8,128)(2,1)S(1)}, bf16[1,512,768]{2,1,0:T(8,128)(2,1)S(1)}, u32[]{:S(2)}, u32[]{:S(2)}) %collective-permute-start.5) | collective-permute-done | bytes 786464 | tf_op jit(solution)/shard_map/ppermute | solution.py:22
  66.5 2.3 %hidden.1 = (bf16[320,768]{1,0:T(8,128)(2,1)S(1)}, f32[320,768]{1,0:T(8,128)S(1)}, f32[320,768]{1,0:T(8,128)S(1)}) custom-call(bf16[80,2048]{1,0:T(8,128)(2,1)S(1)} %get-tuple-element.45.refs_0_, bf16[80,2048]{1,0:T(8,128)(2,1)S(1)} %collective-permute-done.2.refs_1_, bf16[80,2048]{1,0:T(8,128)(2,1)S(1)} %collective-permute-done.3.refs_2_, ...), custom_call_target="tpu_custom_call" | custom-call | tf_op jit(solution)/shard_map/hidden/pallas_call | solution.py:375
  68.9 3.6 %collective-permute-start.14 = (bf16[80,2048]{1,0:T(8,128)(2,1)S(1)}, bf16[80,2048]{1,0:T(8,128)(2,1)S(1)}, u32[]{:S(2)}, u32[]{:S(2)}) collective-permute-start(bf16[80,2048]{1,0:T(8,128)(2,1)S(1)} %get-tuple-element.63), channel_id=1, source_target_pairs={{0,4},{4,0},{8,12},{12,8},{1,5},{5,1},{9,13},{13,9},{2,6},{6,2},{1... | collective-permute-start | bytes 983048 | tf_op jit(solution)/shard_map/ppermute | solution.py:22
  73.8 1.8 %collective-permute-start.12 = (bf16[80,2048]{1,0:T(8,128)(2,1)S(1)}, bf16[80,2048]{1,0:T(8,128)(2,1)S(1)}, u32[]{:S(2)}, u32[]{:S(2)}) collective-permute-start(bf16[80,2048]{1,0:T(8,128)(2,1)S(1)} %get-tuple-element.58), channel_id=1, source_target_pairs={{0,8},{4,12},{8,0},{12,4},{1,9},{5,13},{9,1},{13,5},{2,10},{6,14},... | collective-permute-start | bytes 983048 | tf_op jit(solution)/shard_map/ppermute | solution.py:22
  75.6 1.6 %collective-permute-start.13 = (bf16[80,2048]{1,0:T(8,128)(2,1)S(1)}, bf16[80,2048]{1,0:T(8,128)(2,1)S(1)}, u32[]{:S(2)}, u32[]{:S(2)}) collective-permute-start(bf16[80,2048]{1,0:T(8,128)(2,1)S(1)} %get-tuple-element.59), channel_id=1, source_target_pairs={{0,12},{4,8},{8,4},{12,0},{1,13},{5,9},{9,5},{13,1},{2,14},{6,10},... | collective-permute-start | bytes 983048 | tf_op jit(solution)/shard_map/ppermute | solution.py:22
  77.2 2.2 %collective-permute-done.15.refs_3_ = bf16[80,2048]{1,0:T(8,128)(2,1)S(1)} collective-permute-done((bf16[80,2048]{1,0:T(8,128)(2,1)S(1)}, bf16[80,2048]{1,0:T(8,128)(2,1)S(1)}, u32[]{:S(2)}, u32[]{:S(2)}) %collective-permute-start.15) | collective-permute-done | bytes 327712 | tf_op jit(solution)/shard_map/ppermute | solution.py:22
  79.5 9.1 %collective-permute-done.14.refs_1_ = bf16[80,2048]{1,0:T(8,128)(2,1)S(1)} collective-permute-done((bf16[80,2048]{1,0:T(8,128)(2,1)S(1)}, bf16[80,2048]{1,0:T(8,128)(2,1)S(1)}, u32[]{:S(2)}, u32[]{:S(2)}) %collective-permute-start.14) | collective-permute-done | bytes 327712 | tf_op jit(solution)/shard_map/ppermute | solution.py:22
  88.6 3.2 %backward.1 = (bf16[80,2048]{1,0:T(8,128)(2,1)S(1)}, bf16[80,2048]{1,0:T(8,128)(2,1)S(1)}, bf16[80,2048]{1,0:T(8,128)(2,1)S(1)}, bf16[80,2048]{1,0:T(8,128)(2,1)S(1)}) custom-call(bf16[80,2048]{1,0:T(8,128)(2,1)S(1)} %get-tuple-element.61.refs_0_, bf16[80,2048]{1,0:T(8,128)(2,1)S(1)} %collective-permute-done.14.refs_1_, ...), custom_call_target="tpu_custom_call" | custom-call | tf_op jit(solution)/shard_map/backward/pallas_call | solution.py:386
  91.8 2.6 %collective-permute-start.16 = (bf16[80,2048]{1,0:T(8,128)(2,1)S(1)}, bf16[80,2048]{1,0:T(8,128)(2,1)S(1)}, u32[]{:S(2)}, u32[]{:S(2)}) collective-permute-start(bf16[80,2048]{1,0:T(8,128)(2,1)S(1)} %get-tuple-element.69), channel_id=1, source_target_pairs={{0,4},{4,0},{8,12},{12,8},{1,5},{5,1},{9,13},{13,9},{2,6},{6,2},{1... | collective-permute-start | bytes 983048 | tf_op jit(solution)/shard_map/ppermute | solution.py:22
  97.0 10.6 %collective-permute-done.13.refs_3_ = bf16[80,2048]{1,0:T(8,128)(2,1)S(1)} collective-permute-done((bf16[80,2048]{1,0:T(8,128)(2,1)S(1)}, bf16[80,2048]{1,0:T(8,128)(2,1)S(1)}, u32[]{:S(2)}, u32[]{:S(2)}) %collective-permute-start.13) | collective-permute-done | bytes 327712 | tf_op jit(solution)/shard_map/ppermute | solution.py:22
  107.6 1.9 %layer.1 = bf16[1,128,2048]{2,1,0:T(8,128)(2,1)} custom-call(s32[1,2,128]{2,1,0:T(2,128)S(1)} %bitcast.7, f32[1,2,128]{2,1,0:T(2,128)S(1)} %bitcast.9, bf16[1,128,2048]{2,1,0:T(8,128)(2,1)S(1)} %copy-done.1, bf16[128,2048]{1,0:T(8,128)(2,1)S(1)} %get-tuple-element.60.att_ref, bf16[80,2048]{1,0:T(8,128)(2,1)S(1)} %get-tuple-element.56.refs_0_, ...), custom_call_target="tpu_custom_call" | custom-call | tf_op jit(solution)/shard_map/layer/pallas_call | solution.py:396
  109.5 3.6 %collective-permute-done.16.refs_1_ = bf16[80,2048]{1,0:T(8,128)(2,1)S(1)} collective-permute-done((bf16[80,2048]{1,0:T(8,128)(2,1)S(1)}, bf16[80,2048]{1,0:T(8,128)(2,1)S(1)}, u32[]{:S(2)}, u32[]{:S(2)}) %collective-permute-start.16) | collective-permute-done | bytes 327712 | tf_op jit(solution)/shard_map/ppermute | solution.py:22
  113.1 14.7 %collective-permute-done.17.refs_2_ = bf16[80,2048]{1,0:T(8,128)(2,1)S(1)} collective-permute-done((bf16[80,2048]{1,0:T(8,128)(2,1)S(1)}, bf16[80,2048]{1,0:T(8,128)(2,1)S(1)}, u32[]{:S(2)}, u32[]{:S(2)}) %collective-permute-start.17) | collective-permute-done | bytes 327712 | tf_op jit(solution)/shard_map/ppermute | solution.py:22
  129.0 6.3 %collective-permute-done.18.back_ref = bf16[80,2048]{1,0:T(8,128)(2,1)S(1)} collective-permute-done((bf16[80,2048]{1,0:T(8,128)(2,1)S(1)}, bf16[80,2048]{1,0:T(8,128)(2,1)S(1)}, u32[]{:S(2)}, u32[]{:S(2)}) %collective-permute-start.18) | collective-permute-done | bytes 327712 | tf_op jit(solution)/shard_map/ppermute | solution.py:22
  (47 shorter events, 14.8 us)
Async XLA Ops:
  2.8 18.9 %copy-start.1 = (bf16[1,128,2048]{2,1,0:T(8,128)(2,1)S(1)}, bf16[1,128,2048]{2,1,0:T(8,128)(2,1)}, u32[]{:S(2)}) copy-start(bf16[1,128,2048]{2,1,0:T(8,128)(2,1)} %in_ref.5) | copy-start | bytes 1572868
  2.8 18.9 %copy-start.4 = (bf16[1,128,2048]{2,1,0:T(8,128)(2,1)S(1)}, bf16[1,128,2048]{2,1,0:T(8,128)(2,1)}, u32[]{:S(2)}) copy-start(bf16[1,128,2048]{2,1,0:T(8,128)(2,1)} %refs_1_.1) | copy-start | bytes 1572868
  2.9 16.2 %collective-permute-start = (bf16[1,128,4096]{2,1,0:T(8,128)(2,1)S(1)}, bf16[1,128,4096]{2,1,0:T(8,128)(2,1)S(1)}, u32[]{:S(2)}, u32[]{:S(2)}) collective-permute-start(bf16[1,128,4096]{2,1,0:T(8,128)(2,1)S(1)} %constant_dynamic-update-slice_fusion), channel_id=1, source_target_pairs={{0,1},{1,4},{4,5},{5,8},{8,9},{9,12},{12,13},{2,3},{3,6},{6,7},{7,... | collective-permute-start | bytes 3145736 | tf_op jit(solution)/shard_map/ppermute | solution.py:28
  7.5 49.6 %collective-permute-start.9 = (bf16[2,512,768]{2,1,0:T(8,128)(2,1)}, bf16[2,512,768]{2,1,0:T(8,128)(2,1)S(1)}, u32[]{:S(2)}, u32[]{:S(2)}) collective-permute-start(bf16[2,512,768]{2,1,0:T(8,128)(2,1)} %prepare.1.refs_8_.refs_1_), channel_id=1, source_target_pairs={{0,2},{2,0},{1,3},{3,1},{4,6},{6,4},{5,7},{7,5},{8,10},{10,8},{9,1... | collective-permute-start | bytes 4718600 | tf_op jit(solution)/shard_map/ppermute | solution.py:22
  19.1 23.0 %collective-permute-start.1 = (bf16[80,2048]{1,0:T(8,128)(2,1)S(1)}, bf16[80,2048]{1,0:T(8,128)(2,1)S(1)}, u32[]{:S(2)}, u32[]{:S(2)}) collective-permute-start(bf16[80,2048]{1,0:T(8,128)(2,1)S(1)} %get-tuple-element.44), channel_id=1, source_target_pairs={{0,8},{4,12},{8,0},{12,4},{1,9},{5,13},{9,1},{13,5},{2,10},{6,14},... | collective-permute-start | bytes 983048 | tf_op jit(solution)/shard_map/ppermute | solution.py:22
  21.8 26.3 %copy-start.2 = (bf16[1,512,768]{2,1,0:T(8,128)(2,1)S(1)}, bf16[1,512,768]{2,1,0:T(8,128)(2,1)}, u32[]{:S(2)}) copy-start(bf16[1,512,768]{2,1,0:T(8,128)(2,1)} %refs_4_.3) | copy-start | bytes 2359300
  21.8 35.3 %copy-start = (bf16[2,512,768]{2,1,0:T(8,128)(2,1)S(1)}, bf16[2,512,768]{2,1,0:T(8,128)(2,1)}, u32[]{:S(2)}) copy-start(bf16[2,512,768]{2,1,0:T(8,128)(2,1)} %prepare.1.refs_8_.refs_1_) | copy-start | bytes 4718596
  29.3 27.8 %collective-permute-start.4 = (bf16[80,2048]{1,0:T(8,128)(2,1)S(1)}, bf16[80,2048]{1,0:T(8,128)(2,1)S(1)}, u32[]{:S(2)}, u32[]{:S(2)}) collective-permute-start(bf16[80,2048]{1,0:T(8,128)(2,1)S(1)} %get-tuple-element.50), channel_id=1, source_target_pairs={{0,12},{4,8},{8,4},{12,0},{1,13},{5,9},{9,5},{13,1},{2,14},{6,10},... | collective-permute-start | bytes 983048 | tf_op jit(solution)/shard_map/ppermute | solution.py:22
  42.2 18.7 %collective-permute-start.3 = (bf16[80,2048]{1,0:T(8,128)(2,1)S(1)}, bf16[80,2048]{1,0:T(8,128)(2,1)S(1)}, u32[]{:S(2)}, u32[]{:S(2)}) collective-permute-start(bf16[80,2048]{1,0:T(8,128)(2,1)S(1)} %get-tuple-element.49), channel_id=1, source_target_pairs={{0,8},{4,12},{8,0},{12,4},{1,9},{5,13},{9,1},{13,5},{2,10},{6,14},... | collective-permute-start | bytes 983048 | tf_op jit(solution)/shard_map/ppermute | solution.py:22
  45.6 15.3 %collective-permute-start.2 = (bf16[80,2048]{1,0:T(8,128)(2,1)S(1)}, bf16[80,2048]{1,0:T(8,128)(2,1)S(1)}, u32[]{:S(2)}, u32[]{:S(2)}) collective-permute-start(bf16[80,2048]{1,0:T(8,128)(2,1)S(1)} %get-tuple-element.47), channel_id=1, source_target_pairs={{0,4},{4,0},{8,12},{12,8},{1,5},{5,1},{9,13},{13,9},{2,6},{6,2},{1... | collective-permute-start | bytes 983048 | tf_op jit(solution)/shard_map/ppermute | solution.py:22
  48.0 13.9 %collective-permute-start.6 = (bf16[1,512,768]{2,1,0:T(8,128)(2,1)S(1)}, bf16[1,512,768]{2,1,0:T(8,128)(2,1)S(1)}, u32[]{:S(2)}, u32[]{:S(2)}) collective-permute-start(bf16[1,512,768]{2,1,0:T(8,128)(2,1)S(1)} %copy-done.2), channel_id=1, source_target_pairs={{0,2},{2,0},{1,3},{3,1},{4,6},{6,4},{5,7},{7,5},{8,10},{10,8},{9,1... | collective-permute-start | bytes 2359304 | tf_op jit(solution)/shard_map/ppermute | solution.py:22
  57.1 9.4 %collective-permute-start.8 = (bf16[2,512,768]{2,1,0:T(8,128)(2,1)S(1)}, bf16[2,512,768]{2,1,0:T(8,128)(2,1)S(1)}, u32[]{:S(2)}, u32[]{:S(2)}) collective-permute-start(bf16[2,512,768]{2,1,0:T(8,128)(2,1)S(1)} %copy-done), channel_id=1, source_target_pairs={{0,1},{1,0},{2,3},{3,2},{4,5},{5,4},{6,7},{7,6},{8,9},{9,8},{10,11... | collective-permute-start | bytes 4718600 | tf_op jit(solution)/shard_map/ppermute | solution.py:22
  60.9 5.7 %collective-permute-start.10 = (bf16[2,512,768]{2,1,0:T(8,128)(2,1)S(1)}, bf16[2,512,768]{2,1,0:T(8,128)(2,1)S(1)}, u32[]{:S(2)}, u32[]{:S(2)}) collective-permute-start(bf16[2,512,768]{2,1,0:T(8,128)(2,1)S(1)} %collective-permute-done.9.refs_10_.refs_3_), channel_id=1, source_target_pairs={{0,1},{1,0},{2,3},{3,2},{4,5},{5,4},{6,7},{7,6},{8,9},{9,8},{10,11... | collective-permute-start | bytes 4718600 | tf_op jit(solution)/shard_map/ppermute | solution.py:22
  60.9 4.5 %collective-permute-start.5 = (bf16[1,512,768]{2,1,0:T(8,128)(2,1)S(1)}, bf16[1,512,768]{2,1,0:T(8,128)(2,1)S(1)}, u32[]{:S(2)}, u32[]{:S(2)}) collective-permute-start(bf16[1,512,768]{2,1,0:T(8,128)(2,1)S(1)} %copy-done.2), channel_id=1, source_target_pairs={{0,1},{1,0},{2,3},{3,2},{4,5},{5,4},{6,7},{7,6},{8,9},{9,8},{10,11... | collective-permute-start | bytes 2359304 | tf_op jit(solution)/shard_map/ppermute | solution.py:22
  61.9 4.6 %collective-permute-start.7 = (bf16[1,512,768]{2,1,0:T(8,128)(2,1)S(1)}, bf16[1,512,768]{2,1,0:T(8,128)(2,1)S(1)}, u32[]{:S(2)}, u32[]{:S(2)}) collective-permute-start(bf16[1,512,768]{2,1,0:T(8,128)(2,1)S(1)} %collective-permute-done.6.refs_6_), channel_id=1, source_target_pairs={{0,1},{1,0},{2,3},{3,2},{4,5},{5,4},{6,7},{7,6},{8,9},{9,8},{10,11... | collective-permute-start | bytes 2359304 | tf_op jit(solution)/shard_map/ppermute | solution.py:22
  61.9 17.5 %collective-permute-start.15 = (bf16[80,2048]{1,0:T(8,128)(2,1)S(1)}, bf16[80,2048]{1,0:T(8,128)(2,1)S(1)}, u32[]{:S(2)}, u32[]{:S(2)}) collective-permute-start(bf16[80,2048]{1,0:T(8,128)(2,1)S(1)} %get-tuple-element.65), channel_id=1, source_target_pairs={{0,12},{4,8},{8,4},{12,0},{1,13},{5,9},{9,5},{13,1},{2,14},{6,10},... | collective-permute-start | bytes 983048 | tf_op jit(solution)/shard_map/ppermute | solution.py:22
  68.9 19.8 %collective-permute-start.14 = (bf16[80,2048]{1,0:T(8,128)(2,1)S(1)}, bf16[80,2048]{1,0:T(8,128)(2,1)S(1)}, u32[]{:S(2)}, u32[]{:S(2)}) collective-permute-start(bf16[80,2048]{1,0:T(8,128)(2,1)S(1)} %get-tuple-element.63), channel_id=1, source_target_pairs={{0,4},{4,0},{8,12},{12,8},{1,5},{5,1},{9,13},{13,9},{2,6},{6,2},{1... | collective-permute-start | bytes 983048 | tf_op jit(solution)/shard_map/ppermute | solution.py:22
  73.7 22.1 %collective-permute-start.11 = (bf16[80,2048]{1,0:T(8,128)(2,1)S(1)}, bf16[80,2048]{1,0:T(8,128)(2,1)S(1)}, u32[]{:S(2)}, u32[]{:S(2)}) collective-permute-start(bf16[80,2048]{1,0:T(8,128)(2,1)S(1)} %get-tuple-element.57), channel_id=1, source_target_pairs={{0,4},{4,0},{8,12},{12,8},{1,5},{5,1},{9,13},{13,9},{2,6},{6,2},{1... | collective-permute-start | bytes 983048 | tf_op jit(solution)/shard_map/ppermute | solution.py:22
  73.8 23.2 %collective-permute-start.12 = (bf16[80,2048]{1,0:T(8,128)(2,1)S(1)}, bf16[80,2048]{1,0:T(8,128)(2,1)S(1)}, u32[]{:S(2)}, u32[]{:S(2)}) collective-permute-start(bf16[80,2048]{1,0:T(8,128)(2,1)S(1)} %get-tuple-element.58), channel_id=1, source_target_pairs={{0,8},{4,12},{8,0},{12,4},{1,9},{5,13},{9,1},{13,5},{2,10},{6,14},... | collective-permute-start | bytes 983048 | tf_op jit(solution)/shard_map/ppermute | solution.py:22
  75.6 32.0 %collective-permute-start.13 = (bf16[80,2048]{1,0:T(8,128)(2,1)S(1)}, bf16[80,2048]{1,0:T(8,128)(2,1)S(1)}, u32[]{:S(2)}, u32[]{:S(2)}) collective-permute-start(bf16[80,2048]{1,0:T(8,128)(2,1)S(1)} %get-tuple-element.59), channel_id=1, source_target_pairs={{0,12},{4,8},{8,4},{12,0},{1,13},{5,9},{9,5},{13,1},{2,14},{6,10},... | collective-permute-start | bytes 983048 | tf_op jit(solution)/shard_map/ppermute | solution.py:22
  88.6 19.0 %copy-start.9 = (f32[1,128,2]{1,2,0:T(2,128)S(1)}, f32[1,128,2]{1,2,0:T(2,128)}, u32[]{:S(2)}) copy-start(f32[1,128,2]{1,2,0:T(2,128)} %param.19) | copy-start | bytes 3076
  91.8 21.2 %collective-permute-start.16 = (bf16[80,2048]{1,0:T(8,128)(2,1)S(1)}, bf16[80,2048]{1,0:T(8,128)(2,1)S(1)}, u32[]{:S(2)}, u32[]{:S(2)}) collective-permute-start(bf16[80,2048]{1,0:T(8,128)(2,1)S(1)} %get-tuple-element.69), channel_id=1, source_target_pairs={{0,4},{4,0},{8,12},{12,8},{1,5},{5,1},{9,13},{13,9},{2,6},{6,2},{1... | collective-permute-start | bytes 983048 | tf_op jit(solution)/shard_map/ppermute | solution.py:22
  94.4 33.4 %collective-permute-start.17 = (bf16[80,2048]{1,0:T(8,128)(2,1)S(1)}, bf16[80,2048]{1,0:T(8,128)(2,1)S(1)}, u32[]{:S(2)}, u32[]{:S(2)}) collective-permute-start(bf16[80,2048]{1,0:T(8,128)(2,1)S(1)} %get-tuple-element.70), channel_id=1, source_target_pairs={{0,8},{4,12},{8,0},{12,4},{1,9},{5,13},{9,1},{13,5},{2,10},{6,14},... | collective-permute-start | bytes 983048 | tf_op jit(solution)/shard_map/ppermute | solution.py:22
  95.8 39.6 %collective-permute-start.18 = (bf16[80,2048]{1,0:T(8,128)(2,1)S(1)}, bf16[80,2048]{1,0:T(8,128)(2,1)S(1)}, u32[]{:S(2)}, u32[]{:S(2)}) collective-permute-start(bf16[80,2048]{1,0:T(8,128)(2,1)S(1)} %get-tuple-element.75), channel_id=1, source_target_pairs={{0,12},{4,8},{8,4},{12,0},{1,13},{5,9},{9,5},{13,1},{2,14},{6,10},... | collective-permute-start | bytes 983048 | tf_op jit(solution)/shard_map/ppermute | solution.py:22
  (6 other events, 86.2 us)

commit v8 on v7

--- a/solution.py
+++ b/solution.py
@@ -321,7 +321,7 @@
     def over_x(block):
         return [swapped(block, "fsdp", dx) for dx in range(1, lax.axis_size("fsdp"))]
 
-    both = jnp.concatenate([keys, values], 2)
+    both = jnp.pad(keys, ((0, 0), (0, 0), (0, width))) + jnp.pad(values, ((0, 0), (0, 0), (width, 0)))
     previous = shifted(both, ("expert", "ctx"), 1)
     own_others = pl.pallas_call(
         prepare_kernel,

time: 137 us -> 136 us (level)
  local copies, waits for them, and re-layouts: 2.22 us -> 0.06 us
where the time goes in v8:
time: 136 us
  waiting for transfers between devices  87.5 us (64%)
  starting transfers between devices  23.9 us (18%)
  Pallas kernels  22.4 us (16%)
    ppermute x18, waiting for transfers between devices, swapped(): return lax.ppermute(block, axis, [(i, i ^ distance) for i in range(count)])  77.4 us
    ppermute x18, starting transfers between devices, swapped(): return lax.ppermute(block, axis, [(i, i ^ distance) for i in range(count)])  21.9 us
    ppermute x1, waiting for transfers between devices, shifted(): return lax.ppermute(block, axis, route)  10.1 us
    pallas_call x1, Pallas kernels, shards(): pl.pallas_call(lambda *refs: attend_kernel(slots, *refs), out_shape=[jax....  7.52 us
    pallas_call x1, Pallas kernels, shards(): call(lambda *refs: backward_kernel(len(grads), pieces, slots, *refs), 'ba...  3.23 us
  transfers between devices with their start and end apart: 19, of which 15 were waited for; matrix products, arithmetic and copies ran while one was open for 0% of the time, Pallas kernels for 15%

profile of v8, /device:TPU:10, one launch (start us, length us, event | category | flops | bytes accessed | tf_op | source)
XLA Modules:
  0.0 136.0 jit_solution(17304838545255061214)
XLA Ops:
  2.0 2.1 %collective-permute-start = (bf16[1,128,4096]{2,1,0:T(8,128)(2,1)S(1)}, bf16[1,128,4096]{2,1,0:T(8,128)(2,1)S(1)}, u32[]{:S(2)}, u32[]{:S(2)}) collective-permute-start(bf16[1,128,4096]{2,1,0:T(8,128)(2,1)S(1)} %pad_add_fusion), channel_id=1, source_target_pairs={{0,1},{1,4},{4,5},{5,8},{8,9},{9,12},{12,13},{2,3},{3,6},{6,7},{7,... | collective-permute-start | bytes 3145736 | tf_op jit(solution)/shard_map/ppermute | solution.py:28
  4.1 2.6 %prepare.1.refs_8_.refs_1_ = bf16[2,512,768]{2,1,0:T(8,128)(2,1)} custom-call(bf16[1,512,768]{2,1,0:T(8,128)(2,1)} %u_hbm.1, bf16[1,768,512]{2,1,0:T(8,128)(2,1)} %d_hbm), custom_call_target="tpu_custom_call" | custom-call | tf_op jit(solution)/shard_map/prepare/pallas_call | solution.py:326
  8.2 10.1 %collective-permute-done.refs_3_.refs_4_ = bf16[1,128,4096]{2,1,0:T(8,128)(2,1)S(1)} collective-permute-done((bf16[1,128,4096]{2,1,0:T(8,128)(2,1)S(1)}, bf16[1,128,4096]{2,1,0:T(8,128)(2,1)S(1)}, u32[]{:S(2)}, u32[]{:S(2)}) %collective-permute-start) | collective-permute-done | bytes 1048608 | tf_op jit(solution)/shard_map/ppermute | solution.py:28
  18.2 2.6 %collective-permute-start.1 = (bf16[80,2048]{1,0:T(8,128)(2,1)S(1)}, bf16[80,2048]{1,0:T(8,128)(2,1)S(1)}, u32[]{:S(2)}, u32[]{:S(2)}) collective-permute-start(bf16[80,2048]{1,0:T(8,128)(2,1)S(1)} %get-tuple-element.44), channel_id=1, source_target_pairs={{0,8},{4,12},{8,0},{12,4},{1,9},{5,13},{9,1},{13,5},{2,10},{6,14},... | collective-permute-start | bytes 983048 | tf_op jit(solution)/shard_map/ppermute | solution.py:22
  20.9 7.5 %attend.1 = (bf16[128,2048]{1,0:T(8,128)(2,1)S(1)}, bf16[80,2048]{1,0:T(8,128)(2,1)S(1)}, bf16[80,2048]{1,0:T(8,128)(2,1)S(1)}, bf16[80,2048]{1,0:T(8,128)(2,1)S(1)}, bf16[80,2048]{1,0:T(8,128)(2,1)S(1)}) custom-call(bf16[1,128,2048]{2,1,0:T(8,128)(2,1)S(1)} %copy-done.6, bf16[1,128,2048]{2,1,0:T(8,128)(2,1)S(1)} %copy-done.4, ...), custom_call_target="tpu_custom_call" | custom-call | tf_op jit(solution)/shard_map/attend/pallas_call | solution.py:354
  28.5 12.8 %collective-permute-done.1.refs_2_ = bf16[80,2048]{1,0:T(8,128)(2,1)S(1)} collective-permute-done((bf16[80,2048]{1,0:T(8,128)(2,1)S(1)}, bf16[80,2048]{1,0:T(8,128)(2,1)S(1)}, u32[]{:S(2)}, u32[]{:S(2)}) %collective-permute-start.1) | collective-permute-done | bytes 327712 | tf_op jit(solution)/shard_map/ppermute | solution.py:22
  41.3 3.4 %collective-permute-start.3 = (bf16[80,2048]{1,0:T(8,128)(2,1)S(1)}, bf16[80,2048]{1,0:T(8,128)(2,1)S(1)}, u32[]{:S(2)}, u32[]{:S(2)}) collective-permute-start(bf16[80,2048]{1,0:T(8,128)(2,1)S(1)} %get-tuple-element.49), channel_id=1, source_target_pairs={{0,8},{4,12},{8,0},{12,4},{1,9},{5,13},{9,1},{13,5},{2,10},{6,14},... | collective-permute-start | bytes 983048 | tf_op jit(solution)/shard_map/ppermute | solution.py:22
  44.7 2.5 %collective-permute-start.2 = (bf16[80,2048]{1,0:T(8,128)(2,1)S(1)}, bf16[80,2048]{1,0:T(8,128)(2,1)S(1)}, u32[]{:S(2)}, u32[]{:S(2)}) collective-permute-start(bf16[80,2048]{1,0:T(8,128)(2,1)S(1)} %get-tuple-element.47), channel_id=1, source_target_pairs={{0,4},{4,0},{8,12},{12,8},{1,5},{5,1},{9,13},{13,9},{2,6},{6,2},{1... | collective-permute-start | bytes 983048 | tf_op jit(solution)/shard_map/ppermute | solution.py:22
  47.7 8.5 %collective-permute-done.4.refs_3_ = bf16[80,2048]{1,0:T(8,128)(2,1)S(1)} collective-permute-done((bf16[80,2048]{1,0:T(8,128)(2,1)S(1)}, bf16[80,2048]{1,0:T(8,128)(2,1)S(1)}, u32[]{:S(2)}, u32[]{:S(2)}) %collective-permute-start.4) | collective-permute-done | bytes 327712 | tf_op jit(solution)/shard_map/ppermute | solution.py:22
  56.2 3.8 %collective-permute-done.3.refs_2_ = bf16[80,2048]{1,0:T(8,128)(2,1)S(1)} collective-permute-done((bf16[80,2048]{1,0:T(8,128)(2,1)S(1)}, bf16[80,2048]{1,0:T(8,128)(2,1)S(1)}, u32[]{:S(2)}, u32[]{:S(2)}) %collective-permute-start.3) | collective-permute-done | bytes 327712 | tf_op jit(solution)/shard_map/ppermute | solution.py:22
  62.6 1.9 %collective-permute-done.5.refs_5_ = bf16[1,512,768]{2,1,0:T(8,128)(2,1)S(1)} collective-permute-done((bf16[1,512,768]{2,1,0:T(8,128)(2,1)S(1)}, bf16[1,512,768]{2,1,0:T(8,128)(2,1)S(1)}, u32[]{:S(2)}, u32[]{:S(2)}) %collective-permute-start.5) | collective-permute-done | bytes 786464 | tf_op jit(solution)/shard_map/ppermute | solution.py:22
  65.7 2.3 %hidden.1 = (bf16[320,768]{1,0:T(8,128)(2,1)S(1)}, f32[320,768]{1,0:T(8,128)S(1)}, f32[320,768]{1,0:T(8,128)S(1)}) custom-call(bf16[80,2048]{1,0:T(8,128)(2,1)S(1)} %get-tuple-element.45.refs_0_, bf16[80,2048]{1,0:T(8,128)(2,1)S(1)} %collective-permute-done.2.refs_1_, bf16[80,2048]{1,0:T(8,128)(2,1)S(1)} %collective-permute-done.3.refs_2_, ...), custom_call_target="tpu_custom_call" | custom-call | tf_op jit(solution)/shard_map/hidden/pallas_call | solution.py:375
  68.0 3.6 %collective-permute-start.14 = (bf16[80,2048]{1,0:T(8,128)(2,1)S(1)}, bf16[80,2048]{1,0:T(8,128)(2,1)S(1)}, u32[]{:S(2)}, u32[]{:S(2)}) collective-permute-start(bf16[80,2048]{1,0:T(8,128)(2,1)S(1)} %get-tuple-element.63), channel_id=1, source_target_pairs={{0,4},{4,0},{8,12},{12,8},{1,5},{5,1},{9,13},{13,9},{2,6},{6,2},{1... | collective-permute-start | bytes 983048 | tf_op jit(solution)/shard_map/ppermute | solution.py:22
  72.9 1.8 %collective-permute-start.12 = (bf16[80,2048]{1,0:T(8,128)(2,1)S(1)}, bf16[80,2048]{1,0:T(8,128)(2,1)S(1)}, u32[]{:S(2)}, u32[]{:S(2)}) collective-permute-start(bf16[80,2048]{1,0:T(8,128)(2,1)S(1)} %get-tuple-element.58), channel_id=1, source_target_pairs={{0,8},{4,12},{8,0},{12,4},{1,9},{5,13},{9,1},{13,5},{2,10},{6,14},... | collective-permute-start | bytes 983048 | tf_op jit(solution)/shard_map/ppermute | solution.py:22
  74.7 1.6 %collective-permute-start.13 = (bf16[80,2048]{1,0:T(8,128)(2,1)S(1)}, bf16[80,2048]{1,0:T(8,128)(2,1)S(1)}, u32[]{:S(2)}, u32[]{:S(2)}) collective-permute-start(bf16[80,2048]{1,0:T(8,128)(2,1)S(1)} %get-tuple-element.59), channel_id=1, source_target_pairs={{0,12},{4,8},{8,4},{12,0},{1,13},{5,9},{9,5},{13,1},{2,14},{6,10},... | collective-permute-start | bytes 983048 | tf_op jit(solution)/shard_map/ppermute | solution.py:22
  76.4 2.2 %collective-permute-done.15.refs_3_ = bf16[80,2048]{1,0:T(8,128)(2,1)S(1)} collective-permute-done((bf16[80,2048]{1,0:T(8,128)(2,1)S(1)}, bf16[80,2048]{1,0:T(8,128)(2,1)S(1)}, u32[]{:S(2)}, u32[]{:S(2)}) %collective-permute-start.15) | collective-permute-done | bytes 327712 | tf_op jit(solution)/shard_map/ppermute | solution.py:22
  78.6 9.1 %collective-permute-done.14.refs_1_ = bf16[80,2048]{1,0:T(8,128)(2,1)S(1)} collective-permute-done((bf16[80,2048]{1,0:T(8,128)(2,1)S(1)}, bf16[80,2048]{1,0:T(8,128)(2,1)S(1)}, u32[]{:S(2)}, u32[]{:S(2)}) %collective-permute-start.14) | collective-permute-done | bytes 327712 | tf_op jit(solution)/shard_map/ppermute | solution.py:22
  87.7 3.2 %backward.1 = (bf16[80,2048]{1,0:T(8,128)(2,1)S(1)}, bf16[80,2048]{1,0:T(8,128)(2,1)S(1)}, bf16[80,2048]{1,0:T(8,128)(2,1)S(1)}, bf16[80,2048]{1,0:T(8,128)(2,1)S(1)}) custom-call(bf16[80,2048]{1,0:T(8,128)(2,1)S(1)} %get-tuple-element.61.refs_0_, bf16[80,2048]{1,0:T(8,128)(2,1)S(1)} %collective-permute-done.14.refs_1_, ...), custom_call_target="tpu_custom_call" | custom-call | tf_op jit(solution)/shard_map/backward/pallas_call | solution.py:386
  91.0 2.5 %collective-permute-start.16 = (bf16[80,2048]{1,0:T(8,128)(2,1)S(1)}, bf16[80,2048]{1,0:T(8,128)(2,1)S(1)}, u32[]{:S(2)}, u32[]{:S(2)}) collective-permute-start(bf16[80,2048]{1,0:T(8,128)(2,1)S(1)} %get-tuple-element.69), channel_id=1, source_target_pairs={{0,4},{4,0},{8,12},{12,8},{1,5},{5,1},{9,13},{13,9},{2,6},{6,2},{1... | collective-permute-start | bytes 983048 | tf_op jit(solution)/shard_map/ppermute | solution.py:22
  96.1 10.6 %collective-permute-done.13.refs_3_ = bf16[80,2048]{1,0:T(8,128)(2,1)S(1)} collective-permute-done((bf16[80,2048]{1,0:T(8,128)(2,1)S(1)}, bf16[80,2048]{1,0:T(8,128)(2,1)S(1)}, u32[]{:S(2)}, u32[]{:S(2)}) %collective-permute-start.13) | collective-permute-done | bytes 327712 | tf_op jit(solution)/shard_map/ppermute | solution.py:22
  106.7 1.9 %layer.1 = bf16[1,128,2048]{2,1,0:T(8,128)(2,1)} custom-call(s32[1,2,128]{2,1,0:T(2,128)S(1)} %bitcast.7, f32[1,2,128]{2,1,0:T(2,128)S(1)} %bitcast.9, bf16[1,128,2048]{2,1,0:T(8,128)(2,1)S(1)} %copy-done.1, bf16[128,2048]{1,0:T(8,128)(2,1)S(1)} %get-tuple-element.60.att_ref, bf16[80,2048]{1,0:T(8,128)(2,1)S(1)} %get-tuple-element.56.refs_0_, ...), custom_call_target="tpu_custom_call" | custom-call | tf_op jit(solution)/shard_map/layer/pallas_call | solution.py:396
  108.6 3.6 %collective-permute-done.16.refs_1_ = bf16[80,2048]{1,0:T(8,128)(2,1)S(1)} collective-permute-done((bf16[80,2048]{1,0:T(8,128)(2,1)S(1)}, bf16[80,2048]{1,0:T(8,128)(2,1)S(1)}, u32[]{:S(2)}, u32[]{:S(2)}) %collective-permute-start.16) | collective-permute-done | bytes 327712 | tf_op jit(solution)/shard_map/ppermute | solution.py:22
  112.2 14.7 %collective-permute-done.17.refs_2_ = bf16[80,2048]{1,0:T(8,128)(2,1)S(1)} collective-permute-done((bf16[80,2048]{1,0:T(8,128)(2,1)S(1)}, bf16[80,2048]{1,0:T(8,128)(2,1)S(1)}, u32[]{:S(2)}, u32[]{:S(2)}) %collective-permute-start.17) | collective-permute-done | bytes 327712 | tf_op jit(solution)/shard_map/ppermute | solution.py:22
  128.1 6.3 %collective-permute-done.18.back_ref = bf16[80,2048]{1,0:T(8,128)(2,1)S(1)} collective-permute-done((bf16[80,2048]{1,0:T(8,128)(2,1)S(1)}, bf16[80,2048]{1,0:T(8,128)(2,1)S(1)}, u32[]{:S(2)}, u32[]{:S(2)}) %collective-permute-start.18) | collective-permute-done | bytes 327712 | tf_op jit(solution)/shard_map/ppermute | solution.py:22
  (46 shorter events, 13.9 us)
Async XLA Ops:
  1.9 18.9 %copy-start.1 = (bf16[1,128,2048]{2,1,0:T(8,128)(2,1)S(1)}, bf16[1,128,2048]{2,1,0:T(8,128)(2,1)}, u32[]{:S(2)}) copy-start(bf16[1,128,2048]{2,1,0:T(8,128)(2,1)} %in_ref.5) | copy-start | bytes 1572868
  1.9 18.9 %copy-start.4 = (bf16[1,128,2048]{2,1,0:T(8,128)(2,1)S(1)}, bf16[1,128,2048]{2,1,0:T(8,128)(2,1)}, u32[]{:S(2)}) copy-start(bf16[1,128,2048]{2,1,0:T(8,128)(2,1)} %refs_1_.1) | copy-start | bytes 1572868
  2.0 16.2 %collective-permute-start = (bf16[1,128,4096]{2,1,0:T(8,128)(2,1)S(1)}, bf16[1,128,4096]{2,1,0:T(8,128)(2,1)S(1)}, u32[]{:S(2)}, u32[]{:S(2)}) collective-permute-start(bf16[1,128,4096]{2,1,0:T(8,128)(2,1)S(1)} %pad_add_fusion), channel_id=1, source_target_pairs={{0,1},{1,4},{4,5},{5,8},{8,9},{9,12},{12,13},{2,3},{3,6},{6,7},{7,... | collective-permute-start | bytes 3145736 | tf_op jit(solution)/shard_map/ppermute | solution.py:28
  6.6 49.6 %collective-permute-start.9 = (bf16[2,512,768]{2,1,0:T(8,128)(2,1)}, bf16[2,512,768]{2,1,0:T(8,128)(2,1)S(1)}, u32[]{:S(2)}, u32[]{:S(2)}) collective-permute-start(bf16[2,512,768]{2,1,0:T(8,128)(2,1)} %prepare.1.refs_8_.refs_1_), channel_id=1, source_target_pairs={{0,2},{2,0},{1,3},{3,1},{4,6},{6,4},{5,7},{7,5},{8,10},{10,8},{9,1... | collective-permute-start | bytes 4718600 | tf_op jit(solution)/shard_map/ppermute | solution.py:22
  18.2 23.0 %collective-permute-start.1 = (bf16[80,2048]{1,0:T(8,128)(2,1)S(1)}, bf16[80,2048]{1,0:T(8,128)(2,1)S(1)}, u32[]{:S(2)}, u32[]{:S(2)}) collective-permute-start(bf16[80,2048]{1,0:T(8,128)(2,1)S(1)} %get-tuple-element.44), channel_id=1, source_target_pairs={{0,8},{4,12},{8,0},{12,4},{1,9},{5,13},{9,1},{13,5},{2,10},{6,14},... | collective-permute-start | bytes 983048 | tf_op jit(solution)/shard_map/ppermute | solution.py:22
  20.9 26.3 %copy-start.2 = (bf16[1,512,768]{2,1,0:T(8,128)(2,1)S(1)}, bf16[1,512,768]{2,1,0:T(8,128)(2,1)}, u32[]{:S(2)}) copy-start(bf16[1,512,768]{2,1,0:T(8,128)(2,1)} %refs_4_.3) | copy-start | bytes 2359300
  20.9 35.3 %copy-start = (bf16[2,512,768]{2,1,0:T(8,128)(2,1)S(1)}, bf16[2,512,768]{2,1,0:T(8,128)(2,1)}, u32[]{:S(2)}) copy-start(bf16[2,512,768]{2,1,0:T(8,128)(2,1)} %prepare.1.refs_8_.refs_1_) | copy-start | bytes 4718596
  28.4 27.8 %collective-permute-start.4 = (bf16[80,2048]{1,0:T(8,128)(2,1)S(1)}, bf16[80,2048]{1,0:T(8,128)(2,1)S(1)}, u32[]{:S(2)}, u32[]{:S(2)}) collective-permute-start(bf16[80,2048]{1,0:T(8,128)(2,1)S(1)} %get-tuple-element.50), channel_id=1, source_target_pairs={{0,12},{4,8},{8,4},{12,0},{1,13},{5,9},{9,5},{13,1},{2,14},{6,10},... | collective-permute-start | bytes 983048 | tf_op jit(solution)/shard_map/ppermute | solution.py:22
  41.3 18.7 %collective-permute-start.3 = (bf16[80,2048]{1,0:T(8,128)(2,1)S(1)}, bf16[80,2048]{1,0:T(8,128)(2,1)S(1)}, u32[]{:S(2)}, u32[]{:S(2)}) collective-permute-start(bf16[80,2048]{1,0:T(8,128)(2,1)S(1)} %get-tuple-element.49), channel_id=1, source_target_pairs={{0,8},{4,12},{8,0},{12,4},{1,9},{5,13},{9,1},{13,5},{2,10},{6,14},... | collective-permute-start | bytes 983048 | tf_op jit(solution)/shard_map/ppermute | solution.py:22
  44.7 15.3 %collective-permute-start.2 = (bf16[80,2048]{1,0:T(8,128)(2,1)S(1)}, bf16[80,2048]{1,0:T(8,128)(2,1)S(1)}, u32[]{:S(2)}, u32[]{:S(2)}) collective-permute-start(bf16[80,2048]{1,0:T(8,128)(2,1)S(1)} %get-tuple-element.47), channel_id=1, source_target_pairs={{0,4},{4,0},{8,12},{12,8},{1,5},{5,1},{9,13},{13,9},{2,6},{6,2},{1... | collective-permute-start | bytes 983048 | tf_op jit(solution)/shard_map/ppermute | solution.py:22
  47.2 13.9 %collective-permute-start.6 = (bf16[1,512,768]{2,1,0:T(8,128)(2,1)S(1)}, bf16[1,512,768]{2,1,0:T(8,128)(2,1)S(1)}, u32[]{:S(2)}, u32[]{:S(2)}) collective-permute-start(bf16[1,512,768]{2,1,0:T(8,128)(2,1)S(1)} %copy-done.2), channel_id=1, source_target_pairs={{0,2},{2,0},{1,3},{3,1},{4,6},{6,4},{5,7},{7,5},{8,10},{10,8},{9,1... | collective-permute-start | bytes 2359304 | tf_op jit(solution)/shard_map/ppermute | solution.py:22
  56.2 9.4 %collective-permute-start.8 = (bf16[2,512,768]{2,1,0:T(8,128)(2,1)S(1)}, bf16[2,512,768]{2,1,0:T(8,128)(2,1)S(1)}, u32[]{:S(2)}, u32[]{:S(2)}) collective-permute-start(bf16[2,512,768]{2,1,0:T(8,128)(2,1)S(1)} %copy-done), channel_id=1, source_target_pairs={{0,1},{1,0},{2,3},{3,2},{4,5},{5,4},{6,7},{7,6},{8,9},{9,8},{10,11... | collective-permute-start | bytes 4718600 | tf_op jit(solution)/shard_map/ppermute | solution.py:22
  60.0 5.7 %collective-permute-start.10 = (bf16[2,512,768]{2,1,0:T(8,128)(2,1)S(1)}, bf16[2,512,768]{2,1,0:T(8,128)(2,1)S(1)}, u32[]{:S(2)}, u32[]{:S(2)}) collective-permute-start(bf16[2,512,768]{2,1,0:T(8,128)(2,1)S(1)} %collective-permute-done.9.refs_10_.refs_3_), channel_id=1, source_target_pairs={{0,1},{1,0},{2,3},{3,2},{4,5},{5,4},{6,7},{7,6},{8,9},{9,8},{10,11... | collective-permute-start | bytes 4718600 | tf_op jit(solution)/shard_map/ppermute | solution.py:22
  60.0 4.5 %collective-permute-start.5 = (bf16[1,512,768]{2,1,0:T(8,128)(2,1)S(1)}, bf16[1,512,768]{2,1,0:T(8,128)(2,1)S(1)}, u32[]{:S(2)}, u32[]{:S(2)}) collective-permute-start(bf16[1,512,768]{2,1,0:T(8,128)(2,1)S(1)} %copy-done.2), channel_id=1, source_target_pairs={{0,1},{1,0},{2,3},{3,2},{4,5},{5,4},{6,7},{7,6},{8,9},{9,8},{10,11... | collective-permute-start | bytes 2359304 | tf_op jit(solution)/shard_map/ppermute | solution.py:22
  61.0 4.6 %collective-permute-start.7 = (bf16[1,512,768]{2,1,0:T(8,128)(2,1)S(1)}, bf16[1,512,768]{2,1,0:T(8,128)(2,1)S(1)}, u32[]{:S(2)}, u32[]{:S(2)}) collective-permute-start(bf16[1,512,768]{2,1,0:T(8,128)(2,1)S(1)} %collective-permute-done.6.refs_6_), channel_id=1, source_target_pairs={{0,1},{1,0},{2,3},{3,2},{4,5},{5,4},{6,7},{7,6},{8,9},{9,8},{10,11... | collective-permute-start | bytes 2359304 | tf_op jit(solution)/shard_map/ppermute | solution.py:22
  61.0 17.5 %collective-permute-start.15 = (bf16[80,2048]{1,0:T(8,128)(2,1)S(1)}, bf16[80,2048]{1,0:T(8,128)(2,1)S(1)}, u32[]{:S(2)}, u32[]{:S(2)}) collective-permute-start(bf16[80,2048]{1,0:T(8,128)(2,1)S(1)} %get-tuple-element.65), channel_id=1, source_target_pairs={{0,12},{4,8},{8,4},{12,0},{1,13},{5,9},{9,5},{13,1},{2,14},{6,10},... | collective-permute-start | bytes 983048 | tf_op jit(solution)/shard_map/ppermute | solution.py:22
  68.0 19.8 %collective-permute-start.14 = (bf16[80,2048]{1,0:T(8,128)(2,1)S(1)}, bf16[80,2048]{1,0:T(8,128)(2,1)S(1)}, u32[]{:S(2)}, u32[]{:S(2)}) collective-permute-start(bf16[80,2048]{1,0:T(8,128)(2,1)S(1)} %get-tuple-element.63), channel_id=1, source_target_pairs={{0,4},{4,0},{8,12},{12,8},{1,5},{5,1},{9,13},{13,9},{2,6},{6,2},{1... | collective-permute-start | bytes 983048 | tf_op jit(solution)/shard_map/ppermute | solution.py:22
  72.8 22.1 %collective-permute-start.11 = (bf16[80,2048]{1,0:T(8,128)(2,1)S(1)}, bf16[80,2048]{1,0:T(8,128)(2,1)S(1)}, u32[]{:S(2)}, u32[]{:S(2)}) collective-permute-start(bf16[80,2048]{1,0:T(8,128)(2,1)S(1)} %get-tuple-element.57), channel_id=1, source_target_pairs={{0,4},{4,0},{8,12},{12,8},{1,5},{5,1},{9,13},{13,9},{2,6},{6,2},{1... | collective-permute-start | bytes 983048 | tf_op jit(solution)/shard_map/ppermute | solution.py:22
  72.9 23.2 %collective-permute-start.12 = (bf16[80,2048]{1,0:T(8,128)(2,1)S(1)}, bf16[80,2048]{1,0:T(8,128)(2,1)S(1)}, u32[]{:S(2)}, u32[]{:S(2)}) collective-permute-start(bf16[80,2048]{1,0:T(8,128)(2,1)S(1)} %get-tuple-element.58), channel_id=1, source_target_pairs={{0,8},{4,12},{8,0},{12,4},{1,9},{5,13},{9,1},{13,5},{2,10},{6,14},... | collective-permute-start | bytes 983048 | tf_op jit(solution)/shard_map/ppermute | solution.py:22
  74.7 32.0 %collective-permute-start.13 = (bf16[80,2048]{1,0:T(8,128)(2,1)S(1)}, bf16[80,2048]{1,0:T(8,128)(2,1)S(1)}, u32[]{:S(2)}, u32[]{:S(2)}) collective-permute-start(bf16[80,2048]{1,0:T(8,128)(2,1)S(1)} %get-tuple-element.59), channel_id=1, source_target_pairs={{0,12},{4,8},{8,4},{12,0},{1,13},{5,9},{9,5},{13,1},{2,14},{6,10},... | collective-permute-start | bytes 983048 | tf_op jit(solution)/shard_map/ppermute | solution.py:22
  87.7 19.0 %copy-start.9 = (f32[1,128,2]{1,2,0:T(2,128)S(1)}, f32[1,128,2]{1,2,0:T(2,128)}, u32[]{:S(2)}) copy-start(f32[1,128,2]{1,2,0:T(2,128)} %param.19) | copy-start | bytes 3076
  91.0 21.2 %collective-permute-start.16 = (bf16[80,2048]{1,0:T(8,128)(2,1)S(1)}, bf16[80,2048]{1,0:T(8,128)(2,1)S(1)}, u32[]{:S(2)}, u32[]{:S(2)}) collective-permute-start(bf16[80,2048]{1,0:T(8,128)(2,1)S(1)} %get-tuple-element.69), channel_id=1, source_target_pairs={{0,4},{4,0},{8,12},{12,8},{1,5},{5,1},{9,13},{13,9},{2,6},{6,2},{1... | collective-permute-start | bytes 983048 | tf_op jit(solution)/shard_map/ppermute | solution.py:22
  93.5 33.4 %collective-permute-start.17 = (bf16[80,2048]{1,0:T(8,128)(2,1)S(1)}, bf16[80,2048]{1,0:T(8,128)(2,1)S(1)}, u32[]{:S(2)}, u32[]{:S(2)}) collective-permute-start(bf16[80,2048]{1,0:T(8,128)(2,1)S(1)} %get-tuple-element.70), channel_id=1, source_target_pairs={{0,8},{4,12},{8,0},{12,4},{1,9},{5,13},{9,1},{13,5},{2,10},{6,14},... | collective-permute-start | bytes 983048 | tf_op jit(solution)/shard_map/ppermute | solution.py:22
  94.9 39.6 %collective-permute-start.18 = (bf16[80,2048]{1,0:T(8,128)(2,1)S(1)}, bf16[80,2048]{1,0:T(8,128)(2,1)S(1)}, u32[]{:S(2)}, u32[]{:S(2)}) collective-permute-start(bf16[80,2048]{1,0:T(8,128)(2,1)S(1)} %get-tuple-element.75), channel_id=1, source_target_pairs={{0,12},{4,8},{8,4},{12,0},{1,13},{5,9},{9,5},{13,1},{2,14},{6,10},... | collective-permute-start | bytes 983048 | tf_op jit(solution)/shard_map/ppermute | solution.py:22
  (6 other events, 86.2 us)

commit v9 on v8

--- a/solution.py
+++ b/solution.py
@@ -342,7 +342,7 @@
     ]
     gates_x, others_x = over_x(w_gate), over_x(own_others)
 
-    parts = 4
+    parts = 2
     cut = width // parts
 
     def by_part(*dims):

time: 136 us -> 136 us (level)
  no operation moved by 1% of the time
where the time goes in v9:
time: 136 us
  waiting for transfers between devices  87.9 us (65%)
  starting transfers between devices  23.9 us (18%)
  Pallas kernels  22 us (16%)
    ppermute x18, waiting for transfers between devices, swapped(): return lax.ppermute(block, axis, [(i, i ^ distance) for i in range(count)])  77.8 us
    ppermute x18, starting transfers between devices, swapped(): return lax.ppermute(block, axis, [(i, i ^ distance) for i in range(count)])  21.9 us
    ppermute x1, waiting for transfers between devices, shifted(): return lax.ppermute(block, axis, route)  10.1 us
    pallas_call x1, Pallas kernels, shards(): pl.pallas_call(lambda *refs: attend_kernel(slots, *refs), out_shape=[jax....  7.12 us
    pallas_call x1, Pallas kernels, shards(): call(lambda *refs: backward_kernel(len(grads), pieces, slots, *refs), 'ba...  3.23 us
  transfers between devices with their start and end apart: 19, of which 15 were waited for; matrix products, arithmetic and copies ran while one was open for 0% of the time, Pallas kernels for 15%

profile of v9, /device:TPU:10, one launch (start us, length us, event | category | flops | bytes accessed | tf_op | source)
XLA Modules:
  0.0 136.0 jit_solution(13497081455377689500)
XLA Ops:
  2.0 2.1 %collective-permute-start = (bf16[1,128,4096]{2,1,0:T(8,128)(2,1)S(1)}, bf16[1,128,4096]{2,1,0:T(8,128)(2,1)S(1)}, u32[]{:S(2)}, u32[]{:S(2)}) collective-permute-start(bf16[1,128,4096]{2,1,0:T(8,128)(2,1)S(1)} %pad_add_fusion), channel_id=1, source_target_pairs={{0,1},{1,4},{4,5},{5,8},{8,9},{9,12},{12,13},{2,3},{3,6},{6,7},{7,... | collective-permute-start | bytes 3145736 | tf_op jit(solution)/shard_map/ppermute | solution.py:28
  4.1 2.6 %prepare.1.refs_8_.refs_1_ = bf16[2,512,768]{2,1,0:T(8,128)(2,1)} custom-call(bf16[1,512,768]{2,1,0:T(8,128)(2,1)} %u_hbm.1, bf16[1,768,512]{2,1,0:T(8,128)(2,1)} %d_hbm), custom_call_target="tpu_custom_call" | custom-call | tf_op jit(solution)/shard_map/prepare/pallas_call | solution.py:326
  8.2 10.1 %collective-permute-done.refs_3_.refs_4_ = bf16[1,128,4096]{2,1,0:T(8,128)(2,1)S(1)} collective-permute-done((bf16[1,128,4096]{2,1,0:T(8,128)(2,1)S(1)}, bf16[1,128,4096]{2,1,0:T(8,128)(2,1)S(1)}, u32[]{:S(2)}, u32[]{:S(2)}) %collective-permute-start) | collective-permute-done | bytes 1048608 | tf_op jit(solution)/shard_map/ppermute | solution.py:28
  18.2 2.6 %collective-permute-start.1 = (bf16[80,2048]{1,0:T(8,128)(2,1)S(1)}, bf16[80,2048]{1,0:T(8,128)(2,1)S(1)}, u32[]{:S(2)}, u32[]{:S(2)}) collective-permute-start(bf16[80,2048]{1,0:T(8,128)(2,1)S(1)} %get-tuple-element.44), channel_id=1, source_target_pairs={{0,8},{4,12},{8,0},{12,4},{1,9},{5,13},{9,1},{13,5},{2,10},{6,14},... | collective-permute-start | bytes 983048 | tf_op jit(solution)/shard_map/ppermute | solution.py:22
  20.9 7.1 %attend.1 = (bf16[128,2048]{1,0:T(8,128)(2,1)S(1)}, bf16[80,2048]{1,0:T(8,128)(2,1)S(1)}, bf16[80,2048]{1,0:T(8,128)(2,1)S(1)}, bf16[80,2048]{1,0:T(8,128)(2,1)S(1)}, bf16[80,2048]{1,0:T(8,128)(2,1)S(1)}) custom-call(bf16[1,128,2048]{2,1,0:T(8,128)(2,1)S(1)} %copy-done.6, bf16[1,128,2048]{2,1,0:T(8,128)(2,1)S(1)} %copy-done.4, ...), custom_call_target="tpu_custom_call" | custom-call | tf_op jit(solution)/shard_map/attend/pallas_call | solution.py:354
  28.1 13.2 %collective-permute-done.1.refs_2_ = bf16[80,2048]{1,0:T(8,128)(2,1)S(1)} collective-permute-done((bf16[80,2048]{1,0:T(8,128)(2,1)S(1)}, bf16[80,2048]{1,0:T(8,128)(2,1)S(1)}, u32[]{:S(2)}, u32[]{:S(2)}) %collective-permute-start.1) | collective-permute-done | bytes 327712 | tf_op jit(solution)/shard_map/ppermute | solution.py:22
  41.3 3.4 %collective-permute-start.3 = (bf16[80,2048]{1,0:T(8,128)(2,1)S(1)}, bf16[80,2048]{1,0:T(8,128)(2,1)S(1)}, u32[]{:S(2)}, u32[]{:S(2)}) collective-permute-start(bf16[80,2048]{1,0:T(8,128)(2,1)S(1)} %get-tuple-element.49), channel_id=1, source_target_pairs={{0,8},{4,12},{8,0},{12,4},{1,9},{5,13},{9,1},{13,5},{2,10},{6,14},... | collective-permute-start | bytes 983048 | tf_op jit(solution)/shard_map/ppermute | solution.py:22
  44.7 2.5 %collective-permute-start.2 = (bf16[80,2048]{1,0:T(8,128)(2,1)S(1)}, bf16[80,2048]{1,0:T(8,128)(2,1)S(1)}, u32[]{:S(2)}, u32[]{:S(2)}) collective-permute-start(bf16[80,2048]{1,0:T(8,128)(2,1)S(1)} %get-tuple-element.47), channel_id=1, source_target_pairs={{0,4},{4,0},{8,12},{12,8},{1,5},{5,1},{9,13},{13,9},{2,6},{6,2},{1... | collective-permute-start | bytes 983048 | tf_op jit(solution)/shard_map/ppermute | solution.py:22
  47.7 8.5 %collective-permute-done.4.refs_3_ = bf16[80,2048]{1,0:T(8,128)(2,1)S(1)} collective-permute-done((bf16[80,2048]{1,0:T(8,128)(2,1)S(1)}, bf16[80,2048]{1,0:T(8,128)(2,1)S(1)}, u32[]{:S(2)}, u32[]{:S(2)}) %collective-permute-start.4) | collective-permute-done | bytes 327712 | tf_op jit(solution)/shard_map/ppermute | solution.py:22
  56.2 3.8 %collective-permute-done.3.refs_2_ = bf16[80,2048]{1,0:T(8,128)(2,1)S(1)} collective-permute-done((bf16[80,2048]{1,0:T(8,128)(2,1)S(1)}, bf16[80,2048]{1,0:T(8,128)(2,1)S(1)}, u32[]{:S(2)}, u32[]{:S(2)}) %collective-permute-start.3) | collective-permute-done | bytes 327712 | tf_op jit(solution)/shard_map/ppermute | solution.py:22
  62.6 1.9 %collective-permute-done.5.refs_5_ = bf16[1,512,768]{2,1,0:T(8,128)(2,1)S(1)} collective-permute-done((bf16[1,512,768]{2,1,0:T(8,128)(2,1)S(1)}, bf16[1,512,768]{2,1,0:T(8,128)(2,1)S(1)}, u32[]{:S(2)}, u32[]{:S(2)}) %collective-permute-start.5) | collective-permute-done | bytes 786464 | tf_op jit(solution)/shard_map/ppermute | solution.py:22
  65.7 2.3 %hidden.1 = (bf16[320,768]{1,0:T(8,128)(2,1)S(1)}, f32[320,768]{1,0:T(8,128)S(1)}, f32[320,768]{1,0:T(8,128)S(1)}) custom-call(bf16[80,2048]{1,0:T(8,128)(2,1)S(1)} %get-tuple-element.45.refs_0_, bf16[80,2048]{1,0:T(8,128)(2,1)S(1)} %collective-permute-done.2.refs_1_, bf16[80,2048]{1,0:T(8,128)(2,1)S(1)} %collective-permute-done.3.refs_2_, ...), custom_call_target="tpu_custom_call" | custom-call | tf_op jit(solution)/shard_map/hidden/pallas_call | solution.py:375
  68.0 3.6 %collective-permute-start.14 = (bf16[80,2048]{1,0:T(8,128)(2,1)S(1)}, bf16[80,2048]{1,0:T(8,128)(2,1)S(1)}, u32[]{:S(2)}, u32[]{:S(2)}) collective-permute-start(bf16[80,2048]{1,0:T(8,128)(2,1)S(1)} %get-tuple-element.63), channel_id=1, source_target_pairs={{0,4},{4,0},{8,12},{12,8},{1,5},{5,1},{9,13},{13,9},{2,6},{6,2},{1... | collective-permute-start | bytes 983048 | tf_op jit(solution)/shard_map/ppermute | solution.py:22
  72.9 1.8 %collective-permute-start.12 = (bf16[80,2048]{1,0:T(8,128)(2,1)S(1)}, bf16[80,2048]{1,0:T(8,128)(2,1)S(1)}, u32[]{:S(2)}, u32[]{:S(2)}) collective-permute-start(bf16[80,2048]{1,0:T(8,128)(2,1)S(1)} %get-tuple-element.58), channel_id=1, source_target_pairs={{0,8},{4,12},{8,0},{12,4},{1,9},{5,13},{9,1},{13,5},{2,10},{6,14},... | collective-permute-start | bytes 983048 | tf_op jit(solution)/shard_map/ppermute | solution.py:22
  74.7 1.6 %collective-permute-start.13 = (bf16[80,2048]{1,0:T(8,128)(2,1)S(1)}, bf16[80,2048]{1,0:T(8,128)(2,1)S(1)}, u32[]{:S(2)}, u32[]{:S(2)}) collective-permute-start(bf16[80,2048]{1,0:T(8,128)(2,1)S(1)} %get-tuple-element.59), channel_id=1, source_target_pairs={{0,12},{4,8},{8,4},{12,0},{1,13},{5,9},{9,5},{13,1},{2,14},{6,10},... | collective-permute-start | bytes 983048 | tf_op jit(solution)/shard_map/ppermute | solution.py:22
  76.4 2.2 %collective-permute-done.15.refs_3_ = bf16[80,2048]{1,0:T(8,128)(2,1)S(1)} collective-permute-done((bf16[80,2048]{1,0:T(8,128)(2,1)S(1)}, bf16[80,2048]{1,0:T(8,128)(2,1)S(1)}, u32[]{:S(2)}, u32[]{:S(2)}) %collective-permute-start.15) | collective-permute-done | bytes 327712 | tf_op jit(solution)/shard_map/ppermute | solution.py:22
  78.6 9.1 %collective-permute-done.14.refs_1_ = bf16[80,2048]{1,0:T(8,128)(2,1)S(1)} collective-permute-done((bf16[80,2048]{1,0:T(8,128)(2,1)S(1)}, bf16[80,2048]{1,0:T(8,128)(2,1)S(1)}, u32[]{:S(2)}, u32[]{:S(2)}) %collective-permute-start.14) | collective-permute-done | bytes 327712 | tf_op jit(solution)/shard_map/ppermute | solution.py:22
  87.7 3.2 %backward.1 = (bf16[80,2048]{1,0:T(8,128)(2,1)S(1)}, bf16[80,2048]{1,0:T(8,128)(2,1)S(1)}, bf16[80,2048]{1,0:T(8,128)(2,1)S(1)}, bf16[80,2048]{1,0:T(8,128)(2,1)S(1)}) custom-call(bf16[80,2048]{1,0:T(8,128)(2,1)S(1)} %get-tuple-element.61.refs_0_, bf16[80,2048]{1,0:T(8,128)(2,1)S(1)} %collective-permute-done.14.refs_1_, ...), custom_call_target="tpu_custom_call" | custom-call | tf_op jit(solution)/shard_map/backward/pallas_call | solution.py:386
  91.0 2.5 %collective-permute-start.16 = (bf16[80,2048]{1,0:T(8,128)(2,1)S(1)}, bf16[80,2048]{1,0:T(8,128)(2,1)S(1)}, u32[]{:S(2)}, u32[]{:S(2)}) collective-permute-start(bf16[80,2048]{1,0:T(8,128)(2,1)S(1)} %get-tuple-element.69), channel_id=1, source_target_pairs={{0,4},{4,0},{8,12},{12,8},{1,5},{5,1},{9,13},{13,9},{2,6},{6,2},{1... | collective-permute-start | bytes 983048 | tf_op jit(solution)/shard_map/ppermute | solution.py:22
  96.1 10.6 %collective-permute-done.13.refs_3_ = bf16[80,2048]{1,0:T(8,128)(2,1)S(1)} collective-permute-done((bf16[80,2048]{1,0:T(8,128)(2,1)S(1)}, bf16[80,2048]{1,0:T(8,128)(2,1)S(1)}, u32[]{:S(2)}, u32[]{:S(2)}) %collective-permute-start.13) | collective-permute-done | bytes 327712 | tf_op jit(solution)/shard_map/ppermute | solution.py:22
  106.7 1.9 %layer.1 = bf16[1,128,2048]{2,1,0:T(8,128)(2,1)} custom-call(s32[1,2,128]{2,1,0:T(2,128)S(1)} %bitcast.7, f32[1,2,128]{2,1,0:T(2,128)S(1)} %bitcast.9, bf16[1,128,2048]{2,1,0:T(8,128)(2,1)S(1)} %copy-done.1, bf16[128,2048]{1,0:T(8,128)(2,1)S(1)} %get-tuple-element.60.att_ref, bf16[80,2048]{1,0:T(8,128)(2,1)S(1)} %get-tuple-element.56.refs_0_, ...), custom_call_target="tpu_custom_call" | custom-call | tf_op jit(solution)/shard_map/layer/pallas_call | solution.py:396
  108.6 3.6 %collective-permute-done.16.refs_1_ = bf16[80,2048]{1,0:T(8,128)(2,1)S(1)} collective-permute-done((bf16[80,2048]{1,0:T(8,128)(2,1)S(1)}, bf16[80,2048]{1,0:T(8,128)(2,1)S(1)}, u32[]{:S(2)}, u32[]{:S(2)}) %collective-permute-start.16) | collective-permute-done | bytes 327712 | tf_op jit(solution)/shard_map/ppermute | solution.py:22
  112.2 14.7 %collective-permute-done.17.refs_2_ = bf16[80,2048]{1,0:T(8,128)(2,1)S(1)} collective-permute-done((bf16[80,2048]{1,0:T(8,128)(2,1)S(1)}, bf16[80,2048]{1,0:T(8,128)(2,1)S(1)}, u32[]{:S(2)}, u32[]{:S(2)}) %collective-permute-start.17) | collective-permute-done | bytes 327712 | tf_op jit(solution)/shard_map/ppermute | solution.py:22
  128.1 6.3 %collective-permute-done.18.back_ref = bf16[80,2048]{1,0:T(8,128)(2,1)S(1)} collective-permute-done((bf16[80,2048]{1,0:T(8,128)(2,1)S(1)}, bf16[80,2048]{1,0:T(8,128)(2,1)S(1)}, u32[]{:S(2)}, u32[]{:S(2)}) %collective-permute-start.18) | collective-permute-done | bytes 327712 | tf_op jit(solution)/shard_map/ppermute | solution.py:22
  (46 shorter events, 13.9 us)
Async XLA Ops:
  1.9 18.9 %copy-start.1 = (bf16[1,128,2048]{2,1,0:T(8,128)(2,1)S(1)}, bf16[1,128,2048]{2,1,0:T(8,128)(2,1)}, u32[]{:S(2)}) copy-start(bf16[1,128,2048]{2,1,0:T(8,128)(2,1)} %in_ref.5) | copy-start | bytes 1572868
  1.9 18.9 %copy-start.4 = (bf16[1,128,2048]{2,1,0:T(8,128)(2,1)S(1)}, bf16[1,128,2048]{2,1,0:T(8,128)(2,1)}, u32[]{:S(2)}) copy-start(bf16[1,128,2048]{2,1,0:T(8,128)(2,1)} %refs_1_.1) | copy-start | bytes 1572868
  2.0 16.2 %collective-permute-start = (bf16[1,128,4096]{2,1,0:T(8,128)(2,1)S(1)}, bf16[1,128,4096]{2,1,0:T(8,128)(2,1)S(1)}, u32[]{:S(2)}, u32[]{:S(2)}) collective-permute-start(bf16[1,128,4096]{2,1,0:T(8,128)(2,1)S(1)} %pad_add_fusion), channel_id=1, source_target_pairs={{0,1},{1,4},{4,5},{5,8},{8,9},{9,12},{12,13},{2,3},{3,6},{6,7},{7,... | collective-permute-start | bytes 3145736 | tf_op jit(solution)/shard_map/ppermute | solution.py:28
  6.6 49.6 %collective-permute-start.9 = (bf16[2,512,768]{2,1,0:T(8,128)(2,1)}, bf16[2,512,768]{2,1,0:T(8,128)(2,1)S(1)}, u32[]{:S(2)}, u32[]{:S(2)}) collective-permute-start(bf16[2,512,768]{2,1,0:T(8,128)(2,1)} %prepare.1.refs_8_.refs_1_), channel_id=1, source_target_pairs={{0,2},{2,0},{1,3},{3,1},{4,6},{6,4},{5,7},{7,5},{8,10},{10,8},{9,1... | collective-permute-start | bytes 4718600 | tf_op jit(solution)/shard_map/ppermute | solution.py:22
  18.2 23.0 %collective-permute-start.1 = (bf16[80,2048]{1,0:T(8,128)(2,1)S(1)}, bf16[80,2048]{1,0:T(8,128)(2,1)S(1)}, u32[]{:S(2)}, u32[]{:S(2)}) collective-permute-start(bf16[80,2048]{1,0:T(8,128)(2,1)S(1)} %get-tuple-element.44), channel_id=1, source_target_pairs={{0,8},{4,12},{8,0},{12,4},{1,9},{5,13},{9,1},{13,5},{2,10},{6,14},... | collective-permute-start | bytes 983048 | tf_op jit(solution)/shard_map/ppermute | solution.py:22
  20.9 26.3 %copy-start.2 = (bf16[1,512,768]{2,1,0:T(8,128)(2,1)S(1)}, bf16[1,512,768]{2,1,0:T(8,128)(2,1)}, u32[]{:S(2)}) copy-start(bf16[1,512,768]{2,1,0:T(8,128)(2,1)} %refs_4_.3) | copy-start | bytes 2359300
  20.9 35.3 %copy-start = (bf16[2,512,768]{2,1,0:T(8,128)(2,1)S(1)}, bf16[2,512,768]{2,1,0:T(8,128)(2,1)}, u32[]{:S(2)}) copy-start(bf16[2,512,768]{2,1,0:T(8,128)(2,1)} %prepare.1.refs_8_.refs_1_) | copy-start | bytes 4718596
  28.0 28.2 %collective-permute-start.4 = (bf16[80,2048]{1,0:T(8,128)(2,1)S(1)}, bf16[80,2048]{1,0:T(8,128)(2,1)S(1)}, u32[]{:S(2)}, u32[]{:S(2)}) collective-permute-start(bf16[80,2048]{1,0:T(8,128)(2,1)S(1)} %get-tuple-element.50), channel_id=1, source_target_pairs={{0,12},{4,8},{8,4},{12,0},{1,13},{5,9},{9,5},{13,1},{2,14},{6,10},... | collective-permute-start | bytes 983048 | tf_op jit(solution)/shard_map/ppermute | solution.py:22
  41.3 18.7 %collective-permute-start.3 = (bf16[80,2048]{1,0:T(8,128)(2,1)S(1)}, bf16[80,2048]{1,0:T(8,128)(2,1)S(1)}, u32[]{:S(2)}, u32[]{:S(2)}) collective-permute-start(bf16[80,2048]{1,0:T(8,128)(2,1)S(1)} %get-tuple-element.49), channel_id=1, source_target_pairs={{0,8},{4,12},{8,0},{12,4},{1,9},{5,13},{9,1},{13,5},{2,10},{6,14},... | collective-permute-start | bytes 983048 | tf_op jit(solution)/shard_map/ppermute | solution.py:22
  44.7 15.3 %collective-permute-start.2 = (bf16[80,2048]{1,0:T(8,128)(2,1)S(1)}, bf16[80,2048]{1,0:T(8,128)(2,1)S(1)}, u32[]{:S(2)}, u32[]{:S(2)}) collective-permute-start(bf16[80,2048]{1,0:T(8,128)(2,1)S(1)} %get-tuple-element.47), channel_id=1, source_target_pairs={{0,4},{4,0},{8,12},{12,8},{1,5},{5,1},{9,13},{13,9},{2,6},{6,2},{1... | collective-permute-start | bytes 983048 | tf_op jit(solution)/shard_map/ppermute | solution.py:22
  47.2 13.9 %collective-permute-start.6 = (bf16[1,512,768]{2,1,0:T(8,128)(2,1)S(1)}, bf16[1,512,768]{2,1,0:T(8,128)(2,1)S(1)}, u32[]{:S(2)}, u32[]{:S(2)}) collective-permute-start(bf16[1,512,768]{2,1,0:T(8,128)(2,1)S(1)} %copy-done.2), channel_id=1, source_target_pairs={{0,2},{2,0},{1,3},{3,1},{4,6},{6,4},{5,7},{7,5},{8,10},{10,8},{9,1... | collective-permute-start | bytes 2359304 | tf_op jit(solution)/shard_map/ppermute | solution.py:22
  56.2 9.4 %collective-permute-start.8 = (bf16[2,512,768]{2,1,0:T(8,128)(2,1)S(1)}, bf16[2,512,768]{2,1,0:T(8,128)(2,1)S(1)}, u32[]{:S(2)}, u32[]{:S(2)}) collective-permute-start(bf16[2,512,768]{2,1,0:T(8,128)(2,1)S(1)} %copy-done), channel_id=1, source_target_pairs={{0,1},{1,0},{2,3},{3,2},{4,5},{5,4},{6,7},{7,6},{8,9},{9,8},{10,11... | collective-permute-start | bytes 4718600 | tf_op jit(solution)/shard_map/ppermute | solution.py:22
  60.0 5.7 %collective-permute-start.10 = (bf16[2,512,768]{2,1,0:T(8,128)(2,1)S(1)}, bf16[2,512,768]{2,1,0:T(8,128)(2,1)S(1)}, u32[]{:S(2)}, u32[]{:S(2)}) collective-permute-start(bf16[2,512,768]{2,1,0:T(8,128)(2,1)S(1)} %collective-permute-done.9.refs_10_.refs_3_), channel_id=1, source_target_pairs={{0,1},{1,0},{2,3},{3,2},{4,5},{5,4},{6,7},{7,6},{8,9},{9,8},{10,11... | collective-permute-start | bytes 4718600 | tf_op jit(solution)/shard_map/ppermute | solution.py:22
  60.0 4.5 %collective-permute-start.5 = (bf16[1,512,768]{2,1,0:T(8,128)(2,1)S(1)}, bf16[1,512,768]{2,1,0:T(8,128)(2,1)S(1)}, u32[]{:S(2)}, u32[]{:S(2)}) collective-permute-start(bf16[1,512,768]{2,1,0:T(8,128)(2,1)S(1)} %copy-done.2), channel_id=1, source_target_pairs={{0,1},{1,0},{2,3},{3,2},{4,5},{5,4},{6,7},{7,6},{8,9},{9,8},{10,11... | collective-permute-start | bytes 2359304 | tf_op jit(solution)/shard_map/ppermute | solution.py:22
  61.0 4.6 %collective-permute-start.7 = (bf16[1,512,768]{2,1,0:T(8,128)(2,1)S(1)}, bf16[1,512,768]{2,1,0:T(8,128)(2,1)S(1)}, u32[]{:S(2)}, u32[]{:S(2)}) collective-permute-start(bf16[1,512,768]{2,1,0:T(8,128)(2,1)S(1)} %collective-permute-done.6.refs_6_), channel_id=1, source_target_pairs={{0,1},{1,0},{2,3},{3,2},{4,5},{5,4},{6,7},{7,6},{8,9},{9,8},{10,11... | collective-permute-start | bytes 2359304 | tf_op jit(solution)/shard_map/ppermute | solution.py:22
  61.0 17.5 %collective-permute-start.15 = (bf16[80,2048]{1,0:T(8,128)(2,1)S(1)}, bf16[80,2048]{1,0:T(8,128)(2,1)S(1)}, u32[]{:S(2)}, u32[]{:S(2)}) collective-permute-start(bf16[80,2048]{1,0:T(8,128)(2,1)S(1)} %get-tuple-element.65), channel_id=1, source_target_pairs={{0,12},{4,8},{8,4},{12,0},{1,13},{5,9},{9,5},{13,1},{2,14},{6,10},... | collective-permute-start | bytes 983048 | tf_op jit(solution)/shard_map/ppermute | solution.py:22
  68.0 19.8 %collective-permute-start.14 = (bf16[80,2048]{1,0:T(8,128)(2,1)S(1)}, bf16[80,2048]{1,0:T(8,128)(2,1)S(1)}, u32[]{:S(2)}, u32[]{:S(2)}) collective-permute-start(bf16[80,2048]{1,0:T(8,128)(2,1)S(1)} %get-tuple-element.63), channel_id=1, source_target_pairs={{0,4},{4,0},{8,12},{12,8},{1,5},{5,1},{9,13},{13,9},{2,6},{6,2},{1... | collective-permute-start | bytes 983048 | tf_op jit(solution)/shard_map/ppermute | solution.py:22
  72.8 22.1 %collective-permute-start.11 = (bf16[80,2048]{1,0:T(8,128)(2,1)S(1)}, bf16[80,2048]{1,0:T(8,128)(2,1)S(1)}, u32[]{:S(2)}, u32[]{:S(2)}) collective-permute-start(bf16[80,2048]{1,0:T(8,128)(2,1)S(1)} %get-tuple-element.57), channel_id=1, source_target_pairs={{0,4},{4,0},{8,12},{12,8},{1,5},{5,1},{9,13},{13,9},{2,6},{6,2},{1... | collective-permute-start | bytes 983048 | tf_op jit(solution)/shard_map/ppermute | solution.py:22
  72.9 23.2 %collective-permute-start.12 = (bf16[80,2048]{1,0:T(8,128)(2,1)S(1)}, bf16[80,2048]{1,0:T(8,128)(2,1)S(1)}, u32[]{:S(2)}, u32[]{:S(2)}) collective-permute-start(bf16[80,2048]{1,0:T(8,128)(2,1)S(1)} %get-tuple-element.58), channel_id=1, source_target_pairs={{0,8},{4,12},{8,0},{12,4},{1,9},{5,13},{9,1},{13,5},{2,10},{6,14},... | collective-permute-start | bytes 983048 | tf_op jit(solution)/shard_map/ppermute | solution.py:22
  74.7 32.0 %collective-permute-start.13 = (bf16[80,2048]{1,0:T(8,128)(2,1)S(1)}, bf16[80,2048]{1,0:T(8,128)(2,1)S(1)}, u32[]{:S(2)}, u32[]{:S(2)}) collective-permute-start(bf16[80,2048]{1,0:T(8,128)(2,1)S(1)} %get-tuple-element.59), channel_id=1, source_target_pairs={{0,12},{4,8},{8,4},{12,0},{1,13},{5,9},{9,5},{13,1},{2,14},{6,10},... | collective-permute-start | bytes 983048 | tf_op jit(solution)/shard_map/ppermute | solution.py:22
  87.7 19.0 %copy-start.9 = (f32[1,128,2]{1,2,0:T(2,128)S(1)}, f32[1,128,2]{1,2,0:T(2,128)}, u32[]{:S(2)}) copy-start(f32[1,128,2]{1,2,0:T(2,128)} %param.19) | copy-start | bytes 3076
  91.0 21.2 %collective-permute-start.16 = (bf16[80,2048]{1,0:T(8,128)(2,1)S(1)}, bf16[80,2048]{1,0:T(8,128)(2,1)S(1)}, u32[]{:S(2)}, u32[]{:S(2)}) collective-permute-start(bf16[80,2048]{1,0:T(8,128)(2,1)S(1)} %get-tuple-element.69), channel_id=1, source_target_pairs={{0,4},{4,0},{8,12},{12,8},{1,5},{5,1},{9,13},{13,9},{2,6},{6,2},{1... | collective-permute-start | bytes 983048 | tf_op jit(solution)/shard_map/ppermute | solution.py:22
  93.5 33.4 %collective-permute-start.17 = (bf16[80,2048]{1,0:T(8,128)(2,1)S(1)}, bf16[80,2048]{1,0:T(8,128)(2,1)S(1)}, u32[]{:S(2)}, u32[]{:S(2)}) collective-permute-start(bf16[80,2048]{1,0:T(8,128)(2,1)S(1)} %get-tuple-element.70), channel_id=1, source_target_pairs={{0,8},{4,12},{8,0},{12,4},{1,9},{5,13},{9,1},{13,5},{2,10},{6,14},... | collective-permute-start | bytes 983048 | tf_op jit(solution)/shard_map/ppermute | solution.py:22
  94.9 39.6 %collective-permute-start.18 = (bf16[80,2048]{1,0:T(8,128)(2,1)S(1)}, bf16[80,2048]{1,0:T(8,128)(2,1)S(1)}, u32[]{:S(2)}, u32[]{:S(2)}) collective-permute-start(bf16[80,2048]{1,0:T(8,128)(2,1)S(1)} %get-tuple-element.75), channel_id=1, source_target_pairs={{0,12},{4,8},{8,4},{12,0},{1,13},{5,9},{9,5},{13,1},{2,14},{6,10},... | collective-permute-start | bytes 983048 | tf_op jit(solution)/shard_map/ppermute | solution.py:22
  (6 other events, 86.2 us)
